TPU v7x, 128 devices: a whole 4x4x4 slice. The times are simulated.
128 devices in a mesh: vox: 8 (over x, core), var: 16 (over y, z).
Axes of the slice: x: 4, y: 4, z: 4, core: 2. Of those that a mesh axis runs over, the one named last changes fastest.
Arguments:
- cross: float32 [16384, 24576], P('vox', 'var')
- start: float32 [32, 24576], P(None, 'var'), may hold values from -6 to 6
- levels: int32 [2, 32], replicated, may hold values from 0 to 767, as said below
Outputs:
- deflated: float32 [16384, 24576], P('vox', 'var')
- left_dirs: float32 [32, 16384], P(None, 'vox')
- right_dirs: float32 [32, 24576], P(None, 'var')
- strength: float32 [32], replicated
Inputs may be any that keep to these rules, and one draw needn't show every extreme that they name: `levels`: both 0 and 767 occur in every draw.
All inputs are finite; a program needn't handle non-finite values.
Results may differ from a plain program's by a relative error of at most 0.0003.
Values sent between devices are 32-bit elements; how exact they have to be, the bound alone decides.
No kernel may reach another device: no remote copies, remote signals or barrier semaphores. Data moves between devices by JAX's collectives and lax.ppermute only.
A program may use at most 128 MiB of HBM per device.

v0:
```python
import math

import jax
import jax.numpy as jnp
from jax import lax
from jax.sharding import PartitionSpec as P

NV = 16384
NG = 24576
ITERS = 2


EPSILON = 1e-06
HIGH = lax.Precision.HIGHEST


def shrink(values, thresholds, mean_sq):
    level = (thresholds * jnp.sqrt(mean_sq + EPSILON))[:, None]
    return values - jnp.clip(values, -level, level)


def local_gram(shrunk):
    return lax.dot_general(
        shrunk, shrunk, (((1,), (1,)), ((), ())), precision=HIGH, preferred_element_type=jnp.float32
    )


def apply_gram(shrunk, gram, count):
    gram = gram / count + EPSILON * jnp.eye(gram.shape[0], dtype=jnp.float32)
    factor = jnp.linalg.cholesky(gram)
    return jax.scipy.linalg.solve_triangular(factor, shrunk, lower=True)


def left_update(cross, right_dirs, thresholds):
    partial_sum = lax.dot_general(
        right_dirs,
        cross,
        (((1,), (1,)), ((), ())),
        precision=HIGH,
        preferred_element_type=jnp.float32,
    )
    summed = lax.psum(partial_sum, "var")
    first_sums = lax.psum(jnp.sum(summed * summed, 1), "vox")
    shrunk = shrink(summed, thresholds, first_sums / NV)
    gram = lax.psum(local_gram(shrunk), "vox")
    return apply_gram(shrunk, gram, NV)


def right_update(cross, left_dirs, thresholds):
    partial_sum = jnp.dot(left_dirs, cross, precision=HIGH, preferred_element_type=jnp.float32)
    summed = lax.psum(partial_sum, "vox")
    first_sums = lax.psum(jnp.sum(summed * summed, 1), "var")
    shrunk = shrink(summed, thresholds, first_sums / NG)
    gram = lax.psum(local_gram(shrunk), "var")
    return apply_gram(shrunk, gram, NG)


def per_device(cross, start, levels):
    thresholds = levels.astype(jnp.float32) / 1024.0
    right_dirs = start
    left_dirs = None
    for sweep in range(ITERS):
        left_dirs = left_update(cross, right_dirs, thresholds[0])
        right_dirs = right_update(cross, left_dirs, thresholds[1])
    projected = lax.dot_general(
        right_dirs,
        cross,
        (((1,), (1,)), ((), ())),
        precision=HIGH,
        preferred_element_type=jnp.float32,
    )
    strength = lax.psum(jnp.sum(left_dirs * projected, 1), ("vox", "var")) / math.sqrt(NV * NG)
    scaled = left_dirs * (strength / math.sqrt(NV * NG))[:, None]
    removed = lax.dot_general(
        scaled,
        right_dirs,
        (((0,), (0,)), ((), ())),
        precision=HIGH,
        preferred_element_type=jnp.float32,
    )
    deflated = cross - removed
    return (deflated, left_dirs, right_dirs, strength)


def solution(mesh):
    in_specs = (P("vox", "var"), P(None, "var"), P())
    out_specs = (P("vox", "var"), P(None, "vox"), P(None, "var"), P())
    return jax.shard_map(
        per_device, mesh=mesh, in_specs=in_specs, out_specs=out_specs, check_vma=False
    )
```

profile of v0, /device:TPU:0, one launch (start us, length us, event | category | flops | bytes accessed | tf_op | source)
XLA Modules:
  0.0 772.9 jit_solution(14061262218946055673)
XLA Ops:
  8.1 14.9 %fusion.47 = f32[32,2048]{1,0:T(8,128)} fusion(f32[32,1536]{1,0:T(8,128)S(1)} %copy-done, f32[2048,1536]{1,0:T(8,128)} %param.8), kind=kOutput, calls=%fused_computation.85 | convolution fusion | flops 1207959552 | bytes 13041664 | tf_op jit(solution)/shard_map/dot_general | solution.py:35
  23.1 87.0 %all-reduce.5.cloned.1.call-done = f32[32,2048]{1,0:T(8,128)} async-done(((f32[32,2048]{1,0:T(8,128)}), f32[32,2048]{1,0:T(8,128)}) %all-reduce.5.cloned.1.call-update) | async-done | bytes 262160 | tf_op jit(solution)/shard_map/psum | solution.py:42
  111.1 13.2 %psum.92 = f32[32]{0:T(128)S(1)} all-reduce(f32[32]{0:T(128)S(1)} %multiply_reduce_fusion.1), channel_id=1, replica_groups=mesh['vox'=8,'var'=16] {'vox'}, use_global_device_ids=true, to_apply=%region_2.0 | all-reduce | flops 32 | bytes 256 | tf_op jit(solution)/shard_map/psum | solution.py:43
  125.9 23.6 %psum.93 = f32[32,32]{0,1:T(8,128)S(1)} all-reduce(f32[32,32]{0,1:T(8,128)S(1)} %fusion.3), channel_id=1, replica_groups=mesh['vox'=8,'var'=16] {'vox'}, use_global_device_ids=true, to_apply=%region_3.4 | all-reduce | flops 1024 | bytes 8192 | tf_op jit(solution)/shard_map/psum | solution.py:45
  149.6 2.9 cholesky.74
  157.7 10.8 %fusion.48 = f32[32,1536]{1,0:T(8,128)} fusion(f32[32,2048]{1,0:T(8,128)S(1)} %fusion.2, f32[2048,1536]{1,0:T(8,128)} %param.8), kind=kOutput, calls=%fused_computation.86 | convolution fusion | flops 1207959552 | bytes 13041664 | tf_op jit(solution)/shard_map/dot_general | solution.py:50
  168.6 56.0 %all-reduce.7.cloned.1.call-done = f32[32,1536]{1,0:T(8,128)} async-done(((f32[32,1536]{1,0:T(8,128)}), f32[32,1536]{1,0:T(8,128)}) %all-reduce.7.cloned.1.call-update) | async-done | bytes 196624 | tf_op jit(solution)/shard_map/psum | solution.py:51
  225.6 40.6 %psum.95 = f32[32]{0:T(128)S(1)} all-reduce(f32[32]{0:T(128)S(1)} %multiply_reduce_fusion.3), channel_id=1, replica_groups=mesh['vox'=8,'var'=16] {'var'}, use_global_device_ids=true, to_apply=%region_8.11 | all-reduce | flops 32 | bytes 256 | tf_op jit(solution)/shard_map/psum | solution.py:52
  267.6 69.7 %psum.96 = f32[32,32]{0,1:T(8,128)S(1)} all-reduce(f32[32,32]{0,1:T(8,128)S(1)} %fusion.7), channel_id=1, replica_groups=mesh['vox'=8,'var'=16] {'var'}, use_global_device_ids=true, to_apply=%region_9.12 | all-reduce | flops 1024 | bytes 8192 | tf_op jit(solution)/shard_map/psum | solution.py:54
  337.4 2.9 cholesky.85
  345.4 14.9 %fusion.49 = f32[32,2048]{1,0:T(8,128)} fusion(f32[32,1536]{1,0:T(8,128)S(1)} %fusion.6, f32[2048,1536]{1,0:T(8,128)} %param.8), kind=kOutput, calls=%fused_computation.87 | convolution fusion | flops 1207959552 | bytes 13041664 | tf_op jit(solution)/shard_map/dot_general | solution.py:35
  360.4 78.2 %all-reduce.9.cloned.1.call-done = f32[32,2048]{1,0:T(8,128)} async-done(((f32[32,2048]{1,0:T(8,128)}), f32[32,2048]{1,0:T(8,128)}) %all-reduce.9.cloned.1.call-update) | async-done | bytes 262160 | tf_op jit(solution)/shard_map/psum | solution.py:42
  439.7 13.2 %psum.98 = f32[32]{0:T(128)S(1)} all-reduce(f32[32]{0:T(128)S(1)} %multiply_reduce_fusion), channel_id=1, replica_groups=mesh['vox'=8,'var'=16] {'vox'}, use_global_device_ids=true, to_apply=%region_12.16 | all-reduce | flops 32 | bytes 256 | tf_op jit(solution)/shard_map/psum | solution.py:43
  454.4 23.6 %psum.99 = f32[32,32]{0,1:T(8,128)S(1)} all-reduce(f32[32,32]{0,1:T(8,128)S(1)} %fusion.5), channel_id=1, replica_groups=mesh['vox'=8,'var'=16] {'vox'}, use_global_device_ids=true, to_apply=%region_13.17 | all-reduce | flops 1024 | bytes 8192 | tf_op jit(solution)/shard_map/psum | solution.py:45
  478.1 2.9 cholesky.96
  486.2 10.9 %fusion.50 = f32[32,1536]{1,0:T(8,128)} fusion(f32[32,2048]{1,0:T(8,128)S(1)} %fusion.4, f32[2048,1536]{1,0:T(8,128)} %param.8), kind=kOutput, calls=%fused_computation.88 | convolution fusion | flops 1207959552 | bytes 13041664 | tf_op jit(solution)/shard_map/dot_general | solution.py:50
  497.2 56.0 %all-reduce.11.cloned.1.call-done = f32[32,1536]{1,0:T(8,128)} async-done(((f32[32,1536]{1,0:T(8,128)}), f32[32,1536]{1,0:T(8,128)}) %all-reduce.11.cloned.1.call-update) | async-done | bytes 196624 | tf_op jit(solution)/shard_map/psum | solution.py:51
  554.2 40.6 %psum.101 = f32[32]{0:T(128)S(1)} all-reduce(f32[32]{0:T(128)S(1)} %multiply_reduce_fusion.2), channel_id=1, replica_groups=mesh['vox'=8,'var'=16] {'var'}, use_global_device_ids=true, to_apply=%region_16.20 | all-reduce | flops 32 | bytes 256 | tf_op jit(solution)/shard_map/psum | solution.py:52
  596.2 69.7 %psum.102 = f32[32,32]{0,1:T(8,128)S(1)} all-reduce(f32[32,32]{0,1:T(8,128)S(1)} %fusion.9), channel_id=1, replica_groups=mesh['vox'=8,'var'=16] {'var'}, use_global_device_ids=true, to_apply=%region_17.21 | all-reduce | flops 1024 | bytes 8192 | tf_op jit(solution)/shard_map/psum | solution.py:54
  666.1 2.9 cholesky.107
  670.3 2.4 custom-call.13
  674.1 14.4 %fusion = f32[32]{0:T(128)S(1)} fusion(f32[32,2048]{1,0:T(8,128)S(1)} %fusion.4, f32[32,1536]{1,0:T(8,128)S(1)} %fusion.8, f32[2048,1536]{1,0:T(8,128)} %param.8), kind=kOutput, calls=%fused_computation.2 | convolution fusion | flops 1208090624 | bytes 13041792 | tf_op jit(solution)/shard_map/dot_general | solution.py:65
  688.5 62.5 %psum.103 = f32[32]{0:T(128)S(1)} all-reduce(f32[32]{0:T(128)S(1)} %fusion), channel_id=1, replica_groups=mesh['vox'=8,'var'=16] {'vox','var'}, use_global_device_ids=true, to_apply=%region_19.23 | all-reduce | flops 32 | bytes 256 | tf_op jit(solution)/shard_map/psum | solution.py:72
  751.5 14.9 %convolution_subtract_fusion = f32[2048,1536]{1,0:T(8,128)} fusion(f32[2048,1536]{1,0:T(8,128)} %param.8, f32[32,1536]{1,0:T(8,128)S(1)} %fusion.8, f32[32,2048]{1,0:T(8,128)S(1)} %fusion.4, f32[32]{0:T(128)S(1)} %get-tuple-element.16), kind=kOutput, calls=%fused_computation | convolution fusion | flops 1211170816 | bytes 25624704 | tf_op jit(solution)/shard_map/dot_general | solution.py:74
  (61 shorter events, 30.2 us)
Async XLA Ops:
  7.2 0.9 copy-start
  7.2 15.9 %copy-start.3 = (s32[2,32]{1,0:T(2,128)S(1)}, s32[2,32]{1,0:T(2,128)}, u32[]{:S(2)}) copy-start(s32[2,32]{1,0:T(2,128)} %param.10) | copy-start | bytes 772
  7.2 102.9 %all-reduce.5.cloned.1.call-start = ((), (), s32[]{:S(2)}) async-start(), calls=%async_computation | async-start | bytes 524288 | tf_op jit(solution)/shard_map/psum | solution.py:42
  23.0 201.5 %all-reduce.7.cloned.1.call-start = ((), (), s32[]{:S(2)}) async-start(), calls=%async_computation.1 | async-start | bytes 393216 | tf_op jit(solution)/shard_map/psum | solution.py:51
  168.5 270.1 %all-reduce.9.cloned.1.call-start = ((), (), s32[]{:S(2)}) async-start(), calls=%async_computation.2 | async-start | bytes 524288 | tf_op jit(solution)/shard_map/psum | solution.py:42
  360.3 192.8 %all-reduce.11.cloned.1.call-start = ((), (), s32[]{:S(2)}) async-start(), calls=%async_computation.3 | async-start | bytes 393216 | tf_op jit(solution)/shard_map/psum | solution.py:51
  486.2 265.3 %copy-start.1 = (f32[32,2048]{1,0:T(8,128)}, f32[32,2048]{1,0:T(8,128)S(1)}, u32[]{:S(2)}) copy-start(f32[32,2048]{1,0:T(8,128)S(1)} %fusion.4) | copy-start | bytes 786436
  674.1 92.3 %copy-start.2 = (f32[32,1536]{1,0:T(8,128)}, f32[32,1536]{1,0:T(8,128)S(1)}, u32[]{:S(2)}) copy-start(f32[32,1536]{1,0:T(8,128)S(1)} %fusion.8) | copy-start | bytes 589828
Sparse Core Ops, SparseCore 0:
  23.1 86.9 all-reduce.4
  168.6 55.8 all-reduce.6
  360.5 78.1 all-reduce.8
  497.3 55.8 all-reduce.10
where the time goes:
time: 774 us; the launch traced here: 773 us
  blocking collectives  357 us (46%)
  waiting for transfers between devices  277 us (36%)
  matrix products  92.1 us (12%)
  other arithmetic  31.6 us (4%)
  between operations  14 us (2%)
    psum x2, waiting for transfers between devices, left_update(): summed = lax.psum(partial_sum, 'var')  165 us
    psum x2, blocking collectives, right_update(): gram = lax.psum(local_gram(shrunk), 'var')  139 us
    psum x2, waiting for transfers between devices, right_update(): summed = lax.psum(partial_sum, 'vox')  112 us
    psum x2, blocking collectives, right_update(): first_sums = lax.psum(jnp.sum(summed * summed, 1), 'var')  81.1 us
    psum x1, blocking collectives, per_device(): lax.psum(jnp.sum(left_dirs * projected, 1), ('vox', 'var'))  62.5 us
    psum x2, blocking collectives, left_update(): gram = lax.psum(local_gram(shrunk), 'vox')  47.1 us
    dot_general x2, matrix products, left_update(): lax.dot_general(right_dirs, cross, (((1,), (1,)), ((), ())), precision=HI...  29.8 us
    psum x2, blocking collectives, left_update(): first_sums = lax.psum(jnp.sum(summed * summed, 1), 'vox')  26.5 us
  transfers between devices with their start and end apart: 4, of which 4 were waited for; matrix products, arithmetic and copies ran while one was open for 0% of the time, Pallas kernels for 0%

commit v1 on v0

v1 whole, which is shorter than its diff:
```python
import math

import jax
import jax.numpy as jnp
from jax import lax
from jax.experimental import pallas as pl
from jax.experimental.pallas import tpu as pltpu
from jax.sharding import PartitionSpec as P

NV = 16384
NG = 24576
K = 32
ITERS = 2
ROWS = 2048
COLS = 1536
QUARTER = ROWS // 4
HALF = COLS // 2
BLOCK = 512
LANES = 128

EPSILON = 1e-06
HIGHEST = lax.Precision.HIGHEST
F32 = jnp.float32
BF16 = jnp.bfloat16
NT = (((1,), (1,)), ((), ()))
NN = (((1,), (0,)), ((), ()))
TN = (((0,), (0,)), ((), ()))

X_RINGS = [[x * 2 + c for x in range(4)] for c in range(2)]
CORE_PAIRS = [[x * 2, x * 2 + 1] for x in range(4)]
Y_RINGS = [[y * 4 + z for y in range(4)] for z in range(4)]
Z_RINGS = [[y * 4 + z for z in range(4)] for y in range(4)]
STEPS = (1, 3, 2)

PARAMS = pltpu.CompilerParams(vmem_limit_bytes=40 * 2**20)


def shift(value, axis, rings, step):
    pairs = [(r[i], r[(i + step) % len(r)]) for r in rings for i in range(len(r))]
    return lax.ppermute(value, axis, pairs)


def ring_sum(value, axis, rings):
    got = [shift(value, axis, rings, step) for step in STEPS]
    return (value + got[0]) + (got[1] + got[2])


def pair_sum(value):
    return value + shift(value, "vox", CORE_PAIRS, 1)


def dot(a, b, dims):
    return lax.dot_general(a, b, dims, preferred_element_type=F32)


def full_dot(a, b, dims):
    return lax.dot_general(a, b, dims, precision=HIGHEST, preferred_element_type=F32)


def split2(x):
    high = x.astype(BF16)
    return high, (x - high.astype(F32)).astype(BF16)


def split3(x):
    high = x.astype(BF16)
    rest = x - high.astype(F32)
    middle = rest.astype(BF16)
    return high, middle, (rest - middle.astype(F32)).astype(BF16)


def diagonal(width=LANES, offset=0):
    row = lax.broadcasted_iota(jnp.int32, (K, width), 0)
    lane = lax.broadcasted_iota(jnp.int32, (K, width), 1)
    return lane == row + offset


def to_column(row):
    return jnp.sum(jnp.where(diagonal(K), row, 0.0), axis=1, keepdims=True)


def to_row(column):
    return jnp.sum(jnp.where(diagonal(), column, 0.0), axis=0, keepdims=True)


def cross_gram(a, b):
    parts = dot(jnp.concatenate(split3(a), axis=0), jnp.concatenate(split3(b), axis=0), NT)
    rows = parts[:K] + (parts[K : 2 * K] + parts[2 * K :])
    return rows[:, :K] + (rows[:, K : 2 * K] + rows[:, 2 * K :])


def shrunk_of(values, squares, levels, side, count):
    thresholds = levels[side : side + 1, :].astype(F32) / 1024.0
    level = to_column(thresholds * jnp.sqrt(squares[:, :K] / count + EPSILON))
    return values - jnp.clip(values, -level, level)


def padded(small):
    return jnp.concatenate([small, jnp.zeros((K, LANES - small.shape[1]), F32)], axis=1)


def inverse_factor(gram, count):
    start = gram / count + jnp.where(diagonal(K), EPSILON, 0.0)
    start = jnp.concatenate(
        [jnp.where(diagonal(K), 1.0, 0.0), start, jnp.zeros((K, LANES - 2 * K), F32)], axis=1
    )
    blocks = [start[8 * b : 8 * b + 8] for b in range(4)]
    row = lax.broadcasted_iota(jnp.int32, (8, LANES), 0)
    pivots = []
    for panel in range(4):
        columns = [
            {
                b: jnp.broadcast_to(blocks[b][:, K + 8 * panel + t : K + 8 * panel + t + 1], (8, LANES))
                for b in range(panel, 4)
            }
            for t in range(8)
        ]
        pivot_of = jnp.ones((8, LANES), F32)
        for t in range(8):
            pivot = columns[t][panel][t : t + 1]
            pivot_of = jnp.where(row == t, pivot, pivot_of)
            inverse = 1.0 / pivot
            top = blocks[panel][t : t + 1]
            for b in range(panel, 4):
                factor = columns[t][b] * inverse
                if b == panel:
                    factor = jnp.where(row > t, factor, 0.0)
                columns[t][b] = factor
            for u in range(t + 1, 8):
                head = columns[u][panel][t : t + 1]
                for b in range(panel, 4):
                    columns[u][b] = columns[u][b] - columns[t][b] * head
            for b in range(panel, 4):
                blocks[b] = blocks[b] - columns[t][b] * top
        pivots.append(pivot_of)
    scale = 1.0 / jnp.sqrt(jnp.concatenate(pivots, axis=0))
    return (jnp.concatenate(blocks, axis=0) * scale)[:, :K]


def left_product(right, squares, levels, cross, z):
    first = squares is None
    width = QUARTER if first else QUARTER + LANES

    def kernel(z_ref, *refs):
        if first:
            right_ref, cross_ref, *outs, both_ref = refs
        else:
            right_ref, squares_ref, levels_ref, cross_ref, *outs, both_ref, gram_ref = refs
        step = pl.program_id(0)

        @pl.when(step == 0)
        def _():
            values = right_ref[...]
            if not first:
                values = shrunk_of(values, squares_ref[...], levels_ref[...], 1, NG)
                gram_ref[...] = padded(cross_gram(values, values))
            both_ref[...] = jnp.concatenate(split2(values), axis=0)

        high, low = split2(cross_ref[...])
        whole = dot(both_ref[...], high, NT)
        product = whole[:K] + (whole[K:] + dot(both_ref[:K], low, NT))
        for at in range(4):

            @pl.when(step == at)
            def _():
                outs[at][:, :QUARTER] = product
                if not first:
                    outs[at][:, QUARTER:] = gram_ref[...]

    small = [] if first else [
        pl.BlockSpec((1, LANES), lambda i, z: (0, 0)),
        pl.BlockSpec((2, K), lambda i, z: (0, 0)),
    ]
    scratch = [pltpu.VMEM((2 * K, COLS), BF16)]
    if not first:
        scratch.append(pltpu.VMEM((K, LANES), F32))
    args = (right,) if first else (right, squares, levels)
    return pl.pallas_call(
        kernel,
        grid_spec=pltpu.PrefetchScalarGridSpec(
            num_scalar_prefetch=1,
            grid=(4,),
            in_specs=[pl.BlockSpec((K, COLS), lambda i, z: (0, 0))]
            + small
            + [pl.BlockSpec((QUARTER, COLS), lambda i, z: (lax.rem(z[0] + i, 4), 0))],
            out_specs=[pl.BlockSpec((K, width), lambda i, z: (0, 0)) for _ in range(4)],
            scratch_shapes=scratch,
        ),
        out_shape=[jax.ShapeDtypeStruct((K, width), F32) for _ in range(4)],
        compiler_params=PARAMS,
        name="left_product_first" if first else "left_product",
    )(z.reshape(1), *args, cross)


def right_product(left, squares, levels, cross, core):
    def kernel(core_ref, left_ref, squares_ref, levels_ref, cross_ref, own_ref, other_ref, shrunk_ref, both_ref, sum_ref, gram_ref):
        step = pl.program_id(0)

        @pl.when(step == 0)
        def _():
            values = shrunk_of(left_ref[...], squares_ref[...], levels_ref[...], 0, NV)
            shrunk_ref[...] = values
            gram_ref[...] = padded(cross_gram(values, values))
            both_ref[...] = jnp.concatenate(split2(values), axis=0)

        high, low = split2(cross_ref[...])
        both = both_ref[:, pl.ds(pl.multiple_of(step * BLOCK, BLOCK), BLOCK)]
        whole = dot(both, high, NN)
        product = whole[:K] + (whole[K:] + dot(both[:K], low, NN))

        @pl.when(step == 0)
        def _():
            sum_ref[...] = product

        @pl.when(step > 0)
        def _():
            sum_ref[...] += product

        @pl.when(step == ROWS // BLOCK - 1)
        def _():
            own = pl.multiple_of(core_ref[0] * HALF, HALF)
            other = pl.multiple_of((1 - core_ref[0]) * HALF, HALF)
            own_ref[:, :HALF] = sum_ref[:, pl.ds(own, HALF)]
            other_ref[:, :HALF] = sum_ref[:, pl.ds(other, HALF)]
            own_ref[:, HALF:] = gram_ref[...]
            other_ref[:, HALF:] = gram_ref[...]

    whole = lambda shape: pl.BlockSpec(shape, lambda i, c: (0, 0))
    return pl.pallas_call(
        kernel,
        grid_spec=pltpu.PrefetchScalarGridSpec(
            num_scalar_prefetch=1,
            grid=(ROWS // BLOCK,),
            in_specs=[
                whole((K, ROWS)),
                whole((1, LANES)),
                whole((2, K)),
                pl.BlockSpec((BLOCK, COLS), lambda i, c: (i, 0)),
            ],
            out_specs=[whole((K, HALF + LANES)), whole((K, HALF + LANES)), whole((K, ROWS))],
            scratch_shapes=[
                pltpu.VMEM((2 * K, ROWS), BF16),
                pltpu.VMEM((K, COLS), F32),
                pltpu.VMEM((K, LANES), F32),
            ],
        ),
        out_shape=[
            jax.ShapeDtypeStruct((K, HALF + LANES), F32),
            jax.ShapeDtypeStruct((K, HALF + LANES), F32),
            jax.ShapeDtypeStruct((K, ROWS), F32),
        ],
        compiler_params=PARAMS,
        name="right_product",
    )(core.reshape(1), left, squares, levels, cross)


def factor(gram, count):
    def kernel(gram_ref, out_ref):
        out_ref[...] = padded(inverse_factor(gram_ref[:, :K], count))

    return pl.pallas_call(
        kernel,
        out_shape=jax.ShapeDtypeStruct((K, LANES), F32),
        compiler_params=PARAMS,
        cost_estimate=pl.CostEstimate(flops=10_000_000, bytes_accessed=8_000_000, transcendentals=0),
        name="factor",
    )(gram)


def assemble(inverse, blocks, places, order):
    width = blocks[0].shape[1]
    n = len(blocks)

    def kernel(places_ref, *refs):
        if inverse is not None:
            inverse_ref, *refs = refs
        *ins, out_ref, squares_ref = refs
        total = jnp.zeros((K, 1), F32)
        for at, block in enumerate(ins):
            values = block[...]
            if inverse is not None:
                values = full_dot(inverse_ref[:, :K], values, NN)
            out_ref[:, pl.ds(pl.multiple_of(places_ref[at] * width, width), width)] = values
            total = total + jnp.sum(values * values, axis=1, keepdims=True)
        squares_ref[...] = to_row(total)

    args = blocks if inverse is None else [inverse, *blocks]
    vmem = pl.BlockSpec(memory_space=pltpu.VMEM)
    return pl.pallas_call(
        kernel,
        in_specs=[pl.BlockSpec(memory_space=pltpu.SMEM)] + [vmem] * len(args),
        out_specs=[vmem, vmem],
        out_shape=[
            jax.ShapeDtypeStruct((K, n * width), F32),
            jax.ShapeDtypeStruct((1, LANES), F32),
        ],
        compiler_params=PARAMS,
        name=order,
    )(places, *args)


def last_shrink(right_sum, squares, levels):
    def kernel(right_ref, squares_ref, levels_ref, shrunk_ref, out_ref):
        sums = right_ref[...]
        values = shrunk_of(sums, squares_ref[...], levels_ref[...], 1, NG)
        shrunk_ref[...] = values
        out_ref[...] = jnp.concatenate(
            [cross_gram(values, values), cross_gram(sums, values), jnp.zeros((K, LANES - 2 * K), F32)],
            axis=1,
        )

    return pl.pallas_call(
        kernel,
        out_shape=[
            jax.ShapeDtypeStruct((K, COLS), F32),
            jax.ShapeDtypeStruct((K, LANES), F32),
        ],
        compiler_params=PARAMS,
        name="last_shrink",
    )(right_sum, squares, levels)


def mix_left(inverse, shrunk):
    def kernel(inverse_ref, shrunk_ref, out_ref):
        out_ref[...] = full_dot(inverse_ref[:, :K], shrunk_ref[...], NN)

    return pl.pallas_call(
        kernel,
        out_shape=jax.ShapeDtypeStruct((K, ROWS), F32),
        compiler_params=PARAMS,
        name="mix_left",
    )(inverse, shrunk)


def deflate(last, right_shrunk, left_dirs, cross):
    def kernel(last_ref, shrunk_ref, left_ref, cross_ref, out_ref, right_ref, strength_ref, terms_ref, scale_ref):
        step = pl.program_id(0)

        @pl.when(step == 0)
        def _():
            inverse = inverse_factor(last_ref[:, :K], NG)
            right = full_dot(inverse, shrunk_ref[...], NN)
            right_ref[...] = right
            high, middle, low = split3(right)
            terms_ref[...] = jnp.concatenate([high, middle, high, low, middle, high], axis=0)
            strength = jnp.sum(inverse * last_ref[:, K : 2 * K], axis=1, keepdims=True) / math.sqrt(NV * NG)
            strength_ref[...] = to_row(strength)
            scale_ref[...] = jnp.broadcast_to(strength / math.sqrt(NV * NG), (K, LANES))

        scaled = left_ref[...] * scale_ref[:, :1]
        high, middle, low = split3(scaled)
        terms = jnp.concatenate([high, high, middle, high, middle, low], axis=0)
        out_ref[...] = cross_ref[...] - dot(terms, terms_ref[...], TN)

    whole = lambda shape: pl.BlockSpec(shape, lambda i: (0, 0))
    return pl.pallas_call(
        kernel,
        grid=(ROWS // BLOCK,),
        in_specs=[
            whole((K, LANES)),
            whole((K, COLS)),
            pl.BlockSpec((K, BLOCK), lambda i: (0, i)),
            pl.BlockSpec((BLOCK, COLS), lambda i: (i, 0)),
        ],
        out_specs=[
            pl.BlockSpec((BLOCK, COLS), lambda i: (i, 0)),
            whole((K, COLS)),
            whole((1, LANES)),
        ],
        out_shape=[
            jax.ShapeDtypeStruct((ROWS, COLS), F32),
            jax.ShapeDtypeStruct((K, COLS), F32),
            jax.ShapeDtypeStruct((1, LANES), F32),
        ],
        scratch_shapes=[pltpu.VMEM((6 * K, COLS), BF16), pltpu.VMEM((K, LANES), F32)],
        compiler_params=PARAMS,
        name="deflate",
    )(last, right_shrunk, left_dirs, cross)


def per_device(cross, start, levels):
    core = (lax.axis_index("vox") % 2).astype(jnp.int32)
    z = (lax.axis_index("var") % 4).astype(jnp.int32)
    quarters = jnp.stack([z] + [(z - step) % 4 for step in STEPS])
    halves = jnp.stack([core, 1 - core])
    right_sum, squares = start, None
    for sweep in range(ITERS):
        parts = left_product(right_sum, squares, levels, cross, z)
        total = parts[0]
        for step in STEPS:
            total = total + shift(parts[step], "var", Z_RINGS, step)
        total = ring_sum(total, "var", Y_RINGS)
        block = total[:, :QUARTER]
        blocks = [block] + [shift(block, "var", Z_RINGS, step) for step in STEPS]
        inverse = factor(total[:, QUARTER:], NG) if sweep else None
        left_sum, squares = assemble(inverse, blocks, quarters, "assemble_left")
        squares = ring_sum(pair_sum(squares), "vox", X_RINGS)

        own, other, left_shrunk = right_product(left_sum, squares, levels, cross, core)
        total = own + shift(other, "vox", CORE_PAIRS, 1)
        total = ring_sum(total, "vox", X_RINGS)
        block = total[:, :HALF]
        blocks = [block, shift(block, "vox", CORE_PAIRS, 1)]
        inverse = factor(total[:, HALF:], NV)
        right_sum, squares = assemble(inverse, blocks, halves, "assemble_right")
        squares = ring_sum(ring_sum(squares, "var", Y_RINGS), "var", Z_RINGS)
    left_dirs = mix_left(inverse, left_shrunk)
    right_shrunk, last = last_shrink(right_sum, squares, levels)
    last = ring_sum(ring_sum(last, "var", Y_RINGS), "var", Z_RINGS)
    deflated, right_dirs, strength = deflate(last, right_shrunk, left_dirs, cross)
    return (deflated, left_dirs, right_dirs, strength[0, :K])


def solution(mesh):
    in_specs = (P("vox", "var"), P(None, "var"), P())
    out_specs = (P("vox", "var"), P(None, "vox"), P(None, "var"), P())
    return jax.shard_map(
        per_device, mesh=mesh, in_specs=in_specs, out_specs=out_specs, check_vma=False
    )
```

time: 774 us -> 192 us (0.25)
  blocking collectives: 357 us -> 0 us
  waiting for transfers between devices: 277 us -> 80.1 us
  matrix products: 92.1 us -> 0 us
  starting transfers between devices: 0.16 us -> 53.1 us
  Pallas kernels: 0 us -> 31.8 us
  other arithmetic: 31.6 us -> 0.39 us
  local copies, waits for them, and re-layouts: 1.18 us -> 25.3 us
  between operations: 14 us -> 0.93 us
    psum x9 -> x0, blocking collectives: 357 us -> none  [the longest x2 139 us: right_update(): gram = lax.psum(local_gram(shrunk), 'var')]
    psum x4 -> x0, waiting for transfers between devices: 277 us -> none  [the longest x2 165 us: left_update(): summed = lax.psum(partial_sum, 'var')]
    dot_general x10 -> x0, matrix products: 86.6 us -> none  [the longest x2 29.8 us: left_update(): lax.dot_general(right_dirs, cross, (((1,), (1,)), ((), ())), precision=HI...]
    ppermute x0 -> x54, waiting for transfers between devices: none -> 80.1 us  [shift(): return lax.ppermute(value, axis, pairs)]
    ppermute x0 -> x54, starting transfers between devices: none -> 53.1 us  [shift(): return lax.ppermute(value, axis, pairs)]
    pallas_call x0 -> x14, Pallas kernels: none -> 31.8 us  [the longest x2 9.53 us: left_product(): pl.pallas_call(kernel, grid_spec=pltpu.PrefetchScalarGridSpec(num_scalar_...]
    another operation x20 -> x2, other arithmetic: 26.7 us -> 0.15 us  [the longest x1 0.08 us: per_device(): halves = jnp.stack([core, 1 - core])]
    unnamed x8 -> x16, local copies, waits for them, and re-layouts: 0.89 us -> 24.7 us
  transfers between devices with their start and end apart: 4 -> 54, of which waited for: 4 -> 41; matrix products, arithmetic and copies ran while one was open for 0% -> 0% of each run, Pallas kernels for 0% -> 2%
where the time goes in v1:
time: 192 us
  waiting for transfers between devices  80.1 us (42%)
  starting transfers between devices  53.1 us (28%)
  Pallas kernels  31.8 us (17%)
  local copies, waits for them, and re-layouts  25.3 us (13%)
    ppermute x54, waiting for transfers between devices, shift(): return lax.ppermute(value, axis, pairs)  80.1 us
    ppermute x54, starting transfers between devices, shift(): return lax.ppermute(value, axis, pairs)  53.1 us
    unnamed x16, local copies, waits for them, and re-layouts  24.7 us
    pallas_call x2, Pallas kernels, left_product(): pl.pallas_call(kernel, grid_spec=pltpu.PrefetchScalarGridSpec(num_scalar_...  9.53 us
    pallas_call x2, Pallas kernels, right_product(): pl.pallas_call(kernel, grid_spec=pltpu.PrefetchScalarGridSpec(num_scalar_...  7.78 us
    pallas_call x1, Pallas kernels, deflate(): pl.pallas_call(kernel, grid=(ROWS // BLOCK,), in_specs=[whole((K, LANES))...  6.9 us
  transfers between devices with their start and end apart: 54, of which 41 were waited for; matrix products, arithmetic and copies ran while one was open for 0% of the time, Pallas kernels for 2%

profile of v1, /device:TPU:0, one launch (start us, length us, event | category | flops | bytes accessed | tf_op | source)
XLA Modules:
  0.0 191.6 jit_solution(11076642844180823696)
XLA Ops:
  0.7 4.6 %copy-done = f32[2048,1536]{1,0:T(8,128)S(1)} copy-done((f32[2048,1536]{1,0:T(8,128)S(1)}, f32[2048,1536]{1,0:T(8,128)}, u32[]{:S(2)}) %copy-start) | copy-done | bytes 12582936
  6.2 4.5 %left_product_first.1 = (f32[32,512]{1,0:T(8,128)S(1)}, f32[32,512]{1,0:T(8,128)S(1)}, f32[32,512]{1,0:T(8,128)S(1)}, f32[32,512]{1,0:T(8,128)S(1)}) custom-call(s32[1]{0:T(128)} %bitcast.2.z_ref, f32[32,1536]{1,0:T(8,128)S(1)} %copy-done.6, f32[2048,1536]{1,0:T(8,128)S(1)} %copy-done), custom_call_target="tpu_custom_call" | custom-call | tf_op jit(solution)/shard_map/left_product_first/pallas_call | solution.py:178
  17.1 3.6 %collective-permute-done.2 = f32[32,512]{1,0:T(8,128)S(1)} collective-permute-done((f32[32,512]{1,0:T(8,128)S(1)}, f32[32,512]{1,0:T(8,128)S(1)}, u32[]{:S(2)}, u32[]{:S(2)}) %collective-permute-start.2) | collective-permute-done | bytes 65568 | tf_op jit(solution)/shard_map/ppermute | solution.py:40
  20.8 3.3 %collective-permute-start.5 = (f32[32,512]{1,0:T(8,128)S(1)}, f32[32,512]{1,0:T(8,128)S(1)}, u32[]{:S(2)}, u32[]{:S(2)}) collective-permute-start(f32[32,512]{1,0:T(8,128)S(1)} %add_add_fusion.5), channel_id=1, source_target_pairs={{0,8},{4,12},{8,0},{12,4},{1,9},{5,13},{9,1},{13,5},{2,10},{6,14},... | collective-permute-start | bytes 196616 | tf_op jit(solution)/shard_map/ppermute | solution.py:40
  40.7 3.0 %collective-permute-start.12 = (f32[1,128]{1,0:T(1,128)S(1)}, f32[1,128]{1,0:T(1,128)S(1)}, u32[]{:S(2)}, u32[]{:S(2)}) collective-permute-start(f32[1,128]{1,0:T(1,128)S(1)} %add.168), channel_id=1, source_target_pairs={{0,64},{32,96},{64,0},{96,32},{16,80},{48,112},{80,16},{112,48},{1... | collective-permute-start | bytes 1544 | tf_op jit(solution)/shard_map/ppermute | solution.py:40
  47.2 2.4 %collective-permute-done.10 = f32[1,128]{1,0:T(1,128)S(1)} collective-permute-done((f32[1,128]{1,0:T(1,128)S(1)}, f32[1,128]{1,0:T(1,128)S(1)}, u32[]{:S(2)}, u32[]{:S(2)}) %collective-permute-start.10) | collective-permute-done | bytes 544 | tf_op jit(solution)/shard_map/ppermute | solution.py:40
  49.6 4.6 %copy-done.1 = f32[2048,1536]{1,0:T(8,128)S(1)} copy-done((f32[2048,1536]{1,0:T(8,128)S(1)}, f32[2048,1536]{1,0:T(8,128)}, u32[]{:S(2)}) %copy-start.1) | copy-done | bytes 12582936
  54.2 4.2 %right_product.2 = (f32[32,896]{1,0:T(8,128)S(1)}, f32[32,896]{1,0:T(8,128)S(1)}, f32[32,2048]{1,0:T(8,128)}) custom-call(s32[1]{0:T(128)} %bitcast.core_ref, f32[32,2048]{1,0:T(8,128)S(1)} %get-tuple-element.34.left_ref, f32[1,128]{1,0:T(1,128)S(1)} %add_add_fusion.13.squares_ref, s32[2,32]{1,0:T(2,128)S(1)} %copy-done.7, f32[2048,1536]{1,0:T(8,128)S(1)} %copy-done.1), custom_call_target="tpu_custom_call" | custom-call | tf_op jit(solution)/shard_map/right_product/pallas_call | solution.py:229
  62.2 5.1 %collective-permute-done.16 = f32[32,896]{1,0:T(8,128)S(1)} collective-permute-done((f32[32,896]{1,0:T(8,128)S(1)}, f32[32,896]{1,0:T(8,128)S(1)}, u32[]{:S(2)}, u32[]{:S(2)}) %collective-permute-start.16) | collective-permute-done | bytes 114720 | tf_op jit(solution)/shard_map/ppermute | solution.py:40
  73.9 2.5 %collective-permute-done.20 = f32[1,128]{1,0:T(1,128)S(1)} collective-permute-done((f32[1,128]{1,0:T(1,128)S(1)}, f32[1,128]{1,0:T(1,128)S(1)}, u32[]{:S(2)}, u32[]{:S(2)}) %collective-permute-start.20) | collective-permute-done | bytes 544 | tf_op jit(solution)/shard_map/ppermute | solution.py:40
  83.7 2.3 %collective-permute-done.21 = f32[1,128]{1,0:T(1,128)S(1)} collective-permute-done((f32[1,128]{1,0:T(1,128)S(1)}, f32[1,128]{1,0:T(1,128)S(1)}, u32[]{:S(2)}, u32[]{:S(2)}) %collective-permute-start.21) | collective-permute-done | bytes 544 | tf_op jit(solution)/shard_map/ppermute | solution.py:40
  86.0 4.6 %copy-done.2 = f32[2048,1536]{1,0:T(8,128)S(1)} copy-done((f32[2048,1536]{1,0:T(8,128)S(1)}, f32[2048,1536]{1,0:T(8,128)}, u32[]{:S(2)}) %copy-start.2) | copy-done | bytes 12582936
  90.6 5.0 %left_product.1 = (f32[32,640]{1,0:T(8,128)S(1)}, f32[32,640]{1,0:T(8,128)S(1)}, f32[32,640]{1,0:T(8,128)S(1)}, f32[32,640]{1,0:T(8,128)S(1)}) custom-call(s32[1]{0:T(128)} %bitcast.2.z_ref, f32[32,1536]{1,0:T(8,128)S(1)} %get-tuple-element.38.refs_0_, f32[1,128]{1,0:T(1,128)S(1)} %add_add_fusion.11.refs_1_, s32[2,32]{1,0:T(2,128)S(1)} %copy-done.7, ...), custom_call_target="tpu_custom_call" | custom-call | tf_op jit(solution)/shard_map/left_product/pallas_call | solution.py:178
  95.8 3.2 %collective-permute-start.25 = (f32[32,640]{1,0:T(8,128)S(1)}, f32[32,640]{1,0:T(8,128)S(1)}, u32[]{:S(2)}, u32[]{:S(2)}) collective-permute-start(f32[32,640]{1,0:T(8,128)S(1)} %get-tuple-element.42), channel_id=1, source_target_pairs={{0,3},{1,0},{2,1},{3,2},{4,7},{5,4},{6,5},{7,6},{8,11},{9,8},{10,9... | collective-permute-start | bytes 245768 | tf_op jit(solution)/shard_map/ppermute | solution.py:40
  99.1 2.7 %collective-permute-done.24 = f32[32,640]{1,0:T(8,128)S(1)} collective-permute-done((f32[32,640]{1,0:T(8,128)S(1)}, f32[32,640]{1,0:T(8,128)S(1)}, u32[]{:S(2)}, u32[]{:S(2)}) %collective-permute-start.24) | collective-permute-done | bytes 81952 | tf_op jit(solution)/shard_map/ppermute | solution.py:40
  101.9 3.1 %collective-permute-done.26 = f32[32,640]{1,0:T(8,128)S(1)} collective-permute-done((f32[32,640]{1,0:T(8,128)S(1)}, f32[32,640]{1,0:T(8,128)S(1)}, u32[]{:S(2)}, u32[]{:S(2)}) %collective-permute-start.26) | collective-permute-done | bytes 81952 | tf_op jit(solution)/shard_map/ppermute | solution.py:40
  107.2 3.8 %collective-permute-done.29 = f32[32,640]{1,0:T(8,128)S(1)} collective-permute-done((f32[32,640]{1,0:T(8,128)S(1)}, f32[32,640]{1,0:T(8,128)S(1)}, u32[]{:S(2)}, u32[]{:S(2)}) %collective-permute-start.29) | collective-permute-done | bytes 81952 | tf_op jit(solution)/shard_map/ppermute | solution.py:40
  115.4 2.8 %collective-permute-done.32.refs_4_ = f32[32,512]{1,0:T(8,128)S(1)} collective-permute-done((f32[32,512]{1,0:T(8,128)S(1)}, f32[32,512]{1,0:T(8,128)S(1)}, u32[]{:S(2)}, u32[]{:S(2)}) %collective-permute-start.32) | collective-permute-done | bytes 65568 | tf_op jit(solution)/shard_map/ppermute | solution.py:40
  124.0 2.7 %collective-permute-done.36 = f32[1,128]{1,0:T(1,128)S(1)} collective-permute-done((f32[1,128]{1,0:T(1,128)S(1)}, f32[1,128]{1,0:T(1,128)S(1)}, u32[]{:S(2)}, u32[]{:S(2)}) %collective-permute-start.36) | collective-permute-done | bytes 544 | tf_op jit(solution)/shard_map/ppermute | solution.py:40
  128.7 4.6 %copy-done.3 = f32[2048,1536]{1,0:T(8,128)S(1)} copy-done((f32[2048,1536]{1,0:T(8,128)S(1)}, f32[2048,1536]{1,0:T(8,128)}, u32[]{:S(2)}) %copy-start.3) | copy-done | bytes 12582936
  133.3 3.5 %right_product.3 = (f32[32,896]{1,0:T(8,128)S(1)}, f32[32,896]{1,0:T(8,128)S(1)}, f32[32,2048]{1,0:T(8,128)S(1)}) custom-call(s32[1]{0:T(128)} %bitcast.core_ref, f32[32,2048]{1,0:T(8,128)S(1)} %get-tuple-element.44.left_ref, f32[1,128]{1,0:T(1,128)S(1)} %add_add_fusion.10.squares_ref, s32[2,32]{1,0:T(2,128)S(1)} %copy-done.7, f32[2048,1536]{1,0:T(8,128)S(1)} %copy-done.3), custom_call_target="tpu_custom_call" | custom-call | tf_op jit(solution)/shard_map/right_product/pallas_call | solution.py:229
  140.5 5.4 %collective-permute-done.40 = f32[32,896]{1,0:T(8,128)S(1)} collective-permute-done((f32[32,896]{1,0:T(8,128)S(1)}, f32[32,896]{1,0:T(8,128)S(1)}, u32[]{:S(2)}, u32[]{:S(2)}) %collective-permute-start.40) | collective-permute-done | bytes 114720 | tf_op jit(solution)/shard_map/ppermute | solution.py:40
  178.7 4.6 %copy-done.4 = f32[2048,1536]{1,0:T(8,128)S(1)} copy-done((f32[2048,1536]{1,0:T(8,128)S(1)}, f32[2048,1536]{1,0:T(8,128)}, u32[]{:S(2)}) %copy-start.4) | copy-done | bytes 12582936
  184.2 6.9 %deflate.1 = (f32[2048,1536]{1,0:T(8,128)}, f32[32,1536]{1,0:T(8,128)}, f32[1,128]{1,0:T(1,128)S(1)}) custom-call(f32[32,128]{1,0:T(8,128)S(1)} %add_add_fusion.6.last_ref, f32[32,1536]{1,0:T(8,128)S(1)} %get-tuple-element.51.shrunk_ref, f32[32,2048]{1,0:T(8,128)S(1)} %copy-done.5, f32[2048,1536]{1,0:T(8,128)S(1)} %copy-done.4), custom_call_target="tpu_custom_call" | custom-call | tf_op jit(solution)/shard_map/deflate/pallas_call | solution.py:356
  (141 shorter events, 97.7 us)
Async XLA Ops:
  10.7 6.4 %collective-permute-start = (f32[32,512]{1,0:T(8,128)S(1)}, f32[32,512]{1,0:T(8,128)S(1)}, u32[]{:S(2)}, u32[]{:S(2)}) collective-permute-start(f32[32,512]{1,0:T(8,128)S(1)} %get-tuple-element.31), channel_id=1, source_target_pairs={{0,1},{1,2},{2,3},{3,0},{4,5},{5,6},{6,7},{7,4},{8,9},{9,10},{10,1... | collective-permute-start | bytes 196616 | tf_op jit(solution)/shard_map/ppermute | solution.py:40
  15.0 5.8 %collective-permute-start.2 = (f32[32,512]{1,0:T(8,128)S(1)}, f32[32,512]{1,0:T(8,128)S(1)}, u32[]{:S(2)}, u32[]{:S(2)}) collective-permute-start(f32[32,512]{1,0:T(8,128)S(1)} %get-tuple-element.33), channel_id=1, source_target_pairs={{0,2},{1,3},{2,0},{3,1},{4,6},{5,7},{6,4},{7,5},{8,10},{9,11},{10,... | collective-permute-start | bytes 196616 | tf_op jit(solution)/shard_map/ppermute | solution.py:40
  20.8 6.1 %collective-permute-start.5 = (f32[32,512]{1,0:T(8,128)S(1)}, f32[32,512]{1,0:T(8,128)S(1)}, u32[]{:S(2)}, u32[]{:S(2)}) collective-permute-start(f32[32,512]{1,0:T(8,128)S(1)} %add_add_fusion.5), channel_id=1, source_target_pairs={{0,8},{4,12},{8,0},{12,4},{1,9},{5,13},{9,1},{13,5},{2,10},{6,14},... | collective-permute-start | bytes 196616 | tf_op jit(solution)/shard_map/ppermute | solution.py:40
  25.1 5.5 %collective-permute-start.3 = (f32[32,512]{1,0:T(8,128)S(1)}, f32[32,512]{1,0:T(8,128)S(1)}, u32[]{:S(2)}, u32[]{:S(2)}) collective-permute-start(f32[32,512]{1,0:T(8,128)S(1)} %add_add_fusion.5), channel_id=1, source_target_pairs={{0,4},{4,8},{8,12},{12,0},{1,5},{5,9},{9,13},{13,1},{2,6},{6,10},{... | collective-permute-start | bytes 196616 | tf_op jit(solution)/shard_map/ppermute | solution.py:40
  30.6 5.8 %collective-permute-start.8 = (f32[32,512]{1,0:T(8,128)S(1)}, f32[32,512]{1,0:T(8,128)S(1)}, u32[]{:S(2)}, u32[]{:S(2)}) collective-permute-start(f32[32,512]{1,0:T(8,128)S(1)} %add_add_fusion.4.refs_0_), channel_id=1, source_target_pairs={{0,2},{1,3},{2,0},{3,1},{4,6},{5,7},{6,4},{7,5},{8,10},{9,11},{10,... | collective-permute-start | bytes 196616 | tf_op jit(solution)/shard_map/ppermute | solution.py:40
  33.3 5.5 %collective-permute-start.6 = (f32[32,512]{1,0:T(8,128)S(1)}, f32[32,512]{1,0:T(8,128)S(1)}, u32[]{:S(2)}, u32[]{:S(2)}) collective-permute-start(f32[32,512]{1,0:T(8,128)S(1)} %add_add_fusion.4.refs_0_), channel_id=1, source_target_pairs={{0,1},{1,2},{2,3},{3,0},{4,5},{5,6},{6,7},{7,4},{8,9},{9,10},{10,1... | collective-permute-start | bytes 196616 | tf_op jit(solution)/shard_map/ppermute | solution.py:40
  59.7 7.6 %collective-permute-start.16 = (f32[32,896]{1,0:T(8,128)S(1)}, f32[32,896]{1,0:T(8,128)S(1)}, u32[]{:S(2)}, u32[]{:S(2)}) collective-permute-start(f32[32,896]{1,0:T(8,128)S(1)} %add.172), channel_id=1, source_target_pairs={{0,64},{32,96},{64,0},{96,32},{16,80},{48,112},{80,16},{112,48},{1... | collective-permute-start | bytes 344072 | tf_op jit(solution)/shard_map/ppermute | solution.py:40
  60.1 7.2 %collective-permute-start.15 = (f32[32,896]{1,0:T(8,128)S(1)}, f32[32,896]{1,0:T(8,128)S(1)}, u32[]{:S(2)}, u32[]{:S(2)}) collective-permute-start(f32[32,896]{1,0:T(8,128)S(1)} %add.172), channel_id=1, source_target_pairs={{0,96},{32,0},{64,32},{96,64},{16,112},{48,16},{80,48},{112,80},{1... | collective-permute-start | bytes 344072 | tf_op jit(solution)/shard_map/ppermute | solution.py:40
  62.2 6.8 %collective-permute-start.14 = (f32[32,896]{1,0:T(8,128)S(1)}, f32[32,896]{1,0:T(8,128)S(1)}, u32[]{:S(2)}, u32[]{:S(2)}) collective-permute-start(f32[32,896]{1,0:T(8,128)S(1)} %add.172), channel_id=1, source_target_pairs={{0,32},{32,64},{64,96},{96,0},{16,48},{48,80},{80,112},{112,16},{1... | collective-permute-start | bytes 344072 | tf_op jit(solution)/shard_map/ppermute | solution.py:40
  71.3 5.1 %collective-permute-start.20 = (f32[1,128]{1,0:T(1,128)S(1)}, f32[1,128]{1,0:T(1,128)S(1)}, u32[]{:S(2)}, u32[]{:S(2)}) collective-permute-start(f32[1,128]{1,0:T(1,128)S(1)} %get-tuple-element.39), channel_id=1, source_target_pairs={{0,8},{4,12},{8,0},{12,4},{1,9},{5,13},{9,1},{13,5},{2,10},{6,14},... | collective-permute-start | bytes 1544 | tf_op jit(solution)/shard_map/ppermute | solution.py:40
  95.6 6.1 %collective-permute-start.24 = (f32[32,640]{1,0:T(8,128)S(1)}, f32[32,640]{1,0:T(8,128)S(1)}, u32[]{:S(2)}, u32[]{:S(2)}) collective-permute-start(f32[32,640]{1,0:T(8,128)S(1)} %get-tuple-element.41), channel_id=1, source_target_pairs={{0,1},{1,2},{2,3},{3,0},{4,5},{5,6},{6,7},{7,4},{8,9},{9,10},{10,1... | collective-permute-start | bytes 245768 | tf_op jit(solution)/shard_map/ppermute | solution.py:40
  95.8 6.1 %collective-permute-start.25 = (f32[32,640]{1,0:T(8,128)S(1)}, f32[32,640]{1,0:T(8,128)S(1)}, u32[]{:S(2)}, u32[]{:S(2)}) collective-permute-start(f32[32,640]{1,0:T(8,128)S(1)} %get-tuple-element.42), channel_id=1, source_target_pairs={{0,3},{1,0},{2,1},{3,2},{4,7},{5,4},{6,5},{7,6},{8,11},{9,8},{10,9... | collective-permute-start | bytes 245768 | tf_op jit(solution)/shard_map/ppermute | solution.py:40
  99.0 5.9 %collective-permute-start.26 = (f32[32,640]{1,0:T(8,128)S(1)}, f32[32,640]{1,0:T(8,128)S(1)}, u32[]{:S(2)}, u32[]{:S(2)}) collective-permute-start(f32[32,640]{1,0:T(8,128)S(1)} %get-tuple-element.43), channel_id=1, source_target_pairs={{0,2},{1,3},{2,0},{3,1},{4,6},{5,7},{6,4},{7,5},{8,10},{9,11},{10,... | collective-permute-start | bytes 245768 | tf_op jit(solution)/shard_map/ppermute | solution.py:40
  105.0 6.0 %collective-permute-start.29 = (f32[32,640]{1,0:T(8,128)S(1)}, f32[32,640]{1,0:T(8,128)S(1)}, u32[]{:S(2)}, u32[]{:S(2)}) collective-permute-start(f32[32,640]{1,0:T(8,128)S(1)} %add_add_fusion.3), channel_id=1, source_target_pairs={{0,8},{4,12},{8,0},{12,4},{1,9},{5,13},{9,1},{13,5},{2,10},{6,14},... | collective-permute-start | bytes 245768 | tf_op jit(solution)/shard_map/ppermute | solution.py:40
  105.1 5.9 %collective-permute-start.28 = (f32[32,640]{1,0:T(8,128)S(1)}, f32[32,640]{1,0:T(8,128)S(1)}, u32[]{:S(2)}, u32[]{:S(2)}) collective-permute-start(f32[32,640]{1,0:T(8,128)S(1)} %add_add_fusion.3), channel_id=1, source_target_pairs={{0,12},{4,0},{8,4},{12,8},{1,13},{5,1},{9,5},{13,9},{2,14},{6,2},{... | collective-permute-start | bytes 245768 | tf_op jit(solution)/shard_map/ppermute | solution.py:40
  106.6 5.7 %collective-permute-start.27 = (f32[32,640]{1,0:T(8,128)S(1)}, f32[32,640]{1,0:T(8,128)S(1)}, u32[]{:S(2)}, u32[]{:S(2)}) collective-permute-start(f32[32,640]{1,0:T(8,128)S(1)} %add_add_fusion.3), channel_id=1, source_target_pairs={{0,4},{4,8},{8,12},{12,0},{1,5},{5,9},{9,13},{13,1},{2,6},{6,10},{... | collective-permute-start | bytes 245768 | tf_op jit(solution)/shard_map/ppermute | solution.py:40
  112.3 5.8 %collective-permute-start.32 = (f32[32,512]{1,0:T(8,128)S(1)}, f32[32,512]{1,0:T(8,128)S(1)}, u32[]{:S(2)}, u32[]{:S(2)}) collective-permute-start(f32[32,512]{1,0:T(8,128)S(1)} %slice.31.refs_1_), channel_id=1, source_target_pairs={{0,2},{1,3},{2,0},{3,1},{4,6},{5,7},{6,4},{7,5},{8,10},{9,11},{10,... | collective-permute-start | bytes 196616 | tf_op jit(solution)/shard_map/ppermute | solution.py:40
  112.4 5.8 %collective-permute-start.31 = (f32[32,512]{1,0:T(8,128)S(1)}, f32[32,512]{1,0:T(8,128)S(1)}, u32[]{:S(2)}, u32[]{:S(2)}) collective-permute-start(f32[32,512]{1,0:T(8,128)S(1)} %slice.31.refs_1_), channel_id=1, source_target_pairs={{0,3},{1,0},{2,1},{3,2},{4,7},{5,4},{6,5},{7,6},{8,11},{9,8},{10,9... | collective-permute-start | bytes 196616 | tf_op jit(solution)/shard_map/ppermute | solution.py:40
  114.0 5.5 %collective-permute-start.30 = (f32[32,512]{1,0:T(8,128)S(1)}, f32[32,512]{1,0:T(8,128)S(1)}, u32[]{:S(2)}, u32[]{:S(2)}) collective-permute-start(f32[32,512]{1,0:T(8,128)S(1)} %slice.31.refs_1_), channel_id=1, source_target_pairs={{0,1},{1,2},{2,3},{3,0},{4,5},{5,6},{6,7},{7,4},{8,9},{9,10},{10,1... | collective-permute-start | bytes 196616 | tf_op jit(solution)/shard_map/ppermute | solution.py:40
  138.3 7.6 %collective-permute-start.40 = (f32[32,896]{1,0:T(8,128)S(1)}, f32[32,896]{1,0:T(8,128)S(1)}, u32[]{:S(2)}, u32[]{:S(2)}) collective-permute-start(f32[32,896]{1,0:T(8,128)S(1)} %add.192), channel_id=1, source_target_pairs={{0,64},{32,96},{64,0},{96,32},{16,80},{48,112},{80,16},{112,48},{1... | collective-permute-start | bytes 344072 | tf_op jit(solution)/shard_map/ppermute | solution.py:40
  138.4 7.5 %collective-permute-start.39 = (f32[32,896]{1,0:T(8,128)S(1)}, f32[32,896]{1,0:T(8,128)S(1)}, u32[]{:S(2)}, u32[]{:S(2)}) collective-permute-start(f32[32,896]{1,0:T(8,128)S(1)} %add.192), channel_id=1, source_target_pairs={{0,96},{32,0},{64,32},{96,64},{16,112},{48,16},{80,48},{112,80},{1... | collective-permute-start | bytes 344072 | tf_op jit(solution)/shard_map/ppermute | solution.py:40
  139.8 7.7 %collective-permute-start.38 = (f32[32,896]{1,0:T(8,128)S(1)}, f32[32,896]{1,0:T(8,128)S(1)}, u32[]{:S(2)}, u32[]{:S(2)}) collective-permute-start(f32[32,896]{1,0:T(8,128)S(1)} %add.192), channel_id=1, source_target_pairs={{0,32},{32,64},{64,96},{96,0},{16,48},{48,80},{80,112},{112,16},{1... | collective-permute-start | bytes 344072 | tf_op jit(solution)/shard_map/ppermute | solution.py:40
  164.1 5.3 %collective-permute-start.50 = (f32[32,128]{1,0:T(8,128)S(1)}, f32[32,128]{1,0:T(8,128)S(1)}, u32[]{:S(2)}, u32[]{:S(2)}) collective-permute-start(f32[32,128]{1,0:T(8,128)S(1)} %get-tuple-element.50), channel_id=1, source_target_pairs={{0,8},{4,12},{8,0},{12,4},{1,9},{5,13},{9,1},{13,5},{2,10},{6,14},... | collective-permute-start | bytes 49160 | tf_op jit(solution)/shard_map/ppermute | solution.py:40
  171.4 5.3 %collective-permute-start.53 = (f32[32,128]{1,0:T(8,128)S(1)}, f32[32,128]{1,0:T(8,128)S(1)}, u32[]{:S(2)}, u32[]{:S(2)}) collective-permute-start(f32[32,128]{1,0:T(8,128)S(1)} %add_add_fusion.7), channel_id=1, source_target_pairs={{0,2},{1,3},{2,0},{3,1},{4,6},{5,7},{6,4},{7,5},{8,10},{9,11},{10,... | collective-permute-start | bytes 49160 | tf_op jit(solution)/shard_map/ppermute | solution.py:40
  (38 other events, 192.1 us)

commit v2 on v1

--- a/solution.py
+++ b/solution.py
@@ -32,7 +32,8 @@
 Z_RINGS = [[y * 4 + z for z in range(4)] for y in range(4)]
 STEPS = (1, 3, 2)
 
-PARAMS = pltpu.CompilerParams(vmem_limit_bytes=40 * 2**20)
+PARAMS = pltpu.CompilerParams(vmem_limit_bytes=24 * 2**20)
+FIRST_PARAMS = pltpu.CompilerParams(vmem_limit_bytes=40 * 2**20)
 
 
 def shift(value, axis, rings, step):
@@ -137,13 +138,37 @@
     return (jnp.concatenate(blocks, axis=0) * scale)[:, :K]
 
 
-def left_product(right, squares, levels, cross, z):
+Z_AT, CORE_AT = 0, 4
+
+
+def own_places():
+    def kernel(out_ref):
+        z = lax.rem(lax.axis_index("var"), 4)
+        core = lax.rem(lax.axis_index("vox"), 2)
+        out_ref[Z_AT] = z
+        for at, step in enumerate(STEPS):
+            out_ref[Z_AT + 1 + at] = lax.rem(z + 4 - step, 4)
+        out_ref[CORE_AT] = core
+        out_ref[CORE_AT + 1] = 1 - core
+        out_ref[6] = 0
+        out_ref[7] = 0
+
+    return pl.pallas_call(
+        kernel,
+        out_specs=pl.BlockSpec(memory_space=pltpu.SMEM),
+        out_shape=jax.ShapeDtypeStruct((8,), jnp.int32),
+        compiler_params=PARAMS,
+        name="own_places",
+    )()
+
+
+def left_product(right, squares, levels, cross, places):
     first = squares is None
     width = QUARTER if first else QUARTER + LANES
 
     def kernel(z_ref, *refs):
         if first:
-            right_ref, cross_ref, *outs, both_ref = refs
+            right_ref, cross_ref, *outs, kept_ref, both_ref = refs
         else:
             right_ref, squares_ref, levels_ref, cross_ref, *outs, both_ref, gram_ref = refs
         step = pl.program_id(0)
@@ -156,7 +181,10 @@
                 gram_ref[...] = padded(cross_gram(values, values))
             both_ref[...] = jnp.concatenate(split2(values), axis=0)
 
-        high, low = split2(cross_ref[...])
+        block = cross_ref[...]
+        if first:
+            kept_ref[...] = block
+        high, low = split2(block)
         whole = dot(both_ref[...], high, NT)
         product = whole[:K] + (whole[K:] + dot(both_ref[:K], low, NT))
         for at in range(4):
@@ -182,17 +210,19 @@
             grid=(4,),
             in_specs=[pl.BlockSpec((K, COLS), lambda i, z: (0, 0))]
             + small
-            + [pl.BlockSpec((QUARTER, COLS), lambda i, z: (lax.rem(z[0] + i, 4), 0))],
-            out_specs=[pl.BlockSpec((K, width), lambda i, z: (0, 0)) for _ in range(4)],
+            + [pl.BlockSpec((QUARTER, COLS), lambda i, z: (lax.rem(z[Z_AT] + i, 4), 0))],
+            out_specs=[pl.BlockSpec((K, width), lambda i, z: (0, 0)) for _ in range(4)]
+            + [pl.BlockSpec((QUARTER, COLS), lambda i, z: (lax.rem(z[Z_AT] + i, 4), 0))] * first,
             scratch_shapes=scratch,
         ),
-        out_shape=[jax.ShapeDtypeStruct((K, width), F32) for _ in range(4)],
-        compiler_params=PARAMS,
+        out_shape=[jax.ShapeDtypeStruct((K, width), F32) for _ in range(4)]
+        + [jax.ShapeDtypeStruct((ROWS, COLS), F32)] * first,
+        compiler_params=FIRST_PARAMS if first else PARAMS,
         name="left_product_first" if first else "left_product",
-    )(z.reshape(1), *args, cross)
-
-
-def right_product(left, squares, levels, cross, core):
+    )(places, *args, cross)
+
+
+def right_product(left, squares, levels, cross, places):
     def kernel(core_ref, left_ref, squares_ref, levels_ref, cross_ref, own_ref, other_ref, shrunk_ref, both_ref, sum_ref, gram_ref):
         step = pl.program_id(0)
 
@@ -218,8 +248,8 @@
 
         @pl.when(step == ROWS // BLOCK - 1)
         def _():
-            own = pl.multiple_of(core_ref[0] * HALF, HALF)
-            other = pl.multiple_of((1 - core_ref[0]) * HALF, HALF)
+            own = pl.multiple_of(core_ref[CORE_AT] * HALF, HALF)
+            other = pl.multiple_of((1 - core_ref[CORE_AT]) * HALF, HALF)
             own_ref[:, :HALF] = sum_ref[:, pl.ds(own, HALF)]
             other_ref[:, :HALF] = sum_ref[:, pl.ds(other, HALF)]
             own_ref[:, HALF:] = gram_ref[...]
@@ -251,7 +281,7 @@
         ],
         compiler_params=PARAMS,
         name="right_product",
-    )(core.reshape(1), left, squares, levels, cross)
+    )(places, left, squares, levels, cross)
 
 
 def factor(gram, count):
@@ -267,7 +297,7 @@
     )(gram)
 
 
-def assemble(inverse, blocks, places, order):
+def assemble(inverse, blocks, places, start, order):
     width = blocks[0].shape[1]
     n = len(blocks)
 
@@ -280,7 +310,7 @@
             values = block[...]
             if inverse is not None:
                 values = full_dot(inverse_ref[:, :K], values, NN)
-            out_ref[:, pl.ds(pl.multiple_of(places_ref[at] * width, width), width)] = values
+            out_ref[:, pl.ds(pl.multiple_of(places_ref[start + at] * width, width), width)] = values
             total = total + jnp.sum(values * values, axis=1, keepdims=True)
         squares_ref[...] = to_row(total)
 
@@ -321,19 +351,25 @@
 
 
 def mix_left(inverse, shrunk):
-    def kernel(inverse_ref, shrunk_ref, out_ref):
-        out_ref[...] = full_dot(inverse_ref[:, :K], shrunk_ref[...], NN)
-
-    return pl.pallas_call(
-        kernel,
-        out_shape=jax.ShapeDtypeStruct((K, ROWS), F32),
+    def kernel(inverse_ref, shrunk_ref, out_ref, terms_ref):
+        left = full_dot(inverse_ref[:, :K], shrunk_ref[...], NN)
+        out_ref[...] = left
+        high, middle, low = split3(left)
+        terms_ref[...] = jnp.concatenate([high, high, middle, high, middle, low], axis=0)
+
+    return pl.pallas_call(
+        kernel,
+        out_shape=[
+            jax.ShapeDtypeStruct((K, ROWS), F32),
+            jax.ShapeDtypeStruct((6 * K, ROWS), BF16),
+        ],
         compiler_params=PARAMS,
         name="mix_left",
     )(inverse, shrunk)
 
 
-def deflate(last, right_shrunk, left_dirs, cross):
-    def kernel(last_ref, shrunk_ref, left_ref, cross_ref, out_ref, right_ref, strength_ref, terms_ref, scale_ref):
+def deflate(last, right_shrunk, left_terms, cross):
+    def kernel(last_ref, shrunk_ref, left_ref, cross_ref, out_ref, right_ref, strength_ref, terms_ref):
         step = pl.program_id(0)
 
         @pl.when(step == 0)
@@ -341,16 +377,12 @@
             inverse = inverse_factor(last_ref[:, :K], NG)
             right = full_dot(inverse, shrunk_ref[...], NN)
             right_ref[...] = right
-            high, middle, low = split3(right)
+            strength = jnp.sum(inverse * last_ref[:, K : 2 * K], axis=1, keepdims=True) / math.sqrt(NV * NG)
+            strength_ref[...] = to_row(strength)[:, :K]
+            high, middle, low = split3(right * (strength / math.sqrt(NV * NG)))
             terms_ref[...] = jnp.concatenate([high, middle, high, low, middle, high], axis=0)
-            strength = jnp.sum(inverse * last_ref[:, K : 2 * K], axis=1, keepdims=True) / math.sqrt(NV * NG)
-            strength_ref[...] = to_row(strength)
-            scale_ref[...] = jnp.broadcast_to(strength / math.sqrt(NV * NG), (K, LANES))
-
-        scaled = left_ref[...] * scale_ref[:, :1]
-        high, middle, low = split3(scaled)
-        terms = jnp.concatenate([high, high, middle, high, middle, low], axis=0)
-        out_ref[...] = cross_ref[...] - dot(terms, terms_ref[...], TN)
+
+        out_ref[...] = cross_ref[...] - dot(left_ref[...], terms_ref[...], TN)
 
     whole = lambda shape: pl.BlockSpec(shape, lambda i: (0, 0))
     return pl.pallas_call(
@@ -359,33 +391,32 @@
         in_specs=[
             whole((K, LANES)),
             whole((K, COLS)),
-            pl.BlockSpec((K, BLOCK), lambda i: (0, i)),
+            pl.BlockSpec((6 * K, BLOCK), lambda i: (0, i)),
             pl.BlockSpec((BLOCK, COLS), lambda i: (i, 0)),
         ],
         out_specs=[
             pl.BlockSpec((BLOCK, COLS), lambda i: (i, 0)),
             whole((K, COLS)),
-            whole((1, LANES)),
+            whole((1, K)),
         ],
         out_shape=[
             jax.ShapeDtypeStruct((ROWS, COLS), F32),
             jax.ShapeDtypeStruct((K, COLS), F32),
-            jax.ShapeDtypeStruct((1, LANES), F32),
-        ],
-        scratch_shapes=[pltpu.VMEM((6 * K, COLS), BF16), pltpu.VMEM((K, LANES), F32)],
+            jax.ShapeDtypeStruct((1, K), F32),
+        ],
+        scratch_shapes=[pltpu.VMEM((6 * K, COLS), BF16)],
         compiler_params=PARAMS,
         name="deflate",
-    )(last, right_shrunk, left_dirs, cross)
+    )(last, right_shrunk, left_terms, cross)
 
 
 def per_device(cross, start, levels):
-    core = (lax.axis_index("vox") % 2).astype(jnp.int32)
-    z = (lax.axis_index("var") % 4).astype(jnp.int32)
-    quarters = jnp.stack([z] + [(z - step) % 4 for step in STEPS])
-    halves = jnp.stack([core, 1 - core])
+    places = own_places()
     right_sum, squares = start, None
     for sweep in range(ITERS):
-        parts = left_product(right_sum, squares, levels, cross, z)
+        parts = left_product(right_sum, squares, levels, cross, places)
+        if sweep == 0:
+            cross = parts[4]
         total = parts[0]
         for step in STEPS:
             total = total + shift(parts[step], "var", Z_RINGS, step)
@@ -393,22 +424,22 @@
         block = total[:, :QUARTER]
         blocks = [block] + [shift(block, "var", Z_RINGS, step) for step in STEPS]
         inverse = factor(total[:, QUARTER:], NG) if sweep else None
-        left_sum, squares = assemble(inverse, blocks, quarters, "assemble_left")
+        left_sum, squares = assemble(inverse, blocks, places, Z_AT, "assemble_left")
         squares = ring_sum(pair_sum(squares), "vox", X_RINGS)
 
-        own, other, left_shrunk = right_product(left_sum, squares, levels, cross, core)
+        own, other, left_shrunk = right_product(left_sum, squares, levels, cross, places)
         total = own + shift(other, "vox", CORE_PAIRS, 1)
         total = ring_sum(total, "vox", X_RINGS)
         block = total[:, :HALF]
         blocks = [block, shift(block, "vox", CORE_PAIRS, 1)]
         inverse = factor(total[:, HALF:], NV)
-        right_sum, squares = assemble(inverse, blocks, halves, "assemble_right")
+        right_sum, squares = assemble(inverse, blocks, places, CORE_AT, "assemble_right")
         squares = ring_sum(ring_sum(squares, "var", Y_RINGS), "var", Z_RINGS)
-    left_dirs = mix_left(inverse, left_shrunk)
+    left_dirs, left_terms = mix_left(inverse, left_shrunk)
     right_shrunk, last = last_shrink(right_sum, squares, levels)
     last = ring_sum(ring_sum(last, "var", Y_RINGS), "var", Z_RINGS)
-    deflated, right_dirs, strength = deflate(last, right_shrunk, left_dirs, cross)
-    return (deflated, left_dirs, right_dirs, strength[0, :K])
+    deflated, right_dirs, strength = deflate(last, right_shrunk, left_terms, cross)
+    return (deflated, left_dirs, right_dirs, strength.reshape(K))
 
 
 def solution(mesh):

time: 192 us -> 174 us (0.906)
  local copies, waits for them, and re-layouts: 25.3 us -> 0.96 us
  Pallas kernels: 31.8 us -> 38.5 us
    unnamed x16 -> x4, local copies, waits for them, and re-layouts: 24.7 us -> 0.93 us
    pallas_call x2, Pallas kernels: 9.53 us -> 13.7 us  [left_product(): pl.pallas_call(kernel, grid_spec=pltpu.PrefetchScalarGridSpec(num_scalar_...]
    pallas_call x2, Pallas kernels: 7.78 us -> 9.7 us  [right_product(): pl.pallas_call(kernel, grid_spec=pltpu.PrefetchScalarGridSpec(num_scalar_...]
where the time goes in v2:
time: 174 us
  waiting for transfers between devices  80.2 us (46%)
  starting transfers between devices  53.1 us (31%)
  Pallas kernels  38.5 us (22%)
    ppermute x54, waiting for transfers between devices, shift(): return lax.ppermute(value, axis, pairs)  80.2 us
    ppermute x54, starting transfers between devices, shift(): return lax.ppermute(value, axis, pairs)  53.1 us
    pallas_call x2, Pallas kernels, left_product(): pl.pallas_call(kernel, grid_spec=pltpu.PrefetchScalarGridSpec(num_scalar_...  13.7 us
    pallas_call x2, Pallas kernels, right_product(): pl.pallas_call(kernel, grid_spec=pltpu.PrefetchScalarGridSpec(num_scalar_...  9.7 us
    pallas_call x1, Pallas kernels, deflate(): pl.pallas_call(kernel, grid=(ROWS // BLOCK,), in_specs=[whole((K, LANES))...  6.84 us
  transfers between devices with their start and end apart: 54, of which 41 were waited for; matrix products, arithmetic and copies ran while one was open for 0% of the time, Pallas kernels for 2%

profile of v2, /device:TPU:0, one launch (start us, length us, event | category | flops | bytes accessed | tf_op | source)
XLA Modules:
  0.0 173.9 jit_solution(4430403257806238330)
XLA Ops:
  2.2 8.1 %left_product_first.1 = (f32[32,512]{1,0:T(8,128)S(1)}, f32[32,512]{1,0:T(8,128)S(1)}, f32[32,512]{1,0:T(8,128)S(1)}, f32[32,512]{1,0:T(8,128)S(1)}, f32[2048,1536]{1,0:T(8,128)S(1)}) custom-call(s32[8]{0:T(128)S(1)} %own_places.1.z_ref.places_ref.core_ref, f32[32,1536]{1,0:T(8,128)S(1)} %copy-done, f32[2048,1536]{1,0:T(8,128)} %refs_1_.1), custom_call_target="tpu_custom_call" | custom-call | tf_op jit(solution)/shard_map/left_product_first/pallas_call | solution.py:206
  12.4 2.2 %collective-permute-start.1 = (f32[32,512]{1,0:T(8,128)S(1)}, f32[32,512]{1,0:T(8,128)S(1)}, u32[]{:S(2)}, u32[]{:S(2)}) collective-permute-start(f32[32,512]{1,0:T(8,128)S(1)} %get-tuple-element.35), channel_id=1, source_target_pairs={{0,3},{1,0},{2,1},{3,2},{4,7},{5,4},{6,5},{7,6},{8,11},{9,8},{10,9... | collective-permute-start | bytes 196616 | tf_op jit(solution)/shard_map/ppermute | solution.py:41
  16.8 3.6 %collective-permute-done.2 = f32[32,512]{1,0:T(8,128)S(1)} collective-permute-done((f32[32,512]{1,0:T(8,128)S(1)}, f32[32,512]{1,0:T(8,128)S(1)}, u32[]{:S(2)}, u32[]{:S(2)}) %collective-permute-start.2) | collective-permute-done | bytes 65568 | tf_op jit(solution)/shard_map/ppermute | solution.py:41
  20.4 3.3 %collective-permute-start.5 = (f32[32,512]{1,0:T(8,128)S(1)}, f32[32,512]{1,0:T(8,128)S(1)}, u32[]{:S(2)}, u32[]{:S(2)}) collective-permute-start(f32[32,512]{1,0:T(8,128)S(1)} %add_add_fusion.5), channel_id=1, source_target_pairs={{0,8},{4,12},{8,0},{12,4},{1,9},{5,13},{9,1},{13,5},{2,10},{6,14},... | collective-permute-start | bytes 196616 | tf_op jit(solution)/shard_map/ppermute | solution.py:41
  27.9 2.3 %collective-permute-done.3 = f32[32,512]{1,0:T(8,128)S(1)} collective-permute-done((f32[32,512]{1,0:T(8,128)S(1)}, f32[32,512]{1,0:T(8,128)S(1)}, u32[]{:S(2)}, u32[]{:S(2)}) %collective-permute-start.3) | collective-permute-done | bytes 65568 | tf_op jit(solution)/shard_map/ppermute | solution.py:41
  40.3 3.0 %collective-permute-start.12 = (f32[1,128]{1,0:T(1,128)S(1)}, f32[1,128]{1,0:T(1,128)S(1)}, u32[]{:S(2)}, u32[]{:S(2)}) collective-permute-start(f32[1,128]{1,0:T(1,128)S(1)} %add.144), channel_id=1, source_target_pairs={{0,64},{32,96},{64,0},{96,32},{16,80},{48,112},{80,16},{112,48},{1... | collective-permute-start | bytes 1544 | tf_op jit(solution)/shard_map/ppermute | solution.py:41
  46.8 2.4 %collective-permute-done.10 = f32[1,128]{1,0:T(1,128)S(1)} collective-permute-done((f32[1,128]{1,0:T(1,128)S(1)}, f32[1,128]{1,0:T(1,128)S(1)}, u32[]{:S(2)}, u32[]{:S(2)}) %collective-permute-start.10) | collective-permute-done | bytes 544 | tf_op jit(solution)/shard_map/ppermute | solution.py:41
  49.2 5.2 %right_product.2 = (f32[32,896]{1,0:T(8,128)S(1)}, f32[32,896]{1,0:T(8,128)S(1)}, f32[32,2048]{1,0:T(8,128)}) custom-call(s32[8]{0:T(128)S(1)} %own_places.1.z_ref.places_ref.core_ref, f32[32,2048]{1,0:T(8,128)S(1)} %get-tuple-element.37.left_ref, f32[1,128]{1,0:T(1,128)S(1)} %add_add_fusion.13.squares_ref, s32[2,32]{1,0:T(2,128)S(1)} %copy-done.1, ...), custom_call_target="tpu_custom_call" | custom-call | tf_op jit(solution)/shard_map/right_product/pallas_call | solution.py:259
  58.2 5.1 %collective-permute-done.16 = f32[32,896]{1,0:T(8,128)S(1)} collective-permute-done((f32[32,896]{1,0:T(8,128)S(1)}, f32[32,896]{1,0:T(8,128)S(1)}, u32[]{:S(2)}, u32[]{:S(2)}) %collective-permute-start.16) | collective-permute-done | bytes 114720 | tf_op jit(solution)/shard_map/ppermute | solution.py:41
  69.9 2.5 %collective-permute-done.20 = f32[1,128]{1,0:T(1,128)S(1)} collective-permute-done((f32[1,128]{1,0:T(1,128)S(1)}, f32[1,128]{1,0:T(1,128)S(1)}, u32[]{:S(2)}, u32[]{:S(2)}) %collective-permute-start.20) | collective-permute-done | bytes 544 | tf_op jit(solution)/shard_map/ppermute | solution.py:41
  79.6 2.3 %collective-permute-done.21 = f32[1,128]{1,0:T(1,128)S(1)} collective-permute-done((f32[1,128]{1,0:T(1,128)S(1)}, f32[1,128]{1,0:T(1,128)S(1)}, u32[]{:S(2)}, u32[]{:S(2)}) %collective-permute-start.21) | collective-permute-done | bytes 544 | tf_op jit(solution)/shard_map/ppermute | solution.py:41
  82.0 5.5 %left_product.1 = (f32[32,640]{1,0:T(8,128)S(1)}, f32[32,640]{1,0:T(8,128)S(1)}, f32[32,640]{1,0:T(8,128)S(1)}, f32[32,640]{1,0:T(8,128)S(1)}) custom-call(s32[8]{0:T(128)S(1)} %own_places.1.z_ref.places_ref.core_ref, f32[32,1536]{1,0:T(8,128)S(1)} %get-tuple-element.42.refs_0_, f32[1,128]{1,0:T(1,128)S(1)} %add_add_fusion.11.refs_1_, ...), custom_call_target="tpu_custom_call" | custom-call | tf_op jit(solution)/shard_map/left_product/pallas_call | solution.py:206
  87.8 3.2 %collective-permute-start.25 = (f32[32,640]{1,0:T(8,128)S(1)}, f32[32,640]{1,0:T(8,128)S(1)}, u32[]{:S(2)}, u32[]{:S(2)}) collective-permute-start(f32[32,640]{1,0:T(8,128)S(1)} %get-tuple-element.46), channel_id=1, source_target_pairs={{0,3},{1,0},{2,1},{3,2},{4,7},{5,4},{6,5},{7,6},{8,11},{9,8},{10,9... | collective-permute-start | bytes 245768 | tf_op jit(solution)/shard_map/ppermute | solution.py:41
  91.0 2.7 %collective-permute-done.24 = f32[32,640]{1,0:T(8,128)S(1)} collective-permute-done((f32[32,640]{1,0:T(8,128)S(1)}, f32[32,640]{1,0:T(8,128)S(1)}, u32[]{:S(2)}, u32[]{:S(2)}) %collective-permute-start.24) | collective-permute-done | bytes 81952 | tf_op jit(solution)/shard_map/ppermute | solution.py:41
  93.9 3.1 %collective-permute-done.26 = f32[32,640]{1,0:T(8,128)S(1)} collective-permute-done((f32[32,640]{1,0:T(8,128)S(1)}, f32[32,640]{1,0:T(8,128)S(1)}, u32[]{:S(2)}, u32[]{:S(2)}) %collective-permute-start.26) | collective-permute-done | bytes 81952 | tf_op jit(solution)/shard_map/ppermute | solution.py:41
  99.2 3.8 %collective-permute-done.29 = f32[32,640]{1,0:T(8,128)S(1)} collective-permute-done((f32[32,640]{1,0:T(8,128)S(1)}, f32[32,640]{1,0:T(8,128)S(1)}, u32[]{:S(2)}, u32[]{:S(2)}) %collective-permute-start.29) | collective-permute-done | bytes 81952 | tf_op jit(solution)/shard_map/ppermute | solution.py:41
  107.3 2.8 %collective-permute-done.32.refs_4_ = f32[32,512]{1,0:T(8,128)S(1)} collective-permute-done((f32[32,512]{1,0:T(8,128)S(1)}, f32[32,512]{1,0:T(8,128)S(1)}, u32[]{:S(2)}, u32[]{:S(2)}) %collective-permute-start.32) | collective-permute-done | bytes 65568 | tf_op jit(solution)/shard_map/ppermute | solution.py:41
  115.9 2.7 %collective-permute-done.36 = f32[1,128]{1,0:T(1,128)S(1)} collective-permute-done((f32[1,128]{1,0:T(1,128)S(1)}, f32[1,128]{1,0:T(1,128)S(1)}, u32[]{:S(2)}, u32[]{:S(2)}) %collective-permute-start.36) | collective-permute-done | bytes 544 | tf_op jit(solution)/shard_map/ppermute | solution.py:41
  120.7 4.5 %right_product.3 = (f32[32,896]{1,0:T(8,128)S(1)}, f32[32,896]{1,0:T(8,128)S(1)}, f32[32,2048]{1,0:T(8,128)S(1)}) custom-call(s32[8]{0:T(128)S(1)} %own_places.1.z_ref.places_ref.core_ref, f32[32,2048]{1,0:T(8,128)S(1)} %get-tuple-element.48.left_ref, f32[1,128]{1,0:T(1,128)S(1)} %add_add_fusion.10.squares_ref, s32[2,32]{1,0:T(2,128)S(1)} %copy-done.1, ...), custom_call_target="tpu_custom_call" | custom-call | tf_op jit(solution)/shard_map/right_product/pallas_call | solution.py:259
  128.8 5.4 %collective-permute-done.40 = f32[32,896]{1,0:T(8,128)S(1)} collective-permute-done((f32[32,896]{1,0:T(8,128)S(1)}, f32[32,896]{1,0:T(8,128)S(1)}, u32[]{:S(2)}, u32[]{:S(2)}) %collective-permute-start.40) | collective-permute-done | bytes 114720 | tf_op jit(solution)/shard_map/ppermute | solution.py:41
  141.1 2.2 %collective-permute-done.44 = f32[1,128]{1,0:T(1,128)S(1)} collective-permute-done((f32[1,128]{1,0:T(1,128)S(1)}, f32[1,128]{1,0:T(1,128)S(1)}, u32[]{:S(2)}, u32[]{:S(2)}) %collective-permute-start.44) | collective-permute-done | bytes 544 | tf_op jit(solution)/shard_map/ppermute | solution.py:41
  147.9 2.2 %collective-permute-done.47 = f32[1,128]{1,0:T(1,128)S(1)} collective-permute-done((f32[1,128]{1,0:T(1,128)S(1)}, f32[1,128]{1,0:T(1,128)S(1)}, u32[]{:S(2)}, u32[]{:S(2)}) %collective-permute-start.47) | collective-permute-done | bytes 544 | tf_op jit(solution)/shard_map/ppermute | solution.py:41
  155.6 2.2 %collective-permute-done.50 = f32[32,128]{1,0:T(8,128)S(1)} collective-permute-done((f32[32,128]{1,0:T(8,128)S(1)}, f32[32,128]{1,0:T(8,128)S(1)}, u32[]{:S(2)}, u32[]{:S(2)}) %collective-permute-start.50) | collective-permute-done | bytes 16416 | tf_op jit(solution)/shard_map/ppermute | solution.py:41
  167.0 6.8 %deflate.1 = (f32[2048,1536]{1,0:T(8,128)}, f32[32,1536]{1,0:T(8,128)}, f32[1,32]{1,0:T(1,128)}) custom-call(f32[32,128]{1,0:T(8,128)S(1)} %add_add_fusion.6.last_ref, f32[32,1536]{1,0:T(8,128)S(1)} %get-tuple-element.55.shrunk_ref, bf16[192,2048]{1,0:T(8,128)(2,1)S(1)} %get-tuple-element.57.left_ref, f32[2048,1536]{1,0:T(8,128)S(1)} %get-tuple-element.39.cross_ref.refs_3_), custom_call_target="tpu_custom_call" | custom-call | tf_op jit(solution)/shard_map/deflate/pallas_call | solution.py:388
  (127 shorter events, 85.7 us)
Async XLA Ops:
  10.3 6.4 %collective-permute-start = (f32[32,512]{1,0:T(8,128)S(1)}, f32[32,512]{1,0:T(8,128)S(1)}, u32[]{:S(2)}, u32[]{:S(2)}) collective-permute-start(f32[32,512]{1,0:T(8,128)S(1)} %get-tuple-element.34), channel_id=1, source_target_pairs={{0,1},{1,2},{2,3},{3,0},{4,5},{5,6},{6,7},{7,4},{8,9},{9,10},{10,1... | collective-permute-start | bytes 196616 | tf_op jit(solution)/shard_map/ppermute | solution.py:41
  14.6 5.8 %collective-permute-start.2 = (f32[32,512]{1,0:T(8,128)S(1)}, f32[32,512]{1,0:T(8,128)S(1)}, u32[]{:S(2)}, u32[]{:S(2)}) collective-permute-start(f32[32,512]{1,0:T(8,128)S(1)} %get-tuple-element.36), channel_id=1, source_target_pairs={{0,2},{1,3},{2,0},{3,1},{4,6},{5,7},{6,4},{7,5},{8,10},{9,11},{10,... | collective-permute-start | bytes 196616 | tf_op jit(solution)/shard_map/ppermute | solution.py:41
  20.4 6.1 %collective-permute-start.5 = (f32[32,512]{1,0:T(8,128)S(1)}, f32[32,512]{1,0:T(8,128)S(1)}, u32[]{:S(2)}, u32[]{:S(2)}) collective-permute-start(f32[32,512]{1,0:T(8,128)S(1)} %add_add_fusion.5), channel_id=1, source_target_pairs={{0,8},{4,12},{8,0},{12,4},{1,9},{5,13},{9,1},{13,5},{2,10},{6,14},... | collective-permute-start | bytes 196616 | tf_op jit(solution)/shard_map/ppermute | solution.py:41
  24.7 5.5 %collective-permute-start.3 = (f32[32,512]{1,0:T(8,128)S(1)}, f32[32,512]{1,0:T(8,128)S(1)}, u32[]{:S(2)}, u32[]{:S(2)}) collective-permute-start(f32[32,512]{1,0:T(8,128)S(1)} %add_add_fusion.5), channel_id=1, source_target_pairs={{0,4},{4,8},{8,12},{12,0},{1,5},{5,9},{9,13},{13,1},{2,6},{6,10},{... | collective-permute-start | bytes 196616 | tf_op jit(solution)/shard_map/ppermute | solution.py:41
  30.2 5.8 %collective-permute-start.8 = (f32[32,512]{1,0:T(8,128)S(1)}, f32[32,512]{1,0:T(8,128)S(1)}, u32[]{:S(2)}, u32[]{:S(2)}) collective-permute-start(f32[32,512]{1,0:T(8,128)S(1)} %add_add_fusion.4.refs_0_), channel_id=1, source_target_pairs={{0,2},{1,3},{2,0},{3,1},{4,6},{5,7},{6,4},{7,5},{8,10},{9,11},{10,... | collective-permute-start | bytes 196616 | tf_op jit(solution)/shard_map/ppermute | solution.py:41
  32.9 5.5 %collective-permute-start.6 = (f32[32,512]{1,0:T(8,128)S(1)}, f32[32,512]{1,0:T(8,128)S(1)}, u32[]{:S(2)}, u32[]{:S(2)}) collective-permute-start(f32[32,512]{1,0:T(8,128)S(1)} %add_add_fusion.4.refs_0_), channel_id=1, source_target_pairs={{0,1},{1,2},{2,3},{3,0},{4,5},{5,6},{6,7},{7,4},{8,9},{9,10},{10,1... | collective-permute-start | bytes 196616 | tf_op jit(solution)/shard_map/ppermute | solution.py:41
  55.7 7.6 %collective-permute-start.16 = (f32[32,896]{1,0:T(8,128)S(1)}, f32[32,896]{1,0:T(8,128)S(1)}, u32[]{:S(2)}, u32[]{:S(2)}) collective-permute-start(f32[32,896]{1,0:T(8,128)S(1)} %add.148), channel_id=1, source_target_pairs={{0,64},{32,96},{64,0},{96,32},{16,80},{48,112},{80,16},{112,48},{1... | collective-permute-start | bytes 344072 | tf_op jit(solution)/shard_map/ppermute | solution.py:41
  56.1 7.2 %collective-permute-start.15 = (f32[32,896]{1,0:T(8,128)S(1)}, f32[32,896]{1,0:T(8,128)S(1)}, u32[]{:S(2)}, u32[]{:S(2)}) collective-permute-start(f32[32,896]{1,0:T(8,128)S(1)} %add.148), channel_id=1, source_target_pairs={{0,96},{32,0},{64,32},{96,64},{16,112},{48,16},{80,48},{112,80},{1... | collective-permute-start | bytes 344072 | tf_op jit(solution)/shard_map/ppermute | solution.py:41
  58.2 6.8 %collective-permute-start.14 = (f32[32,896]{1,0:T(8,128)S(1)}, f32[32,896]{1,0:T(8,128)S(1)}, u32[]{:S(2)}, u32[]{:S(2)}) collective-permute-start(f32[32,896]{1,0:T(8,128)S(1)} %add.148), channel_id=1, source_target_pairs={{0,32},{32,64},{64,96},{96,0},{16,48},{48,80},{80,112},{112,16},{1... | collective-permute-start | bytes 344072 | tf_op jit(solution)/shard_map/ppermute | solution.py:41
  67.3 5.1 %collective-permute-start.20 = (f32[1,128]{1,0:T(1,128)S(1)}, f32[1,128]{1,0:T(1,128)S(1)}, u32[]{:S(2)}, u32[]{:S(2)}) collective-permute-start(f32[1,128]{1,0:T(1,128)S(1)} %get-tuple-element.43), channel_id=1, source_target_pairs={{0,8},{4,12},{8,0},{12,4},{1,9},{5,13},{9,1},{13,5},{2,10},{6,14},... | collective-permute-start | bytes 1544 | tf_op jit(solution)/shard_map/ppermute | solution.py:41
  87.5 6.1 %collective-permute-start.24 = (f32[32,640]{1,0:T(8,128)S(1)}, f32[32,640]{1,0:T(8,128)S(1)}, u32[]{:S(2)}, u32[]{:S(2)}) collective-permute-start(f32[32,640]{1,0:T(8,128)S(1)} %get-tuple-element.45), channel_id=1, source_target_pairs={{0,1},{1,2},{2,3},{3,0},{4,5},{5,6},{6,7},{7,4},{8,9},{9,10},{10,1... | collective-permute-start | bytes 245768 | tf_op jit(solution)/shard_map/ppermute | solution.py:41
  87.8 6.1 %collective-permute-start.25 = (f32[32,640]{1,0:T(8,128)S(1)}, f32[32,640]{1,0:T(8,128)S(1)}, u32[]{:S(2)}, u32[]{:S(2)}) collective-permute-start(f32[32,640]{1,0:T(8,128)S(1)} %get-tuple-element.46), channel_id=1, source_target_pairs={{0,3},{1,0},{2,1},{3,2},{4,7},{5,4},{6,5},{7,6},{8,11},{9,8},{10,9... | collective-permute-start | bytes 245768 | tf_op jit(solution)/shard_map/ppermute | solution.py:41
  91.0 5.9 %collective-permute-start.26 = (f32[32,640]{1,0:T(8,128)S(1)}, f32[32,640]{1,0:T(8,128)S(1)}, u32[]{:S(2)}, u32[]{:S(2)}) collective-permute-start(f32[32,640]{1,0:T(8,128)S(1)} %get-tuple-element.47), channel_id=1, source_target_pairs={{0,2},{1,3},{2,0},{3,1},{4,6},{5,7},{6,4},{7,5},{8,10},{9,11},{10,... | collective-permute-start | bytes 245768 | tf_op jit(solution)/shard_map/ppermute | solution.py:41
  97.0 6.0 %collective-permute-start.29 = (f32[32,640]{1,0:T(8,128)S(1)}, f32[32,640]{1,0:T(8,128)S(1)}, u32[]{:S(2)}, u32[]{:S(2)}) collective-permute-start(f32[32,640]{1,0:T(8,128)S(1)} %add_add_fusion.3), channel_id=1, source_target_pairs={{0,8},{4,12},{8,0},{12,4},{1,9},{5,13},{9,1},{13,5},{2,10},{6,14},... | collective-permute-start | bytes 245768 | tf_op jit(solution)/shard_map/ppermute | solution.py:41
  97.1 5.9 %collective-permute-start.28 = (f32[32,640]{1,0:T(8,128)S(1)}, f32[32,640]{1,0:T(8,128)S(1)}, u32[]{:S(2)}, u32[]{:S(2)}) collective-permute-start(f32[32,640]{1,0:T(8,128)S(1)} %add_add_fusion.3), channel_id=1, source_target_pairs={{0,12},{4,0},{8,4},{12,8},{1,13},{5,1},{9,5},{13,9},{2,14},{6,2},{... | collective-permute-start | bytes 245768 | tf_op jit(solution)/shard_map/ppermute | solution.py:41
  98.6 5.7 %collective-permute-start.27 = (f32[32,640]{1,0:T(8,128)S(1)}, f32[32,640]{1,0:T(8,128)S(1)}, u32[]{:S(2)}, u32[]{:S(2)}) collective-permute-start(f32[32,640]{1,0:T(8,128)S(1)} %add_add_fusion.3), channel_id=1, source_target_pairs={{0,4},{4,8},{8,12},{12,0},{1,5},{5,9},{9,13},{13,1},{2,6},{6,10},{... | collective-permute-start | bytes 245768 | tf_op jit(solution)/shard_map/ppermute | solution.py:41
  104.3 5.8 %collective-permute-start.32 = (f32[32,512]{1,0:T(8,128)S(1)}, f32[32,512]{1,0:T(8,128)S(1)}, u32[]{:S(2)}, u32[]{:S(2)}) collective-permute-start(f32[32,512]{1,0:T(8,128)S(1)} %slice.27.refs_1_), channel_id=1, source_target_pairs={{0,2},{1,3},{2,0},{3,1},{4,6},{5,7},{6,4},{7,5},{8,10},{9,11},{10,... | collective-permute-start | bytes 196616 | tf_op jit(solution)/shard_map/ppermute | solution.py:41
  104.4 5.8 %collective-permute-start.31 = (f32[32,512]{1,0:T(8,128)S(1)}, f32[32,512]{1,0:T(8,128)S(1)}, u32[]{:S(2)}, u32[]{:S(2)}) collective-permute-start(f32[32,512]{1,0:T(8,128)S(1)} %slice.27.refs_1_), channel_id=1, source_target_pairs={{0,3},{1,0},{2,1},{3,2},{4,7},{5,4},{6,5},{7,6},{8,11},{9,8},{10,9... | collective-permute-start | bytes 196616 | tf_op jit(solution)/shard_map/ppermute | solution.py:41
  105.9 5.5 %collective-permute-start.30 = (f32[32,512]{1,0:T(8,128)S(1)}, f32[32,512]{1,0:T(8,128)S(1)}, u32[]{:S(2)}, u32[]{:S(2)}) collective-permute-start(f32[32,512]{1,0:T(8,128)S(1)} %slice.27.refs_1_), channel_id=1, source_target_pairs={{0,1},{1,2},{2,3},{3,0},{4,5},{5,6},{6,7},{7,4},{8,9},{9,10},{10,1... | collective-permute-start | bytes 196616 | tf_op jit(solution)/shard_map/ppermute | solution.py:41
  126.6 7.6 %collective-permute-start.40 = (f32[32,896]{1,0:T(8,128)S(1)}, f32[32,896]{1,0:T(8,128)S(1)}, u32[]{:S(2)}, u32[]{:S(2)}) collective-permute-start(f32[32,896]{1,0:T(8,128)S(1)} %add.168), channel_id=1, source_target_pairs={{0,64},{32,96},{64,0},{96,32},{16,80},{48,112},{80,16},{112,48},{1... | collective-permute-start | bytes 344072 | tf_op jit(solution)/shard_map/ppermute | solution.py:41
  126.7 7.5 %collective-permute-start.39 = (f32[32,896]{1,0:T(8,128)S(1)}, f32[32,896]{1,0:T(8,128)S(1)}, u32[]{:S(2)}, u32[]{:S(2)}) collective-permute-start(f32[32,896]{1,0:T(8,128)S(1)} %add.168), channel_id=1, source_target_pairs={{0,96},{32,0},{64,32},{96,64},{16,112},{48,16},{80,48},{112,80},{1... | collective-permute-start | bytes 344072 | tf_op jit(solution)/shard_map/ppermute | solution.py:41
  128.2 7.7 %collective-permute-start.38 = (f32[32,896]{1,0:T(8,128)S(1)}, f32[32,896]{1,0:T(8,128)S(1)}, u32[]{:S(2)}, u32[]{:S(2)}) collective-permute-start(f32[32,896]{1,0:T(8,128)S(1)} %add.168), channel_id=1, source_target_pairs={{0,32},{32,64},{64,96},{96,0},{16,48},{48,80},{80,112},{112,16},{1... | collective-permute-start | bytes 344072 | tf_op jit(solution)/shard_map/ppermute | solution.py:41
  152.5 5.3 %collective-permute-start.50 = (f32[32,128]{1,0:T(8,128)S(1)}, f32[32,128]{1,0:T(8,128)S(1)}, u32[]{:S(2)}, u32[]{:S(2)}) collective-permute-start(f32[32,128]{1,0:T(8,128)S(1)} %get-tuple-element.54), channel_id=1, source_target_pairs={{0,8},{4,12},{8,0},{12,4},{1,9},{5,13},{9,1},{13,5},{2,10},{6,14},... | collective-permute-start | bytes 49160 | tf_op jit(solution)/shard_map/ppermute | solution.py:41
  159.7 5.3 %collective-permute-start.53 = (f32[32,128]{1,0:T(8,128)S(1)}, f32[32,128]{1,0:T(8,128)S(1)}, u32[]{:S(2)}, u32[]{:S(2)}) collective-permute-start(f32[32,128]{1,0:T(8,128)S(1)} %add_add_fusion.7), channel_id=1, source_target_pairs={{0,2},{1,3},{2,0},{3,1},{4,6},{5,7},{6,4},{7,5},{8,10},{9,11},{10,... | collective-permute-start | bytes 49160 | tf_op jit(solution)/shard_map/ppermute | solution.py:41
  (32 other events, 167.8 us)

commit v3 on v2

--- a/solution.py
+++ b/solution.py
@@ -30,24 +30,24 @@
 CORE_PAIRS = [[x * 2, x * 2 + 1] for x in range(4)]
 Y_RINGS = [[y * 4 + z for y in range(4)] for z in range(4)]
 Z_RINGS = [[y * 4 + z for z in range(4)] for y in range(4)]
-STEPS = (1, 3, 2)
+MASKS = (1, 3, 2)
 
 PARAMS = pltpu.CompilerParams(vmem_limit_bytes=24 * 2**20)
 FIRST_PARAMS = pltpu.CompilerParams(vmem_limit_bytes=40 * 2**20)
 
 
-def shift(value, axis, rings, step):
-    pairs = [(r[i], r[(i + step) % len(r)]) for r in rings for i in range(len(r))]
+def swap(value, axis, rings, mask):
+    pairs = [(r[i], r[i ^ mask]) for r in rings for i in range(len(r))]
     return lax.ppermute(value, axis, pairs)
 
 
 def ring_sum(value, axis, rings):
-    got = [shift(value, axis, rings, step) for step in STEPS]
+    got = [swap(value, axis, rings, mask) for mask in MASKS]
     return (value + got[0]) + (got[1] + got[2])
 
 
 def pair_sum(value):
-    return value + shift(value, "vox", CORE_PAIRS, 1)
+    return value + swap(value, "vox", CORE_PAIRS, 1)
 
 
 def dot(a, b, dims):
@@ -146,8 +146,8 @@
         z = lax.rem(lax.axis_index("var"), 4)
         core = lax.rem(lax.axis_index("vox"), 2)
         out_ref[Z_AT] = z
-        for at, step in enumerate(STEPS):
-            out_ref[Z_AT + 1 + at] = lax.rem(z + 4 - step, 4)
+        for at, mask in enumerate(MASKS):
+            out_ref[Z_AT + 1 + at] = lax.bitwise_xor(z, jnp.int32(mask))
         out_ref[CORE_AT] = core
         out_ref[CORE_AT + 1] = 1 - core
         out_ref[6] = 0
@@ -162,77 +162,119 @@
     )()
 
 
-def left_product(right, squares, levels, cross, places):
-    first = squares is None
-    width = QUARTER if first else QUARTER + LANES
-
-    def kernel(z_ref, *refs):
-        if first:
-            right_ref, cross_ref, *outs, kept_ref, both_ref = refs
-        else:
-            right_ref, squares_ref, levels_ref, cross_ref, *outs, both_ref, gram_ref = refs
+def left_product_first(right, cross, places):
+    def kernel(places_ref, right_ref, cross_ref, *refs):
+        *outs, kept_ref, both_ref = refs
         step = pl.program_id(0)
 
         @pl.when(step == 0)
         def _():
-            values = right_ref[...]
-            if not first:
-                values = shrunk_of(values, squares_ref[...], levels_ref[...], 1, NG)
-                gram_ref[...] = padded(cross_gram(values, values))
+            both_ref[...] = jnp.concatenate(split2(right_ref[...]), axis=0)
+
+        block = cross_ref[...]
+        kept_ref[...] = block
+        product = left_terms_of(both_ref, block)
+        for at in range(4):
+
+            @pl.when(step == at)
+            def _():
+                outs[at][...] = product
+
+    quarter = pl.BlockSpec((QUARTER, COLS), lambda i, p: (p[Z_AT + i], 0))
+    return pl.pallas_call(
+        kernel,
+        grid_spec=pltpu.PrefetchScalarGridSpec(
+            num_scalar_prefetch=1,
+            grid=(4,),
+            in_specs=[pl.BlockSpec((K, COLS), lambda i, p: (0, 0)), quarter],
+            out_specs=[pl.BlockSpec((K, QUARTER), lambda i, p: (0, 0))] * 4 + [quarter],
+            scratch_shapes=[pltpu.VMEM((2 * K, COLS), BF16)],
+        ),
+        out_shape=[jax.ShapeDtypeStruct((K, QUARTER), F32)] * 4
+        + [jax.ShapeDtypeStruct((ROWS, COLS), F32)],
+        compiler_params=FIRST_PARAMS,
+        name="left_product_first",
+    )(places, right, cross)
+
+
+def left_terms_of(both_ref, block):
+    high, low = split2(block)
+    whole = dot(both_ref[...], high, NT)
+    return whole[:K] + (whole[K:] + dot(both_ref[:K], low, NT))
+
+
+def left_partners(right_sum, squares, levels, cross, places):
+    def kernel(places_ref, right_ref, squares_ref, levels_ref, cross_ref, *refs):
+        *outs, both_ref, gram_ref = refs
+        step = pl.program_id(0)
+
+        @pl.when(step == 0)
+        def _():
+            values = shrunk_of(right_ref[...], squares_ref[...], levels_ref[...], 1, NG)
             both_ref[...] = jnp.concatenate(split2(values), axis=0)
-
-        block = cross_ref[...]
-        if first:
-            kept_ref[...] = block
-        high, low = split2(block)
-        whole = dot(both_ref[...], high, NT)
-        product = whole[:K] + (whole[K:] + dot(both_ref[:K], low, NT))
-        for at in range(4):
+            gram_ref[...] = padded(cross_gram(values, values))
+
+        product = left_terms_of(both_ref, cross_ref[...])
+        for at in range(3):
 
             @pl.when(step == at)
             def _():
                 outs[at][:, :QUARTER] = product
-                if not first:
-                    outs[at][:, QUARTER:] = gram_ref[...]
-
-    small = [] if first else [
-        pl.BlockSpec((1, LANES), lambda i, z: (0, 0)),
-        pl.BlockSpec((2, K), lambda i, z: (0, 0)),
-    ]
-    scratch = [pltpu.VMEM((2 * K, COLS), BF16)]
-    if not first:
-        scratch.append(pltpu.VMEM((K, LANES), F32))
-    args = (right,) if first else (right, squares, levels)
+                outs[at][:, QUARTER:] = gram_ref[...]
+
+    whole = lambda shape: pl.BlockSpec(shape, lambda i, p: (0, 0))
+    shapes = [((K, QUARTER + LANES), F32)] * 3 + [((2 * K, COLS), BF16), ((K, LANES), F32)]
     return pl.pallas_call(
         kernel,
         grid_spec=pltpu.PrefetchScalarGridSpec(
             num_scalar_prefetch=1,
-            grid=(4,),
-            in_specs=[pl.BlockSpec((K, COLS), lambda i, z: (0, 0))]
-            + small
-            + [pl.BlockSpec((QUARTER, COLS), lambda i, z: (lax.rem(z[Z_AT] + i, 4), 0))],
-            out_specs=[pl.BlockSpec((K, width), lambda i, z: (0, 0)) for _ in range(4)]
-            + [pl.BlockSpec((QUARTER, COLS), lambda i, z: (lax.rem(z[Z_AT] + i, 4), 0))] * first,
-            scratch_shapes=scratch,
+            grid=(3,),
+            in_specs=[whole((K, COLS)), whole((1, LANES)), whole((2, K))]
+            + [pl.BlockSpec((QUARTER, COLS), lambda i, p: (p[Z_AT + 1 + i], 0))],
+            out_specs=[whole(shape) for shape, _ in shapes],
         ),
-        out_shape=[jax.ShapeDtypeStruct((K, width), F32) for _ in range(4)]
-        + [jax.ShapeDtypeStruct((ROWS, COLS), F32)] * first,
-        compiler_params=FIRST_PARAMS if first else PARAMS,
-        name="left_product_first" if first else "left_product",
-    )(places, *args, cross)
-
-
-def right_product(left, squares, levels, cross, places):
-    def kernel(core_ref, left_ref, squares_ref, levels_ref, cross_ref, own_ref, other_ref, shrunk_ref, both_ref, sum_ref, gram_ref):
+        out_shape=[jax.ShapeDtypeStruct(*shape) for shape in shapes],
+        compiler_params=PARAMS,
+        name="left_partners",
+    )(places, right_sum, squares, levels, cross)
+
+
+def left_own(both, gram, cross, places):
+    def kernel(places_ref, both_ref, gram_ref, cross_ref, out_ref):
+        out_ref[:, :QUARTER] = left_terms_of(both_ref, cross_ref[...])
+        out_ref[:, QUARTER:] = gram_ref[...]
+
+    whole = lambda shape: pl.BlockSpec(shape, lambda i, p: (0, 0))
+    return pl.pallas_call(
+        kernel,
+        grid_spec=pltpu.PrefetchScalarGridSpec(
+            num_scalar_prefetch=1,
+            grid=(1,),
+            in_specs=[whole((2 * K, COLS)), whole((K, LANES))]
+            + [pl.BlockSpec((QUARTER, COLS), lambda i, p: (p[Z_AT], 0))],
+            out_specs=whole((K, QUARTER + LANES)),
+        ),
+        out_shape=jax.ShapeDtypeStruct((K, QUARTER + LANES), F32),
+        compiler_params=PARAMS,
+        cost_estimate=pl.CostEstimate(flops=600_000_000, bytes_accessed=4_000_000, transcendentals=0),
+        name="left_own",
+    )(places, both, gram, cross)
+
+
+def right_half(head, given, cross, places, at):
+    def kernel(places_ref, *refs):
         step = pl.program_id(0)
-
-        @pl.when(step == 0)
-        def _():
-            values = shrunk_of(left_ref[...], squares_ref[...], levels_ref[...], 0, NV)
-            shrunk_ref[...] = values
-            gram_ref[...] = padded(cross_gram(values, values))
-            both_ref[...] = jnp.concatenate(split2(values), axis=0)
-
+        if head:
+            left_ref, squares_ref, levels_ref, cross_ref, out_ref, both_ref, gram_ref, shrunk_ref = refs
+
+            @pl.when(step == 0)
+            def _():
+                values = shrunk_of(left_ref[...], squares_ref[...], levels_ref[...], 0, NV)
+                shrunk_ref[...] = values
+                both_ref[...] = jnp.concatenate(split2(values), axis=0)
+                gram_ref[...] = padded(cross_gram(values, values))
+        else:
+            both_ref, gram_ref, cross_ref, out_ref = refs
         high, low = split2(cross_ref[...])
         both = both_ref[:, pl.ds(pl.multiple_of(step * BLOCK, BLOCK), BLOCK)]
         whole = dot(both, high, NN)
@@ -240,48 +282,35 @@
 
         @pl.when(step == 0)
         def _():
-            sum_ref[...] = product
+            out_ref[:, :HALF] = product
+            out_ref[:, HALF:] = gram_ref[...]
 
         @pl.when(step > 0)
         def _():
-            sum_ref[...] += product
-
-        @pl.when(step == ROWS // BLOCK - 1)
-        def _():
-            own = pl.multiple_of(core_ref[CORE_AT] * HALF, HALF)
-            other = pl.multiple_of((1 - core_ref[CORE_AT]) * HALF, HALF)
-            own_ref[:, :HALF] = sum_ref[:, pl.ds(own, HALF)]
-            other_ref[:, :HALF] = sum_ref[:, pl.ds(other, HALF)]
-            own_ref[:, HALF:] = gram_ref[...]
-            other_ref[:, HALF:] = gram_ref[...]
-
-    whole = lambda shape: pl.BlockSpec(shape, lambda i, c: (0, 0))
+            out_ref[:, :HALF] += product
+
+    whole = lambda shape: pl.BlockSpec(shape, lambda i, p: (0, 0))
+    out_shape = [jax.ShapeDtypeStruct((K, HALF + LANES), F32)]
+    if head:
+        out_shape += [
+            jax.ShapeDtypeStruct((2 * K, ROWS), BF16),
+            jax.ShapeDtypeStruct((K, LANES), F32),
+            jax.ShapeDtypeStruct((K, ROWS), F32),
+        ]
     return pl.pallas_call(
         kernel,
         grid_spec=pltpu.PrefetchScalarGridSpec(
             num_scalar_prefetch=1,
             grid=(ROWS // BLOCK,),
-            in_specs=[
-                whole((K, ROWS)),
-                whole((1, LANES)),
-                whole((2, K)),
-                pl.BlockSpec((BLOCK, COLS), lambda i, c: (i, 0)),
-            ],
-            out_specs=[whole((K, HALF + LANES)), whole((K, HALF + LANES)), whole((K, ROWS))],
-            scratch_shapes=[
-                pltpu.VMEM((2 * K, ROWS), BF16),
-                pltpu.VMEM((K, COLS), F32),
-                pltpu.VMEM((K, LANES), F32),
-            ],
+            in_specs=[whole(g.shape) for g in given]
+            + [pl.BlockSpec((BLOCK, HALF), lambda i, p: (i, p[CORE_AT + at]))],
+            out_specs=[whole(o.shape) for o in out_shape],
         ),
-        out_shape=[
-            jax.ShapeDtypeStruct((K, HALF + LANES), F32),
-            jax.ShapeDtypeStruct((K, HALF + LANES), F32),
-            jax.ShapeDtypeStruct((K, ROWS), F32),
-        ],
-        compiler_params=PARAMS,
-        name="right_product",
-    )(places, left, squares, levels, cross)
+        out_shape=out_shape,
+        compiler_params=PARAMS,
+        cost_estimate=pl.CostEstimate(flops=1_200_000_000, bytes_accessed=8_000_000, transcendentals=0),
+        name="right_half_head" if head else "right_half",
+    )(places, *given, cross)
 
 
 def factor(gram, count):
@@ -412,26 +441,29 @@
 
 def per_device(cross, start, levels):
     places = own_places()
-    right_sum, squares = start, None
     for sweep in range(ITERS):
-        parts = left_product(right_sum, squares, levels, cross, places)
         if sweep == 0:
-            cross = parts[4]
-        total = parts[0]
-        for step in STEPS:
-            total = total + shift(parts[step], "var", Z_RINGS, step)
+            *parts, cross = left_product_first(start, cross, places)
+            got = [swap(parts[at + 1], "var", Z_RINGS, mask) for at, mask in enumerate(MASKS)]
+            total = parts[0]
+        else:
+            *parts, both, gram = left_partners(right_sum, squares, levels, cross, places)
+            got = [swap(part, "var", Z_RINGS, mask) for part, mask in zip(parts, MASKS)]
+            total = left_own(both, gram, cross, places)
+        total = (total + got[0]) + (got[1] + got[2])
         total = ring_sum(total, "var", Y_RINGS)
         block = total[:, :QUARTER]
-        blocks = [block] + [shift(block, "var", Z_RINGS, step) for step in STEPS]
+        blocks = [block] + [swap(block, "var", Z_RINGS, mask) for mask in MASKS]
         inverse = factor(total[:, QUARTER:], NG) if sweep else None
         left_sum, squares = assemble(inverse, blocks, places, Z_AT, "assemble_left")
         squares = ring_sum(pair_sum(squares), "vox", X_RINGS)
 
-        own, other, left_shrunk = right_product(left_sum, squares, levels, cross, places)
-        total = own + shift(other, "vox", CORE_PAIRS, 1)
-        total = ring_sum(total, "vox", X_RINGS)
+        part, both, gram, left_shrunk = right_half(True, (left_sum, squares, levels), cross, places, 1)
+        got = swap(part, "vox", CORE_PAIRS, 1)
+        (total,) = right_half(False, (both, gram), cross, places, 0)
+        total = ring_sum(total + got, "vox", X_RINGS)
         block = total[:, :HALF]
-        blocks = [block, shift(block, "vox", CORE_PAIRS, 1)]
+        blocks = [block, swap(block, "vox", CORE_PAIRS, 1)]
         inverse = factor(total[:, HALF:], NV)
         right_sum, squares = assemble(inverse, blocks, places, CORE_AT, "assemble_right")
         squares = ring_sum(ring_sum(squares, "var", Y_RINGS), "var", Z_RINGS)

time: 174 us -> 167 us (0.960)
  waiting for transfers between devices: 80.2 us -> 61.9 us
  starting transfers between devices: 53.1 us -> 61.7 us
  Pallas kernels: 38.5 us -> 41.4 us
    ppermute x54, waiting for transfers between devices: 80.2 us -> 61.9 us  [swap(): return lax.ppermute(value, axis, pairs)]
    ppermute x54, starting transfers between devices: 53.1 us -> 61.7 us  [swap(): return lax.ppermute(value, axis, pairs)]
    pallas_call x4 -> x7, Pallas kernels: 23.4 us -> 26.3 us  [the longest x4 12.2 us: right_half(): pl.pallas_call(kernel, grid_spec=pltpu.PrefetchScalarGridSpec(num_scalar_...]
  transfers between devices with their start and end apart: 54 -> 54, of which waited for: 41 -> 38; matrix products, arithmetic and copies ran while one was open for 0% -> 0% of each run, Pallas kernels for 2% -> 6%
where the time goes in v3:
time: 167 us
  waiting for transfers between devices  61.9 us (37%)
  starting transfers between devices  61.7 us (37%)
  Pallas kernels  41.4 us (25%)
    ppermute x54, waiting for transfers between devices, swap(): return lax.ppermute(value, axis, pairs)  61.9 us
    ppermute x54, starting transfers between devices, swap(): return lax.ppermute(value, axis, pairs)  61.7 us
    pallas_call x4, Pallas kernels, right_half(): pl.pallas_call(kernel, grid_spec=pltpu.PrefetchScalarGridSpec(num_scalar_...  12.2 us
    pallas_call x1, Pallas kernels, left_product_first(): pl.pallas_call(kernel, grid_spec=pltpu.PrefetchScalarGridSpec(num_scalar_...  8.13 us
    pallas_call x1, Pallas kernels, deflate(): pl.pallas_call(kernel, grid=(ROWS // BLOCK,), in_specs=[whole((K, LANES))...  6.84 us
    pallas_call x1, Pallas kernels, left_partners(): pl.pallas_call(kernel, grid_spec=pltpu.PrefetchScalarGridSpec(num_scalar_...  4.41 us
    pallas_call x4, Pallas kernels, assemble(): pl.pallas_call(kernel, in_specs=[pl.BlockSpec(memory_space=pltpu.SMEM)] +...  3.44 us
  transfers between devices with their start and end apart: 54, of which 38 were waited for; matrix products, arithmetic and copies ran while one was open for 0% of the time, Pallas kernels for 6%

profile of v3, /device:TPU:0, one launch (start us, length us, event | category | flops | bytes accessed | tf_op | source)
XLA Modules:
  0.0 167.1 jit_solution(16194518545347235721)
XLA Ops:
  2.2 8.1 %left_product_first.1 = (f32[32,512]{1,0:T(8,128)S(1)}, f32[32,512]{1,0:T(8,128)S(1)}, f32[32,512]{1,0:T(8,128)S(1)}, f32[32,512]{1,0:T(8,128)S(1)}, f32[2048,1536]{1,0:T(8,128)S(1)}) custom-call(s32[8]{0:T(128)S(1)} %own_places.1.places_ref, f32[32,1536]{1,0:T(8,128)S(1)} %copy-done, f32[2048,1536]{1,0:T(8,128)} %cross_ref.1), custom_call_target="tpu_custom_call" | custom-call | tf_op jit(solution)/shard_map/left_product_first/pallas_call | solution.py:184
  12.4 2.5 %collective-permute-start.1 = (f32[32,512]{1,0:T(8,128)S(1)}, f32[32,512]{1,0:T(8,128)S(1)}, u32[]{:S(2)}, u32[]{:S(2)}) collective-permute-start(f32[32,512]{1,0:T(8,128)S(1)} %get-tuple-element.38), channel_id=1, source_target_pairs={{0,3},{1,2},{2,1},{3,0},{4,7},{5,6},{6,5},{7,4},{8,11},{9,10},{10,... | collective-permute-start | bytes 196616 | tf_op jit(solution)/shard_map/ppermute | solution.py:41
  17.9 2.8 %collective-permute-done.2 = f32[32,512]{1,0:T(8,128)S(1)} collective-permute-done((f32[32,512]{1,0:T(8,128)S(1)}, f32[32,512]{1,0:T(8,128)S(1)}, u32[]{:S(2)}, u32[]{:S(2)}) %collective-permute-start.2) | collective-permute-done | bytes 65568 | tf_op jit(solution)/shard_map/ppermute | solution.py:41
  20.7 3.3 %collective-permute-start.5 = (f32[32,512]{1,0:T(8,128)S(1)}, f32[32,512]{1,0:T(8,128)S(1)}, u32[]{:S(2)}, u32[]{:S(2)}) collective-permute-start(f32[32,512]{1,0:T(8,128)S(1)} %add_add_fusion.5), channel_id=1, source_target_pairs={{0,8},{4,12},{8,0},{12,4},{1,9},{5,13},{9,1},{13,5},{2,10},{6,14},... | collective-permute-start | bytes 196616 | tf_op jit(solution)/shard_map/ppermute | solution.py:41
  26.7 2.8 %collective-permute-done.4 = f32[32,512]{1,0:T(8,128)S(1)} collective-permute-done((f32[32,512]{1,0:T(8,128)S(1)}, f32[32,512]{1,0:T(8,128)S(1)}, u32[]{:S(2)}, u32[]{:S(2)}) %collective-permute-start.4) | collective-permute-done | bytes 65568 | tf_op jit(solution)/shard_map/ppermute | solution.py:41
  30.6 2.6 %collective-permute-start.7 = (f32[32,512]{1,0:T(8,128)S(1)}, f32[32,512]{1,0:T(8,128)S(1)}, u32[]{:S(2)}, u32[]{:S(2)}) collective-permute-start(f32[32,512]{1,0:T(8,128)S(1)} %add_add_fusion.4.refs_0_), channel_id=1, source_target_pairs={{0,3},{1,2},{2,1},{3,0},{4,7},{5,6},{6,5},{7,4},{8,11},{9,10},{10,... | collective-permute-start | bytes 196616 | tf_op jit(solution)/shard_map/ppermute | solution.py:41
  39.4 3.0 %collective-permute-start.12 = (f32[1,128]{1,0:T(1,128)S(1)}, f32[1,128]{1,0:T(1,128)S(1)}, u32[]{:S(2)}, u32[]{:S(2)}) collective-permute-start(f32[1,128]{1,0:T(1,128)S(1)} %add.144), channel_id=1, source_target_pairs={{0,64},{32,96},{64,0},{96,32},{16,80},{48,112},{80,16},{112,48},{1... | collective-permute-start | bytes 1544 | tf_op jit(solution)/shard_map/ppermute | solution.py:41
  44.4 2.7 %collective-permute-done.11 = f32[1,128]{1,0:T(1,128)S(1)} collective-permute-done((f32[1,128]{1,0:T(1,128)S(1)}, f32[1,128]{1,0:T(1,128)S(1)}, u32[]{:S(2)}, u32[]{:S(2)}) %collective-permute-start.11) | collective-permute-done | bytes 544 | tf_op jit(solution)/shard_map/ppermute | solution.py:41
  47.2 3.8 %right_half_head.2 = (f32[32,896]{1,0:T(8,128)S(1)}, bf16[64,2048]{1,0:T(8,128)(2,1)S(1)}, f32[32,128]{1,0:T(8,128)S(1)}, f32[32,2048]{1,0:T(8,128)}) custom-call(s32[8]{0:T(128)S(1)} %own_places.1.places_ref, f32[32,2048]{1,0:T(8,128)S(1)} %get-tuple-element.40.refs_0_, f32[1,128]{1,0:T(1,128)S(1)} %add_add_fusion.13.refs_1_, s32[2,32]{1,0:T(2,128)S(1)} %copy-done.1, ...), custom_call_target="tpu_custom_call" | custom-call | flops 1200000000 | bytes 8000000 | tf_op jit(solution)/shard_map/right_half_head/pallas_call | solution.py:300
  51.0 2.6 %right_half.2 = f32[32,896]{1,0:T(8,128)S(1)} custom-call(s32[8]{0:T(128)S(1)} %own_places.1.places_ref, bf16[64,2048]{1,0:T(8,128)(2,1)S(1)} %get-tuple-element.43.refs_0_, f32[32,128]{1,0:T(8,128)S(1)} %get-tuple-element.44.refs_1_, f32[2048,1536]{1,0:T(8,128)S(1)} %get-tuple-element.42.refs_3_.refs_2_.cross_ref), custom_call_target="tpu_custom_call" | custom-call | flops 1200000000 | bytes 8000000 | tf_op jit(solution)/shard_map/right_half/pallas_call | solution.py:300
  57.2 4.0 %collective-permute-done.16 = f32[32,896]{1,0:T(8,128)S(1)} collective-permute-done((f32[32,896]{1,0:T(8,128)S(1)}, f32[32,896]{1,0:T(8,128)S(1)}, u32[]{:S(2)}, u32[]{:S(2)}) %collective-permute-start.16) | collective-permute-done | bytes 114720 | tf_op jit(solution)/shard_map/ppermute | solution.py:41
  72.2 2.5 %collective-permute-start.22 = (f32[1,128]{1,0:T(1,128)S(1)}, f32[1,128]{1,0:T(1,128)S(1)}, u32[]{:S(2)}, u32[]{:S(2)}) collective-permute-start(f32[1,128]{1,0:T(1,128)S(1)} %add_add_fusion.12), channel_id=1, source_target_pairs={{0,3},{1,2},{2,1},{3,0},{4,7},{5,6},{6,5},{7,4},{8,11},{9,10},{10,... | collective-permute-start | bytes 1544 | tf_op jit(solution)/shard_map/ppermute | solution.py:41
  78.3 4.4 %left_partners.1 = (f32[32,640]{1,0:T(8,128)S(1)}, f32[32,640]{1,0:T(8,128)S(1)}, f32[32,640]{1,0:T(8,128)S(1)}, bf16[64,1536]{1,0:T(8,128)(2,1)S(1)}, f32[32,128]{1,0:T(8,128)S(1)}) custom-call(s32[8]{0:T(128)S(1)} %own_places.1.places_ref, f32[32,1536]{1,0:T(8,128)S(1)} %get-tuple-element.46.right_ref, f32[1,128]{1,0:T(1,128)S(1)} %add_add_fusion.11.squares_ref, ...), custom_call_target="tpu_custom_call" | custom-call | tf_op jit(solution)/shard_map/left_partners/pallas_call | solution.py:227
  90.8 2.2 %collective-permute-start.29 = (f32[32,640]{1,0:T(8,128)S(1)}, f32[32,640]{1,0:T(8,128)S(1)}, u32[]{:S(2)}, u32[]{:S(2)}) collective-permute-start(f32[32,640]{1,0:T(8,128)S(1)} %add_add_fusion.3), channel_id=1, source_target_pairs={{0,8},{4,12},{8,0},{12,4},{1,9},{5,13},{9,1},{13,5},{2,10},{6,14},... | collective-permute-start | bytes 245768 | tf_op jit(solution)/shard_map/ppermute | solution.py:41
  94.4 2.5 %collective-permute-done.29 = f32[32,640]{1,0:T(8,128)S(1)} collective-permute-done((f32[32,640]{1,0:T(8,128)S(1)}, f32[32,640]{1,0:T(8,128)S(1)}, u32[]{:S(2)}, u32[]{:S(2)}) %collective-permute-start.29) | collective-permute-done | bytes 81952 | tf_op jit(solution)/shard_map/ppermute | solution.py:41
  98.7 2.1 %collective-permute-start.32 = (f32[32,512]{1,0:T(8,128)S(1)}, f32[32,512]{1,0:T(8,128)S(1)}, u32[]{:S(2)}, u32[]{:S(2)}) collective-permute-start(f32[32,512]{1,0:T(8,128)S(1)} %slice.27.refs_1_), channel_id=1, source_target_pairs={{0,2},{1,3},{2,0},{3,1},{4,6},{5,7},{6,4},{7,5},{8,10},{9,11},{10,... | collective-permute-start | bytes 196616 | tf_op jit(solution)/shard_map/ppermute | solution.py:41
  114.7 3.1 %right_half_head.3 = (f32[32,896]{1,0:T(8,128)S(1)}, bf16[64,2048]{1,0:T(8,128)(2,1)S(1)}, f32[32,128]{1,0:T(8,128)S(1)}, f32[32,2048]{1,0:T(8,128)S(1)}) custom-call(s32[8]{0:T(128)S(1)} %own_places.1.places_ref, f32[32,2048]{1,0:T(8,128)S(1)} %get-tuple-element.53.refs_0_, f32[1,128]{1,0:T(1,128)S(1)} %add_add_fusion.10.refs_1_, s32[2,32]{1,0:T(2,128)S(1)} %copy-done.1, ...), custom_call_target="tpu_custom_call" | custom-call | flops 1200000000 | bytes 8000000 | tf_op jit(solution)/shard_map/right_half_head/pallas_call | solution.py:300
  117.9 2.6 %right_half.3 = f32[32,896]{1,0:T(8,128)S(1)} custom-call(s32[8]{0:T(128)S(1)} %own_places.1.places_ref, bf16[64,2048]{1,0:T(8,128)(2,1)S(1)} %get-tuple-element.55.refs_0_, f32[32,128]{1,0:T(8,128)S(1)} %get-tuple-element.56.refs_1_, f32[2048,1536]{1,0:T(8,128)S(1)} %get-tuple-element.42.refs_3_.refs_2_.cross_ref), custom_call_target="tpu_custom_call" | custom-call | flops 1200000000 | bytes 8000000 | tf_op jit(solution)/shard_map/right_half/pallas_call | solution.py:300
  120.6 2.3 %collective-permute-start.40 = (f32[32,896]{1,0:T(8,128)S(1)}, f32[32,896]{1,0:T(8,128)S(1)}, u32[]{:S(2)}, u32[]{:S(2)}) collective-permute-start(f32[32,896]{1,0:T(8,128)S(1)} %add.168), channel_id=1, source_target_pairs={{0,64},{32,96},{64,0},{96,32},{16,80},{48,112},{80,16},{112,48},{1... | collective-permute-start | bytes 344072 | tf_op jit(solution)/shard_map/ppermute | solution.py:41
  124.2 3.6 %collective-permute-done.40 = f32[32,896]{1,0:T(8,128)S(1)} collective-permute-done((f32[32,896]{1,0:T(8,128)S(1)}, f32[32,896]{1,0:T(8,128)S(1)}, u32[]{:S(2)}, u32[]{:S(2)}) %collective-permute-start.40) | collective-permute-done | bytes 114720 | tf_op jit(solution)/shard_map/ppermute | solution.py:41
  127.8 2.4 %collective-permute-done.39 = f32[32,896]{1,0:T(8,128)S(1)} collective-permute-done((f32[32,896]{1,0:T(8,128)S(1)}, f32[32,896]{1,0:T(8,128)S(1)}, u32[]{:S(2)}, u32[]{:S(2)}) %collective-permute-start.39) | collective-permute-done | bytes 114720 | tf_op jit(solution)/shard_map/ppermute | solution.py:41
  146.0 2.2 %collective-permute-start.50 = (f32[32,128]{1,0:T(8,128)S(1)}, f32[32,128]{1,0:T(8,128)S(1)}, u32[]{:S(2)}, u32[]{:S(2)}) collective-permute-start(f32[32,128]{1,0:T(8,128)S(1)} %get-tuple-element.60), channel_id=1, source_target_pairs={{0,8},{4,12},{8,0},{12,4},{1,9},{5,13},{9,1},{13,5},{2,10},{6,14},... | collective-permute-start | bytes 49160 | tf_op jit(solution)/shard_map/ppermute | solution.py:41
  153.2 2.1 %collective-permute-start.53 = (f32[32,128]{1,0:T(8,128)S(1)}, f32[32,128]{1,0:T(8,128)S(1)}, u32[]{:S(2)}, u32[]{:S(2)}) collective-permute-start(f32[32,128]{1,0:T(8,128)S(1)} %add_add_fusion.7), channel_id=1, source_target_pairs={{0,2},{1,3},{2,0},{3,1},{4,6},{5,7},{6,4},{7,5},{8,10},{9,11},{10,... | collective-permute-start | bytes 49160 | tf_op jit(solution)/shard_map/ppermute | solution.py:41
  160.3 6.8 %deflate.1 = (f32[2048,1536]{1,0:T(8,128)}, f32[32,1536]{1,0:T(8,128)}, f32[1,32]{1,0:T(1,128)}) custom-call(f32[32,128]{1,0:T(8,128)S(1)} %add_add_fusion.6.last_ref, f32[32,1536]{1,0:T(8,128)S(1)} %get-tuple-element.61.shrunk_ref, bf16[192,2048]{1,0:T(8,128)(2,1)S(1)} %get-tuple-element.63.left_ref, ...), custom_call_target="tpu_custom_call" | custom-call | tf_op jit(solution)/shard_map/deflate/pallas_call | solution.py:417
  (130 shorter events, 88.9 us)
Async XLA Ops:
  10.3 5.7 %collective-permute-start = (f32[32,512]{1,0:T(8,128)S(1)}, f32[32,512]{1,0:T(8,128)S(1)}, u32[]{:S(2)}, u32[]{:S(2)}) collective-permute-start(f32[32,512]{1,0:T(8,128)S(1)} %get-tuple-element.37), channel_id=1, source_target_pairs={{0,1},{1,0},{2,3},{3,2},{4,5},{5,4},{6,7},{7,6},{8,9},{9,8},{10,11... | collective-permute-start | bytes 196616 | tf_op jit(solution)/shard_map/ppermute | solution.py:41
  12.4 5.5 %collective-permute-start.1 = (f32[32,512]{1,0:T(8,128)S(1)}, f32[32,512]{1,0:T(8,128)S(1)}, u32[]{:S(2)}, u32[]{:S(2)}) collective-permute-start(f32[32,512]{1,0:T(8,128)S(1)} %get-tuple-element.38), channel_id=1, source_target_pairs={{0,3},{1,2},{2,1},{3,0},{4,7},{5,6},{6,5},{7,4},{8,11},{9,10},{10,... | collective-permute-start | bytes 196616 | tf_op jit(solution)/shard_map/ppermute | solution.py:41
  14.9 5.8 %collective-permute-start.2 = (f32[32,512]{1,0:T(8,128)S(1)}, f32[32,512]{1,0:T(8,128)S(1)}, u32[]{:S(2)}, u32[]{:S(2)}) collective-permute-start(f32[32,512]{1,0:T(8,128)S(1)} %get-tuple-element.39), channel_id=1, source_target_pairs={{0,2},{1,3},{2,0},{3,1},{4,6},{5,7},{6,4},{7,5},{8,10},{9,11},{10,... | collective-permute-start | bytes 196616 | tf_op jit(solution)/shard_map/ppermute | solution.py:41
  20.7 6.0 %collective-permute-start.5 = (f32[32,512]{1,0:T(8,128)S(1)}, f32[32,512]{1,0:T(8,128)S(1)}, u32[]{:S(2)}, u32[]{:S(2)}) collective-permute-start(f32[32,512]{1,0:T(8,128)S(1)} %add_add_fusion.5), channel_id=1, source_target_pairs={{0,8},{4,12},{8,0},{12,4},{1,9},{5,13},{9,1},{13,5},{2,10},{6,14},... | collective-permute-start | bytes 196616 | tf_op jit(solution)/shard_map/ppermute | solution.py:41
  24.0 5.5 %collective-permute-start.4 = (f32[32,512]{1,0:T(8,128)S(1)}, f32[32,512]{1,0:T(8,128)S(1)}, u32[]{:S(2)}, u32[]{:S(2)}) collective-permute-start(f32[32,512]{1,0:T(8,128)S(1)} %add_add_fusion.5), channel_id=1, source_target_pairs={{0,12},{4,8},{8,4},{12,0},{1,13},{5,9},{9,5},{13,1},{2,14},{6,10},... | collective-permute-start | bytes 196616 | tf_op jit(solution)/shard_map/ppermute | solution.py:41
  29.5 5.8 %collective-permute-start.8 = (f32[32,512]{1,0:T(8,128)S(1)}, f32[32,512]{1,0:T(8,128)S(1)}, u32[]{:S(2)}, u32[]{:S(2)}) collective-permute-start(f32[32,512]{1,0:T(8,128)S(1)} %add_add_fusion.4.refs_0_), channel_id=1, source_target_pairs={{0,2},{1,3},{2,0},{3,1},{4,6},{5,7},{6,4},{7,5},{8,10},{9,11},{10,... | collective-permute-start | bytes 196616 | tf_op jit(solution)/shard_map/ppermute | solution.py:41
  30.6 5.5 %collective-permute-start.7 = (f32[32,512]{1,0:T(8,128)S(1)}, f32[32,512]{1,0:T(8,128)S(1)}, u32[]{:S(2)}, u32[]{:S(2)}) collective-permute-start(f32[32,512]{1,0:T(8,128)S(1)} %add_add_fusion.4.refs_0_), channel_id=1, source_target_pairs={{0,3},{1,2},{2,1},{3,0},{4,7},{5,6},{6,5},{7,4},{8,11},{9,10},{10,... | collective-permute-start | bytes 196616 | tf_op jit(solution)/shard_map/ppermute | solution.py:41
  53.6 7.5 %collective-permute-start.16 = (f32[32,896]{1,0:T(8,128)S(1)}, f32[32,896]{1,0:T(8,128)S(1)}, u32[]{:S(2)}, u32[]{:S(2)}) collective-permute-start(f32[32,896]{1,0:T(8,128)S(1)} %add.148), channel_id=1, source_target_pairs={{0,64},{32,96},{64,0},{96,32},{16,80},{48,112},{80,16},{112,48},{1... | collective-permute-start | bytes 344072 | tf_op jit(solution)/shard_map/ppermute | solution.py:41
  55.2 8.1 %collective-permute-start.15 = (f32[32,896]{1,0:T(8,128)S(1)}, f32[32,896]{1,0:T(8,128)S(1)}, u32[]{:S(2)}, u32[]{:S(2)}) collective-permute-start(f32[32,896]{1,0:T(8,128)S(1)} %add.148), channel_id=1, source_target_pairs={{0,96},{32,64},{64,32},{96,0},{16,112},{48,80},{80,48},{112,16},{1... | collective-permute-start | bytes 344072 | tf_op jit(solution)/shard_map/ppermute | solution.py:41
  56.3 6.9 %collective-permute-start.14 = (f32[32,896]{1,0:T(8,128)S(1)}, f32[32,896]{1,0:T(8,128)S(1)}, u32[]{:S(2)}, u32[]{:S(2)}) collective-permute-start(f32[32,896]{1,0:T(8,128)S(1)} %add.148), channel_id=1, source_target_pairs={{0,32},{32,0},{64,96},{96,64},{16,48},{48,16},{80,112},{112,80},{1... | collective-permute-start | bytes 344072 | tf_op jit(solution)/shard_map/ppermute | solution.py:41
  65.6 5.1 %collective-permute-start.20 = (f32[1,128]{1,0:T(1,128)S(1)}, f32[1,128]{1,0:T(1,128)S(1)}, u32[]{:S(2)}, u32[]{:S(2)}) collective-permute-start(f32[1,128]{1,0:T(1,128)S(1)} %get-tuple-element.47), channel_id=1, source_target_pairs={{0,8},{4,12},{8,0},{12,4},{1,9},{5,13},{9,1},{13,5},{2,10},{6,14},... | collective-permute-start | bytes 1544 | tf_op jit(solution)/shard_map/ppermute | solution.py:41
  72.0 5.1 %collective-permute-start.23 = (f32[1,128]{1,0:T(1,128)S(1)}, f32[1,128]{1,0:T(1,128)S(1)}, u32[]{:S(2)}, u32[]{:S(2)}) collective-permute-start(f32[1,128]{1,0:T(1,128)S(1)} %add_add_fusion.12), channel_id=1, source_target_pairs={{0,2},{1,3},{2,0},{3,1},{4,6},{5,7},{6,4},{7,5},{8,10},{9,11},{10,... | collective-permute-start | bytes 1544 | tf_op jit(solution)/shard_map/ppermute | solution.py:41
  82.7 5.8 %collective-permute-start.24 = (f32[32,640]{1,0:T(8,128)S(1)}, f32[32,640]{1,0:T(8,128)S(1)}, u32[]{:S(2)}, u32[]{:S(2)}) collective-permute-start(f32[32,640]{1,0:T(8,128)S(1)} %get-tuple-element.50), channel_id=1, source_target_pairs={{0,1},{1,0},{2,3},{3,2},{4,5},{5,4},{6,7},{7,6},{8,9},{9,8},{10,11... | collective-permute-start | bytes 245768 | tf_op jit(solution)/shard_map/ppermute | solution.py:41
  83.6 5.7 %collective-permute-start.25 = (f32[32,640]{1,0:T(8,128)S(1)}, f32[32,640]{1,0:T(8,128)S(1)}, u32[]{:S(2)}, u32[]{:S(2)}) collective-permute-start(f32[32,640]{1,0:T(8,128)S(1)} %get-tuple-element.51), channel_id=1, source_target_pairs={{0,3},{1,2},{2,1},{3,0},{4,7},{5,6},{6,5},{7,4},{8,11},{9,10},{10,... | collective-permute-start | bytes 245768 | tf_op jit(solution)/shard_map/ppermute | solution.py:41
  84.8 5.9 %collective-permute-start.26 = (f32[32,640]{1,0:T(8,128)S(1)}, f32[32,640]{1,0:T(8,128)S(1)}, u32[]{:S(2)}, u32[]{:S(2)}) collective-permute-start(f32[32,640]{1,0:T(8,128)S(1)} %get-tuple-element.52), channel_id=1, source_target_pairs={{0,2},{1,3},{2,0},{3,1},{4,6},{5,7},{6,4},{7,5},{8,10},{9,11},{10,... | collective-permute-start | bytes 245768 | tf_op jit(solution)/shard_map/ppermute | solution.py:41
  90.8 6.0 %collective-permute-start.29 = (f32[32,640]{1,0:T(8,128)S(1)}, f32[32,640]{1,0:T(8,128)S(1)}, u32[]{:S(2)}, u32[]{:S(2)}) collective-permute-start(f32[32,640]{1,0:T(8,128)S(1)} %add_add_fusion.3), channel_id=1, source_target_pairs={{0,8},{4,12},{8,0},{12,4},{1,9},{5,13},{9,1},{13,5},{2,10},{6,14},... | collective-permute-start | bytes 245768 | tf_op jit(solution)/shard_map/ppermute | solution.py:41
  93.0 5.7 %collective-permute-start.28 = (f32[32,640]{1,0:T(8,128)S(1)}, f32[32,640]{1,0:T(8,128)S(1)}, u32[]{:S(2)}, u32[]{:S(2)}) collective-permute-start(f32[32,640]{1,0:T(8,128)S(1)} %add_add_fusion.3), channel_id=1, source_target_pairs={{0,12},{4,8},{8,4},{12,0},{1,13},{5,9},{9,5},{13,1},{2,14},{6,10},... | collective-permute-start | bytes 245768 | tf_op jit(solution)/shard_map/ppermute | solution.py:41
  98.7 5.8 %collective-permute-start.32 = (f32[32,512]{1,0:T(8,128)S(1)}, f32[32,512]{1,0:T(8,128)S(1)}, u32[]{:S(2)}, u32[]{:S(2)}) collective-permute-start(f32[32,512]{1,0:T(8,128)S(1)} %slice.27.refs_1_), channel_id=1, source_target_pairs={{0,2},{1,3},{2,0},{3,1},{4,6},{5,7},{6,4},{7,5},{8,10},{9,11},{10,... | collective-permute-start | bytes 196616 | tf_op jit(solution)/shard_map/ppermute | solution.py:41
  100.8 5.5 %collective-permute-start.31 = (f32[32,512]{1,0:T(8,128)S(1)}, f32[32,512]{1,0:T(8,128)S(1)}, u32[]{:S(2)}, u32[]{:S(2)}) collective-permute-start(f32[32,512]{1,0:T(8,128)S(1)} %slice.27.refs_1_), channel_id=1, source_target_pairs={{0,3},{1,2},{2,1},{3,0},{4,7},{5,6},{6,5},{7,4},{8,11},{9,10},{10,... | collective-permute-start | bytes 196616 | tf_op jit(solution)/shard_map/ppermute | solution.py:41
  120.6 7.2 %collective-permute-start.40 = (f32[32,896]{1,0:T(8,128)S(1)}, f32[32,896]{1,0:T(8,128)S(1)}, u32[]{:S(2)}, u32[]{:S(2)}) collective-permute-start(f32[32,896]{1,0:T(8,128)S(1)} %add.168), channel_id=1, source_target_pairs={{0,64},{32,96},{64,0},{96,32},{16,80},{48,112},{80,16},{112,48},{1... | collective-permute-start | bytes 344072 | tf_op jit(solution)/shard_map/ppermute | solution.py:41
  122.9 7.3 %collective-permute-start.39 = (f32[32,896]{1,0:T(8,128)S(1)}, f32[32,896]{1,0:T(8,128)S(1)}, u32[]{:S(2)}, u32[]{:S(2)}) collective-permute-start(f32[32,896]{1,0:T(8,128)S(1)} %add.168), channel_id=1, source_target_pairs={{0,96},{32,64},{64,32},{96,0},{16,112},{48,80},{80,48},{112,16},{1... | collective-permute-start | bytes 344072 | tf_op jit(solution)/shard_map/ppermute | solution.py:41
  124.2 6.0 %collective-permute-start.38 = (f32[32,896]{1,0:T(8,128)S(1)}, f32[32,896]{1,0:T(8,128)S(1)}, u32[]{:S(2)}, u32[]{:S(2)}) collective-permute-start(f32[32,896]{1,0:T(8,128)S(1)} %add.168), channel_id=1, source_target_pairs={{0,32},{32,0},{64,96},{96,64},{16,48},{48,16},{80,112},{112,80},{1... | collective-permute-start | bytes 344072 | tf_op jit(solution)/shard_map/ppermute | solution.py:41
  146.0 5.3 %collective-permute-start.50 = (f32[32,128]{1,0:T(8,128)S(1)}, f32[32,128]{1,0:T(8,128)S(1)}, u32[]{:S(2)}, u32[]{:S(2)}) collective-permute-start(f32[32,128]{1,0:T(8,128)S(1)} %get-tuple-element.60), channel_id=1, source_target_pairs={{0,8},{4,12},{8,0},{12,4},{1,9},{5,13},{9,1},{13,5},{2,10},{6,14},... | collective-permute-start | bytes 49160 | tf_op jit(solution)/shard_map/ppermute | solution.py:41
  153.2 5.3 %collective-permute-start.53 = (f32[32,128]{1,0:T(8,128)S(1)}, f32[32,128]{1,0:T(8,128)S(1)}, u32[]{:S(2)}, u32[]{:S(2)}) collective-permute-start(f32[32,128]{1,0:T(8,128)S(1)} %add_add_fusion.7), channel_id=1, source_target_pairs={{0,2},{1,3},{2,0},{3,1},{4,6},{5,7},{6,4},{7,5},{8,10},{9,11},{10,... | collective-permute-start | bytes 49160 | tf_op jit(solution)/shard_map/ppermute | solution.py:41
  (32 other events, 163.3 us)

commit v4 on v3

--- a/solution.py
+++ b/solution.py
@@ -15,7 +15,7 @@
 COLS = 1536
 QUARTER = ROWS // 4
 HALF = COLS // 2
-BLOCK = 512
+BLOCK = 1024
 LANES = 128
 
 EPSILON = 1e-06
@@ -24,7 +24,6 @@
 BF16 = jnp.bfloat16
 NT = (((1,), (1,)), ((), ()))
 NN = (((1,), (0,)), ((), ()))
-TN = (((0,), (0,)), ((), ()))
 
 X_RINGS = [[x * 2 + c for x in range(4)] for c in range(2)]
 CORE_PAIRS = [[x * 2, x * 2 + 1] for x in range(4)]
@@ -46,6 +45,10 @@
     return (value + got[0]) + (got[1] + got[2])
 
 
+def from_all(value):
+    return lax.all_to_all(value, "var", 0, 0)
+
+
 def pair_sum(value):
     return value + swap(value, "vox", CORE_PAIRS, 1)
 
@@ -91,6 +94,7 @@
 
 
 def shrunk_of(values, squares, levels, side, count):
+    squares = jnp.sum(squares, axis=0)
     thresholds = levels[side : side + 1, :].astype(F32) / 1024.0
     level = to_column(thresholds * jnp.sqrt(squares[:, :K] / count + EPSILON))
     return values - jnp.clip(values, -level, level)
@@ -222,14 +226,14 @@
                 outs[at][:, :QUARTER] = product
                 outs[at][:, QUARTER:] = gram_ref[...]
 
-    whole = lambda shape: pl.BlockSpec(shape, lambda i, p: (0, 0))
+    whole = lambda shape: pl.BlockSpec(shape, lambda i, p: (0,) * len(shape))
     shapes = [((K, QUARTER + LANES), F32)] * 3 + [((2 * K, COLS), BF16), ((K, LANES), F32)]
     return pl.pallas_call(
         kernel,
         grid_spec=pltpu.PrefetchScalarGridSpec(
             num_scalar_prefetch=1,
             grid=(3,),
-            in_specs=[whole((K, COLS)), whole((1, LANES)), whole((2, K))]
+            in_specs=[whole((K, COLS)), whole((16, 1, LANES)), whole((2, K))]
             + [pl.BlockSpec((QUARTER, COLS), lambda i, p: (p[Z_AT + 1 + i], 0))],
             out_specs=[whole(shape) for shape, _ in shapes],
         ),
@@ -244,7 +248,7 @@
         out_ref[:, :QUARTER] = left_terms_of(both_ref, cross_ref[...])
         out_ref[:, QUARTER:] = gram_ref[...]
 
-    whole = lambda shape: pl.BlockSpec(shape, lambda i, p: (0, 0))
+    whole = lambda shape: pl.BlockSpec(shape, lambda i, p: (0,) * len(shape))
     return pl.pallas_call(
         kernel,
         grid_spec=pltpu.PrefetchScalarGridSpec(
@@ -263,33 +267,21 @@
 
 def right_half(head, given, cross, places, at):
     def kernel(places_ref, *refs):
-        step = pl.program_id(0)
         if head:
             left_ref, squares_ref, levels_ref, cross_ref, out_ref, both_ref, gram_ref, shrunk_ref = refs
 
-            @pl.when(step == 0)
-            def _():
-                values = shrunk_of(left_ref[...], squares_ref[...], levels_ref[...], 0, NV)
-                shrunk_ref[...] = values
-                both_ref[...] = jnp.concatenate(split2(values), axis=0)
-                gram_ref[...] = padded(cross_gram(values, values))
+            values = shrunk_of(left_ref[...], squares_ref[...], levels_ref[...], 0, NV)
+            shrunk_ref[...] = values
+            both_ref[...] = jnp.concatenate(split2(values), axis=0)
+            gram_ref[...] = padded(cross_gram(values, values))
         else:
             both_ref, gram_ref, cross_ref, out_ref = refs
         high, low = split2(cross_ref[...])
-        both = both_ref[:, pl.ds(pl.multiple_of(step * BLOCK, BLOCK), BLOCK)]
-        whole = dot(both, high, NN)
-        product = whole[:K] + (whole[K:] + dot(both[:K], low, NN))
-
-        @pl.when(step == 0)
-        def _():
-            out_ref[:, :HALF] = product
-            out_ref[:, HALF:] = gram_ref[...]
-
-        @pl.when(step > 0)
-        def _():
-            out_ref[:, :HALF] += product
-
-    whole = lambda shape: pl.BlockSpec(shape, lambda i, p: (0, 0))
+        product = dot(both_ref[...], high, NN)
+        out_ref[:, :HALF] = product[:K] + (product[K:] + dot(both_ref[:K], low, NN))
+        out_ref[:, HALF:] = gram_ref[...]
+
+    whole = lambda shape: pl.BlockSpec(shape, lambda i, p: (0,) * len(shape))
     out_shape = [jax.ShapeDtypeStruct((K, HALF + LANES), F32)]
     if head:
         out_shape += [
@@ -301,9 +293,9 @@
         kernel,
         grid_spec=pltpu.PrefetchScalarGridSpec(
             num_scalar_prefetch=1,
-            grid=(ROWS // BLOCK,),
+            grid=(1,),
             in_specs=[whole(g.shape) for g in given]
-            + [pl.BlockSpec((BLOCK, HALF), lambda i, p: (i, p[CORE_AT + at]))],
+            + [pl.BlockSpec((ROWS, HALF), lambda i, p: (0, p[CORE_AT + at]))],
             out_specs=[whole(o.shape) for o in out_shape],
         ),
         out_shape=out_shape,
@@ -326,7 +318,7 @@
     )(gram)
 
 
-def assemble(inverse, blocks, places, start, order):
+def assemble(inverse, blocks, places, start, copies, order):
     width = blocks[0].shape[1]
     n = len(blocks)
 
@@ -341,7 +333,7 @@
                 values = full_dot(inverse_ref[:, :K], values, NN)
             out_ref[:, pl.ds(pl.multiple_of(places_ref[start + at] * width, width), width)] = values
             total = total + jnp.sum(values * values, axis=1, keepdims=True)
-        squares_ref[...] = to_row(total)
+        squares_ref[...] = jnp.broadcast_to(to_row(total)[None], (copies, 1, LANES))
 
     args = blocks if inverse is None else [inverse, *blocks]
     vmem = pl.BlockSpec(memory_space=pltpu.VMEM)
@@ -351,7 +343,7 @@
         out_specs=[vmem, vmem],
         out_shape=[
             jax.ShapeDtypeStruct((K, n * width), F32),
-            jax.ShapeDtypeStruct((1, LANES), F32),
+            jax.ShapeDtypeStruct((copies, 1, LANES), F32),
         ],
         compiler_params=PARAMS,
         name=order,
@@ -363,16 +355,15 @@
         sums = right_ref[...]
         values = shrunk_of(sums, squares_ref[...], levels_ref[...], 1, NG)
         shrunk_ref[...] = values
-        out_ref[...] = jnp.concatenate(
-            [cross_gram(values, values), cross_gram(sums, values), jnp.zeros((K, LANES - 2 * K), F32)],
-            axis=1,
-        )
+        both = jnp.concatenate([cross_gram(values, values), cross_gram(sums, values)], axis=1)
+        packed = jnp.concatenate([both[: K // 2], both[K // 2 :]], axis=1)
+        out_ref[...] = jnp.broadcast_to(packed[None], (16, K // 2, LANES))
 
     return pl.pallas_call(
         kernel,
         out_shape=[
             jax.ShapeDtypeStruct((K, COLS), F32),
-            jax.ShapeDtypeStruct((K, LANES), F32),
+            jax.ShapeDtypeStruct((16, K // 2, LANES), F32),
         ],
         compiler_params=PARAMS,
         name="last_shrink",
@@ -384,13 +375,13 @@
         left = full_dot(inverse_ref[:, :K], shrunk_ref[...], NN)
         out_ref[...] = left
         high, middle, low = split3(left)
-        terms_ref[...] = jnp.concatenate([high, high, middle, high, middle, low], axis=0)
+        terms_ref[...] = jnp.concatenate([high, high, middle, high, middle, low], axis=0).T
 
     return pl.pallas_call(
         kernel,
         out_shape=[
             jax.ShapeDtypeStruct((K, ROWS), F32),
-            jax.ShapeDtypeStruct((6 * K, ROWS), BF16),
+            jax.ShapeDtypeStruct((ROWS, 6 * K), BF16),
         ],
         compiler_params=PARAMS,
         name="mix_left",
@@ -403,24 +394,26 @@
 
         @pl.when(step == 0)
         def _():
-            inverse = inverse_factor(last_ref[:, :K], NG)
+            packed = jnp.sum(last_ref[...], axis=0)
+            last = jnp.concatenate([packed[:, : 2 * K], packed[:, 2 * K :]], axis=0)
+            inverse = inverse_factor(last[:, :K], NG)
             right = full_dot(inverse, shrunk_ref[...], NN)
             right_ref[...] = right
-            strength = jnp.sum(inverse * last_ref[:, K : 2 * K], axis=1, keepdims=True) / math.sqrt(NV * NG)
+            strength = jnp.sum(inverse * last[:, K:], axis=1, keepdims=True) / math.sqrt(NV * NG)
             strength_ref[...] = to_row(strength)[:, :K]
             high, middle, low = split3(right * (strength / math.sqrt(NV * NG)))
             terms_ref[...] = jnp.concatenate([high, middle, high, low, middle, high], axis=0)
 
-        out_ref[...] = cross_ref[...] - dot(left_ref[...], terms_ref[...], TN)
-
-    whole = lambda shape: pl.BlockSpec(shape, lambda i: (0, 0))
+        out_ref[...] = cross_ref[...] - dot(left_ref[...], terms_ref[...], NN)
+
+    whole = lambda shape: pl.BlockSpec(shape, lambda i: (0,) * len(shape))
     return pl.pallas_call(
         kernel,
         grid=(ROWS // BLOCK,),
         in_specs=[
-            whole((K, LANES)),
+            whole((16, K // 2, LANES)),
             whole((K, COLS)),
-            pl.BlockSpec((6 * K, BLOCK), lambda i: (0, i)),
+            pl.BlockSpec((BLOCK, 6 * K), lambda i: (i, 0)),
             pl.BlockSpec((BLOCK, COLS), lambda i: (i, 0)),
         ],
         out_specs=[
@@ -455,7 +448,7 @@
         block = total[:, :QUARTER]
         blocks = [block] + [swap(block, "var", Z_RINGS, mask) for mask in MASKS]
         inverse = factor(total[:, QUARTER:], NG) if sweep else None
-        left_sum, squares = assemble(inverse, blocks, places, Z_AT, "assemble_left")
+        left_sum, squares = assemble(inverse, blocks, places, Z_AT, 1, "assemble_left")
         squares = ring_sum(pair_sum(squares), "vox", X_RINGS)
 
         part, both, gram, left_shrunk = right_half(True, (left_sum, squares, levels), cross, places, 1)
@@ -463,13 +456,16 @@
         (total,) = right_half(False, (both, gram), cross, places, 0)
         total = ring_sum(total + got, "vox", X_RINGS)
         block = total[:, :HALF]
-        blocks = [block, swap(block, "vox", CORE_PAIRS, 1)]
+        got = swap(block, "vox", CORE_PAIRS, 1)
         inverse = factor(total[:, HALF:], NV)
-        right_sum, squares = assemble(inverse, blocks, places, CORE_AT, "assemble_right")
-        squares = ring_sum(ring_sum(squares, "var", Y_RINGS), "var", Z_RINGS)
-    left_dirs, left_terms = mix_left(inverse, left_shrunk)
+        if sweep == ITERS - 1:
+            left_dirs, left_terms = mix_left(inverse, left_shrunk)
+            got, left_terms = lax.optimization_barrier((got, left_terms))
+        blocks = [block, got]
+        right_sum, squares = assemble(inverse, blocks, places, CORE_AT, 16, "assemble_right")
+        squares = from_all(squares)
     right_shrunk, last = last_shrink(right_sum, squares, levels)
-    last = ring_sum(ring_sum(last, "var", Y_RINGS), "var", Z_RINGS)
+    last = from_all(last)
     deflated, right_dirs, strength = deflate(last, right_shrunk, left_terms, cross)
     return (deflated, left_dirs, right_dirs, strength.reshape(K))
 

time: 167 us -> 159 us (0.952)
  blocking collectives: 0 us -> 33.7 us
  starting transfers between devices: 61.7 us -> 40.4 us
  waiting for transfers between devices: 61.9 us -> 44 us
  Pallas kernels: 41.4 us -> 38.5 us
    all_to_all x0 -> x3, blocking collectives: none -> 33.7 us  [from_all(): return lax.all_to_all(value, 'var', 0, 0)]
    ppermute x54 -> x36, starting transfers between devices: 61.7 us -> 40.4 us  [swap(): return lax.ppermute(value, axis, pairs)]
    ppermute x54 -> x36, waiting for transfers between devices: 61.9 us -> 44 us  [swap(): return lax.ppermute(value, axis, pairs)]
    pallas_call x4, Pallas kernels: 12.2 us -> 8.88 us  [right_half(): pl.pallas_call(kernel, grid_spec=pltpu.PrefetchScalarGridSpec(num_scalar_...]
  transfers between devices with their start and end apart: 54 -> 36, of which waited for: 38 -> 25; matrix products, arithmetic and copies ran while one was open for 0% -> 0% of each run, Pallas kernels for 6% -> 6%
where the time goes in v4:
time: 159 us
  waiting for transfers between devices  44 us (28%)
  starting transfers between devices  40.4 us (25%)
  Pallas kernels  38.5 us (24%)
  blocking collectives  33.7 us (21%)
    ppermute x36, waiting for transfers between devices, swap(): return lax.ppermute(value, axis, pairs)  44 us
    ppermute x36, starting transfers between devices, swap(): return lax.ppermute(value, axis, pairs)  40.4 us
    all_to_all x3, blocking collectives, from_all(): return lax.all_to_all(value, 'var', 0, 0)  33.7 us
    pallas_call x4, Pallas kernels, right_half(): pl.pallas_call(kernel, grid_spec=pltpu.PrefetchScalarGridSpec(num_scalar_...  8.88 us
    pallas_call x1, Pallas kernels, left_product_first(): pl.pallas_call(kernel, grid_spec=pltpu.PrefetchScalarGridSpec(num_scalar_...  8.13 us
    pallas_call x1, Pallas kernels, deflate(): pl.pallas_call(kernel, grid=(ROWS // BLOCK,), in_specs=[whole((16, K // 2...  7.07 us
    pallas_call x1, Pallas kernels, left_partners(): pl.pallas_call(kernel, grid_spec=pltpu.PrefetchScalarGridSpec(num_scalar_...  4.46 us
    pallas_call x4, Pallas kernels, assemble(): pl.pallas_call(kernel, in_specs=[pl.BlockSpec(memory_space=pltpu.SMEM)] +...  3.44 us
  transfers between devices with their start and end apart: 36, of which 25 were waited for; matrix products, arithmetic and copies ran while one was open for 0% of the time, Pallas kernels for 6%

profile of v4, /device:TPU:0, one launch (start us, length us, event | category | flops | bytes accessed | tf_op | source)
XLA Modules:
  0.0 158.6 jit_solution(11830512043144582028)
XLA Ops:
  2.2 8.1 %left_product_first.1 = (f32[32,512]{1,0:T(8,128)S(1)}, f32[32,512]{1,0:T(8,128)S(1)}, f32[32,512]{1,0:T(8,128)S(1)}, f32[32,512]{1,0:T(8,128)S(1)}, f32[2048,1536]{1,0:T(8,128)S(1)}) custom-call(s32[8]{0:T(128)S(1)} %own_places.1.places_ref, f32[32,1536]{1,0:T(8,128)S(1)} %copy-done, f32[2048,1536]{1,0:T(8,128)} %cross_ref.1), custom_call_target="tpu_custom_call" | custom-call | tf_op jit(solution)/shard_map/left_product_first/pallas_call | solution.py:188
  12.4 2.5 %collective-permute-start.1 = (f32[32,512]{1,0:T(8,128)S(1)}, f32[32,512]{1,0:T(8,128)S(1)}, u32[]{:S(2)}, u32[]{:S(2)}) collective-permute-start(f32[32,512]{1,0:T(8,128)S(1)} %get-tuple-element.40), channel_id=1, source_target_pairs={{0,3},{1,2},{2,1},{3,0},{4,7},{5,6},{6,5},{7,4},{8,11},{9,10},{10,... | collective-permute-start | bytes 196616 | tf_op jit(solution)/shard_map/ppermute | solution.py:40
  17.9 2.8 %collective-permute-done.2 = f32[32,512]{1,0:T(8,128)S(1)} collective-permute-done((f32[32,512]{1,0:T(8,128)S(1)}, f32[32,512]{1,0:T(8,128)S(1)}, u32[]{:S(2)}, u32[]{:S(2)}) %collective-permute-start.2) | collective-permute-done | bytes 65568 | tf_op jit(solution)/shard_map/ppermute | solution.py:40
  20.7 3.3 %collective-permute-start.5 = (f32[32,512]{1,0:T(8,128)S(1)}, f32[32,512]{1,0:T(8,128)S(1)}, u32[]{:S(2)}, u32[]{:S(2)}) collective-permute-start(f32[32,512]{1,0:T(8,128)S(1)} %add_add_fusion.5), channel_id=1, source_target_pairs={{0,8},{4,12},{8,0},{12,4},{1,9},{5,13},{9,1},{13,5},{2,10},{6,14},... | collective-permute-start | bytes 196616 | tf_op jit(solution)/shard_map/ppermute | solution.py:40
  26.7 2.8 %collective-permute-done.4 = f32[32,512]{1,0:T(8,128)S(1)} collective-permute-done((f32[32,512]{1,0:T(8,128)S(1)}, f32[32,512]{1,0:T(8,128)S(1)}, u32[]{:S(2)}, u32[]{:S(2)}) %collective-permute-start.4) | collective-permute-done | bytes 65568 | tf_op jit(solution)/shard_map/ppermute | solution.py:40
  30.6 2.6 %collective-permute-start.7 = (f32[32,512]{1,0:T(8,128)S(1)}, f32[32,512]{1,0:T(8,128)S(1)}, u32[]{:S(2)}, u32[]{:S(2)}) collective-permute-start(f32[32,512]{1,0:T(8,128)S(1)} %add_add_fusion.4.refs_0_), channel_id=1, source_target_pairs={{0,3},{1,2},{2,1},{3,0},{4,7},{5,6},{6,5},{7,4},{8,11},{9,10},{10,... | collective-permute-start | bytes 196616 | tf_op jit(solution)/shard_map/ppermute | solution.py:40
  39.4 3.0 %collective-permute-start.12 = (f32[1,1,128]{2,1,0:T(1,128)S(1)}, f32[1,1,128]{2,1,0:T(1,128)S(1)}, u32[]{:S(2)}, u32[]{:S(2)}) collective-permute-start(f32[1,1,128]{2,1,0:T(1,128)S(1)} %add.90), channel_id=1, source_target_pairs={{0,64},{32,96},{64,0},{96,32},{16,80},{48,112},{80,16},{112,48},{1... | collective-permute-start | bytes 1544 | tf_op jit(solution)/shard_map/ppermute | solution.py:40
  44.4 2.7 %collective-permute-done.11 = f32[1,1,128]{2,1,0:T(1,128)S(1)} collective-permute-done((f32[1,1,128]{2,1,0:T(1,128)S(1)}, f32[1,1,128]{2,1,0:T(1,128)S(1)}, u32[]{:S(2)}, u32[]{:S(2)}) %collective-permute-start.11) | collective-permute-done | bytes 544 | tf_op jit(solution)/shard_map/ppermute | solution.py:40
  47.2 2.2 %right_half_head.2 = (f32[32,896]{1,0:T(8,128)S(1)}, bf16[64,2048]{1,0:T(8,128)(2,1)S(1)}, f32[32,128]{1,0:T(8,128)S(1)}, f32[32,2048]{1,0:T(8,128)}) custom-call(s32[8]{0:T(128)S(1)} %own_places.1.places_ref, f32[32,2048]{1,0:T(8,128)S(1)} %get-tuple-element.42.refs_0_, f32[1,1,128]{2,1,0:T(1,128)S(1)} %add_add_fusion.7.refs_1_, s32[2,32]{1,0:T(2,128)S(1)} %copy-done.1, ...), custom_call_target="tpu_custom_call" | custom-call | flops 1200000000 | bytes 8000000 | tf_op jit(solution)/shard_map/right_half_head/pallas_call | solution.py:292
  49.5 2.2 %right_half.2 = f32[32,896]{1,0:T(8,128)S(1)} custom-call(s32[8]{0:T(128)S(1)} %own_places.1.places_ref, bf16[64,2048]{1,0:T(8,128)(2,1)S(1)} %get-tuple-element.45.refs_0_, f32[32,128]{1,0:T(8,128)S(1)} %get-tuple-element.46.refs_1_, f32[2048,1536]{1,0:T(8,128)S(1)} %get-tuple-element.44.refs_3_.refs_2_.cross_ref), custom_call_target="tpu_custom_call" | custom-call | flops 1200000000 | bytes 8000000 | tf_op jit(solution)/shard_map/right_half/pallas_call | solution.py:292
  55.3 3.9 %collective-permute-done.16 = f32[32,896]{1,0:T(8,128)S(1)} collective-permute-done((f32[32,896]{1,0:T(8,128)S(1)}, f32[32,896]{1,0:T(8,128)S(1)}, u32[]{:S(2)}, u32[]{:S(2)}) %collective-permute-start.16) | collective-permute-done | bytes 114720 | tf_op jit(solution)/shard_map/ppermute | solution.py:40
  63.7 11.4 %all_to_all.15.squares_ref = f32[16,1,128]{2,1,0:T(1,128)S(1)} all-to-all(f32[16,1,128]{2,1,0:T(1,128)S(1)} %get-tuple-element.49), channel_id=1, replica_groups=mesh['vox'=8,'var'=16] {'var'}, dimensions={0} | all-to-all | bytes 16384 | tf_op jit(solution)/shard_map/all_to_all | solution.py:49
  75.1 4.5 %left_partners.1 = (f32[32,640]{1,0:T(8,128)S(1)}, f32[32,640]{1,0:T(8,128)S(1)}, f32[32,640]{1,0:T(8,128)S(1)}, bf16[64,1536]{1,0:T(8,128)(2,1)S(1)}, f32[32,128]{1,0:T(8,128)S(1)}) custom-call(s32[8]{0:T(128)S(1)} %own_places.1.places_ref, f32[32,1536]{1,0:T(8,128)S(1)} %get-tuple-element.48.right_ref, f32[16,1,128]{2,1,0:T(1,128)S(1)} %all_to_all.15.squares_ref, ...), custom_call_target="tpu_custom_call" | custom-call | tf_op jit(solution)/shard_map/left_partners/pallas_call | solution.py:231
  81.4 2.3 %collective-permute-start.20 = (f32[32,640]{1,0:T(8,128)S(1)}, f32[32,640]{1,0:T(8,128)S(1)}, u32[]{:S(2)}, u32[]{:S(2)}) collective-permute-start(f32[32,640]{1,0:T(8,128)S(1)} %get-tuple-element.54), channel_id=1, source_target_pairs={{0,2},{1,3},{2,0},{3,1},{4,6},{5,7},{6,4},{7,5},{8,10},{9,11},{10,... | collective-permute-start | bytes 245768 | tf_op jit(solution)/shard_map/ppermute | solution.py:40
  90.9 2.5 %collective-permute-done.23 = f32[32,640]{1,0:T(8,128)S(1)} collective-permute-done((f32[32,640]{1,0:T(8,128)S(1)}, f32[32,640]{1,0:T(8,128)S(1)}, u32[]{:S(2)}, u32[]{:S(2)}) %collective-permute-start.23) | collective-permute-done | bytes 81952 | tf_op jit(solution)/shard_map/ppermute | solution.py:40
  95.2 2.4 %collective-permute-start.26 = (f32[32,512]{1,0:T(8,128)S(1)}, f32[32,512]{1,0:T(8,128)S(1)}, u32[]{:S(2)}, u32[]{:S(2)}) collective-permute-start(f32[32,512]{1,0:T(8,128)S(1)} %slice.27.refs_1_), channel_id=1, source_target_pairs={{0,2},{1,3},{2,0},{3,1},{4,6},{5,7},{6,4},{7,5},{8,10},{9,11},{10,... | collective-permute-start | bytes 196616 | tf_op jit(solution)/shard_map/ppermute | solution.py:40
  111.4 2.2 %right_half_head.3 = (f32[32,896]{1,0:T(8,128)S(1)}, bf16[64,2048]{1,0:T(8,128)(2,1)S(1)}, f32[32,128]{1,0:T(8,128)S(1)}, f32[32,2048]{1,0:T(8,128)S(1)}) custom-call(s32[8]{0:T(128)S(1)} %own_places.1.places_ref, f32[32,2048]{1,0:T(8,128)S(1)} %get-tuple-element.55.refs_0_, f32[1,1,128]{2,1,0:T(1,128)S(1)} %add_add_fusion.6.refs_1_, s32[2,32]{1,0:T(2,128)S(1)} %copy-done.1, ...), custom_call_target="tpu_custom_call" | custom-call | flops 1200000000 | bytes 8000000 | tf_op jit(solution)/shard_map/right_half_head/pallas_call | solution.py:292
  113.8 2.2 %right_half.3 = f32[32,896]{1,0:T(8,128)S(1)} custom-call(s32[8]{0:T(128)S(1)} %own_places.1.places_ref, bf16[64,2048]{1,0:T(8,128)(2,1)S(1)} %get-tuple-element.57.refs_0_, f32[32,128]{1,0:T(8,128)S(1)} %get-tuple-element.58.refs_1_, f32[2048,1536]{1,0:T(8,128)S(1)} %get-tuple-element.44.refs_3_.refs_2_.cross_ref), custom_call_target="tpu_custom_call" | custom-call | flops 1200000000 | bytes 8000000 | tf_op jit(solution)/shard_map/right_half/pallas_call | solution.py:292
  116.0 2.3 %collective-permute-start.34 = (f32[32,896]{1,0:T(8,128)S(1)}, f32[32,896]{1,0:T(8,128)S(1)}, u32[]{:S(2)}, u32[]{:S(2)}) collective-permute-start(f32[32,896]{1,0:T(8,128)S(1)} %add.108), channel_id=1, source_target_pairs={{0,64},{32,96},{64,0},{96,32},{16,80},{48,112},{80,16},{112,48},{1... | collective-permute-start | bytes 344072 | tf_op jit(solution)/shard_map/ppermute | solution.py:40
  119.6 3.6 %collective-permute-done.34 = f32[32,896]{1,0:T(8,128)S(1)} collective-permute-done((f32[32,896]{1,0:T(8,128)S(1)}, f32[32,896]{1,0:T(8,128)S(1)}, u32[]{:S(2)}, u32[]{:S(2)}) %collective-permute-start.34) | collective-permute-done | bytes 114720 | tf_op jit(solution)/shard_map/ppermute | solution.py:40
  123.2 2.4 %collective-permute-done.33 = f32[32,896]{1,0:T(8,128)S(1)} collective-permute-done((f32[32,896]{1,0:T(8,128)S(1)}, f32[32,896]{1,0:T(8,128)S(1)}, u32[]{:S(2)}, u32[]{:S(2)}) %collective-permute-start.33) | collective-permute-done | bytes 114720 | tf_op jit(solution)/shard_map/ppermute | solution.py:40
  128.6 11.4 %all_to_all.16.squares_ref = f32[16,1,128]{2,1,0:T(1,128)S(1)} all-to-all(f32[16,1,128]{2,1,0:T(1,128)S(1)} %get-tuple-element.64), channel_id=1, replica_groups=mesh['vox'=8,'var'=16] {'var'}, dimensions={0} | all-to-all | bytes 16384 | tf_op jit(solution)/shard_map/all_to_all | solution.py:49
  140.7 10.8 %all_to_all.17.last_ref = f32[16,16,128]{2,1,0:T(8,128)S(1)} all-to-all(f32[16,16,128]{2,1,0:T(8,128)S(1)} %get-tuple-element.65), channel_id=1, replica_groups=mesh['vox'=8,'var'=16] {'var'}, dimensions={0} | all-to-all | bytes 262144 | tf_op jit(solution)/shard_map/all_to_all | solution.py:49
  151.6 7.1 %deflate.1 = (f32[2048,1536]{1,0:T(8,128)}, f32[32,1536]{1,0:T(8,128)}, f32[1,32]{1,0:T(1,128)}) custom-call(f32[16,16,128]{2,1,0:T(8,128)S(1)} %all_to_all.17.last_ref, f32[32,1536]{1,0:T(8,128)S(1)} %get-tuple-element.66.shrunk_ref, bf16[2048,192]{1,0:T(8,128)(2,1)S(1)} %get-tuple-element.67.left_ref, ...), custom_call_target="tpu_custom_call" | custom-call | tf_op jit(solution)/shard_map/deflate/pallas_call | solution.py:410
  (91 shorter events, 56.3 us)
Async XLA Ops:
  10.3 5.7 %collective-permute-start = (f32[32,512]{1,0:T(8,128)S(1)}, f32[32,512]{1,0:T(8,128)S(1)}, u32[]{:S(2)}, u32[]{:S(2)}) collective-permute-start(f32[32,512]{1,0:T(8,128)S(1)} %get-tuple-element.39), channel_id=1, source_target_pairs={{0,1},{1,0},{2,3},{3,2},{4,5},{5,4},{6,7},{7,6},{8,9},{9,8},{10,11... | collective-permute-start | bytes 196616 | tf_op jit(solution)/shard_map/ppermute | solution.py:40
  12.4 5.5 %collective-permute-start.1 = (f32[32,512]{1,0:T(8,128)S(1)}, f32[32,512]{1,0:T(8,128)S(1)}, u32[]{:S(2)}, u32[]{:S(2)}) collective-permute-start(f32[32,512]{1,0:T(8,128)S(1)} %get-tuple-element.40), channel_id=1, source_target_pairs={{0,3},{1,2},{2,1},{3,0},{4,7},{5,6},{6,5},{7,4},{8,11},{9,10},{10,... | collective-permute-start | bytes 196616 | tf_op jit(solution)/shard_map/ppermute | solution.py:40
  14.9 5.8 %collective-permute-start.2 = (f32[32,512]{1,0:T(8,128)S(1)}, f32[32,512]{1,0:T(8,128)S(1)}, u32[]{:S(2)}, u32[]{:S(2)}) collective-permute-start(f32[32,512]{1,0:T(8,128)S(1)} %get-tuple-element.41), channel_id=1, source_target_pairs={{0,2},{1,3},{2,0},{3,1},{4,6},{5,7},{6,4},{7,5},{8,10},{9,11},{10,... | collective-permute-start | bytes 196616 | tf_op jit(solution)/shard_map/ppermute | solution.py:40
  20.7 6.0 %collective-permute-start.5 = (f32[32,512]{1,0:T(8,128)S(1)}, f32[32,512]{1,0:T(8,128)S(1)}, u32[]{:S(2)}, u32[]{:S(2)}) collective-permute-start(f32[32,512]{1,0:T(8,128)S(1)} %add_add_fusion.5), channel_id=1, source_target_pairs={{0,8},{4,12},{8,0},{12,4},{1,9},{5,13},{9,1},{13,5},{2,10},{6,14},... | collective-permute-start | bytes 196616 | tf_op jit(solution)/shard_map/ppermute | solution.py:40
  24.0 5.5 %collective-permute-start.4 = (f32[32,512]{1,0:T(8,128)S(1)}, f32[32,512]{1,0:T(8,128)S(1)}, u32[]{:S(2)}, u32[]{:S(2)}) collective-permute-start(f32[32,512]{1,0:T(8,128)S(1)} %add_add_fusion.5), channel_id=1, source_target_pairs={{0,12},{4,8},{8,4},{12,0},{1,13},{5,9},{9,5},{13,1},{2,14},{6,10},... | collective-permute-start | bytes 196616 | tf_op jit(solution)/shard_map/ppermute | solution.py:40
  29.5 5.8 %collective-permute-start.8 = (f32[32,512]{1,0:T(8,128)S(1)}, f32[32,512]{1,0:T(8,128)S(1)}, u32[]{:S(2)}, u32[]{:S(2)}) collective-permute-start(f32[32,512]{1,0:T(8,128)S(1)} %add_add_fusion.4.refs_0_), channel_id=1, source_target_pairs={{0,2},{1,3},{2,0},{3,1},{4,6},{5,7},{6,4},{7,5},{8,10},{9,11},{10,... | collective-permute-start | bytes 196616 | tf_op jit(solution)/shard_map/ppermute | solution.py:40
  30.6 5.5 %collective-permute-start.7 = (f32[32,512]{1,0:T(8,128)S(1)}, f32[32,512]{1,0:T(8,128)S(1)}, u32[]{:S(2)}, u32[]{:S(2)}) collective-permute-start(f32[32,512]{1,0:T(8,128)S(1)} %add_add_fusion.4.refs_0_), channel_id=1, source_target_pairs={{0,3},{1,2},{2,1},{3,0},{4,7},{5,6},{6,5},{7,4},{8,11},{9,10},{10,... | collective-permute-start | bytes 196616 | tf_op jit(solution)/shard_map/ppermute | solution.py:40
  39.4 5.0 %collective-permute-start.12 = (f32[1,1,128]{2,1,0:T(1,128)S(1)}, f32[1,1,128]{2,1,0:T(1,128)S(1)}, u32[]{:S(2)}, u32[]{:S(2)}) collective-permute-start(f32[1,1,128]{2,1,0:T(1,128)S(1)} %add.90), channel_id=1, source_target_pairs={{0,64},{32,96},{64,0},{96,32},{16,80},{48,112},{80,16},{112,48},{1... | collective-permute-start | bytes 1544 | tf_op jit(solution)/shard_map/ppermute | solution.py:40
  42.4 4.8 %collective-permute-start.11 = (f32[1,1,128]{2,1,0:T(1,128)S(1)}, f32[1,1,128]{2,1,0:T(1,128)S(1)}, u32[]{:S(2)}, u32[]{:S(2)}) collective-permute-start(f32[1,1,128]{2,1,0:T(1,128)S(1)} %add.90), channel_id=1, source_target_pairs={{0,96},{32,64},{64,32},{96,0},{16,112},{48,80},{80,48},{112,16},{1... | collective-permute-start | bytes 1544 | tf_op jit(solution)/shard_map/ppermute | solution.py:40
  51.7 7.5 %collective-permute-start.16 = (f32[32,896]{1,0:T(8,128)S(1)}, f32[32,896]{1,0:T(8,128)S(1)}, u32[]{:S(2)}, u32[]{:S(2)}) collective-permute-start(f32[32,896]{1,0:T(8,128)S(1)} %add.94), channel_id=1, source_target_pairs={{0,64},{32,96},{64,0},{96,32},{16,80},{48,112},{80,16},{112,48},{1... | collective-permute-start | bytes 344072 | tf_op jit(solution)/shard_map/ppermute | solution.py:40
  53.3 8.1 %collective-permute-start.15 = (f32[32,896]{1,0:T(8,128)S(1)}, f32[32,896]{1,0:T(8,128)S(1)}, u32[]{:S(2)}, u32[]{:S(2)}) collective-permute-start(f32[32,896]{1,0:T(8,128)S(1)} %add.94), channel_id=1, source_target_pairs={{0,96},{32,64},{64,32},{96,0},{16,112},{48,80},{80,48},{112,16},{1... | collective-permute-start | bytes 344072 | tf_op jit(solution)/shard_map/ppermute | solution.py:40
  54.4 6.9 %collective-permute-start.14 = (f32[32,896]{1,0:T(8,128)S(1)}, f32[32,896]{1,0:T(8,128)S(1)}, u32[]{:S(2)}, u32[]{:S(2)}) collective-permute-start(f32[32,896]{1,0:T(8,128)S(1)} %add.94), channel_id=1, source_target_pairs={{0,32},{32,0},{64,96},{96,64},{16,48},{48,16},{80,112},{112,80},{1... | collective-permute-start | bytes 344072 | tf_op jit(solution)/shard_map/ppermute | solution.py:40
  79.6 5.8 %collective-permute-start.18 = (f32[32,640]{1,0:T(8,128)S(1)}, f32[32,640]{1,0:T(8,128)S(1)}, u32[]{:S(2)}, u32[]{:S(2)}) collective-permute-start(f32[32,640]{1,0:T(8,128)S(1)} %get-tuple-element.52), channel_id=1, source_target_pairs={{0,1},{1,0},{2,3},{3,2},{4,5},{5,4},{6,7},{7,6},{8,9},{9,8},{10,11... | collective-permute-start | bytes 245768 | tf_op jit(solution)/shard_map/ppermute | solution.py:40
  80.2 5.8 %collective-permute-start.19 = (f32[32,640]{1,0:T(8,128)S(1)}, f32[32,640]{1,0:T(8,128)S(1)}, u32[]{:S(2)}, u32[]{:S(2)}) collective-permute-start(f32[32,640]{1,0:T(8,128)S(1)} %get-tuple-element.53), channel_id=1, source_target_pairs={{0,3},{1,2},{2,1},{3,0},{4,7},{5,6},{6,5},{7,4},{8,11},{9,10},{10,... | collective-permute-start | bytes 245768 | tf_op jit(solution)/shard_map/ppermute | solution.py:40
  81.4 5.9 %collective-permute-start.20 = (f32[32,640]{1,0:T(8,128)S(1)}, f32[32,640]{1,0:T(8,128)S(1)}, u32[]{:S(2)}, u32[]{:S(2)}) collective-permute-start(f32[32,640]{1,0:T(8,128)S(1)} %get-tuple-element.54), channel_id=1, source_target_pairs={{0,2},{1,3},{2,0},{3,1},{4,6},{5,7},{6,4},{7,5},{8,10},{9,11},{10,... | collective-permute-start | bytes 245768 | tf_op jit(solution)/shard_map/ppermute | solution.py:40
  87.4 6.0 %collective-permute-start.23 = (f32[32,640]{1,0:T(8,128)S(1)}, f32[32,640]{1,0:T(8,128)S(1)}, u32[]{:S(2)}, u32[]{:S(2)}) collective-permute-start(f32[32,640]{1,0:T(8,128)S(1)} %add_add_fusion.3), channel_id=1, source_target_pairs={{0,8},{4,12},{8,0},{12,4},{1,9},{5,13},{9,1},{13,5},{2,10},{6,14},... | collective-permute-start | bytes 245768 | tf_op jit(solution)/shard_map/ppermute | solution.py:40
  88.6 5.7 %collective-permute-start.22 = (f32[32,640]{1,0:T(8,128)S(1)}, f32[32,640]{1,0:T(8,128)S(1)}, u32[]{:S(2)}, u32[]{:S(2)}) collective-permute-start(f32[32,640]{1,0:T(8,128)S(1)} %add_add_fusion.3), channel_id=1, source_target_pairs={{0,12},{4,8},{8,4},{12,0},{1,13},{5,9},{9,5},{13,1},{2,14},{6,10},... | collective-permute-start | bytes 245768 | tf_op jit(solution)/shard_map/ppermute | solution.py:40
  95.2 5.8 %collective-permute-start.26 = (f32[32,512]{1,0:T(8,128)S(1)}, f32[32,512]{1,0:T(8,128)S(1)}, u32[]{:S(2)}, u32[]{:S(2)}) collective-permute-start(f32[32,512]{1,0:T(8,128)S(1)} %slice.27.refs_1_), channel_id=1, source_target_pairs={{0,2},{1,3},{2,0},{3,1},{4,6},{5,7},{6,4},{7,5},{8,10},{9,11},{10,... | collective-permute-start | bytes 196616 | tf_op jit(solution)/shard_map/ppermute | solution.py:40
  97.6 5.5 %collective-permute-start.25 = (f32[32,512]{1,0:T(8,128)S(1)}, f32[32,512]{1,0:T(8,128)S(1)}, u32[]{:S(2)}, u32[]{:S(2)}) collective-permute-start(f32[32,512]{1,0:T(8,128)S(1)} %slice.27.refs_1_), channel_id=1, source_target_pairs={{0,3},{1,2},{2,1},{3,0},{4,7},{5,6},{6,5},{7,4},{8,11},{9,10},{10,... | collective-permute-start | bytes 196616 | tf_op jit(solution)/shard_map/ppermute | solution.py:40
  105.2 5.0 %collective-permute-start.30 = (f32[1,1,128]{2,1,0:T(1,128)S(1)}, f32[1,1,128]{2,1,0:T(1,128)S(1)}, u32[]{:S(2)}, u32[]{:S(2)}) collective-permute-start(f32[1,1,128]{2,1,0:T(1,128)S(1)} %add.104), channel_id=1, source_target_pairs={{0,64},{32,96},{64,0},{96,32},{16,80},{48,112},{80,16},{112,48},{1... | collective-permute-start | bytes 1544 | tf_op jit(solution)/shard_map/ppermute | solution.py:40
  106.7 4.8 %collective-permute-start.29 = (f32[1,1,128]{2,1,0:T(1,128)S(1)}, f32[1,1,128]{2,1,0:T(1,128)S(1)}, u32[]{:S(2)}, u32[]{:S(2)}) collective-permute-start(f32[1,1,128]{2,1,0:T(1,128)S(1)} %add.104), channel_id=1, source_target_pairs={{0,96},{32,64},{64,32},{96,0},{16,112},{48,80},{80,48},{112,16},{1... | collective-permute-start | bytes 1544 | tf_op jit(solution)/shard_map/ppermute | solution.py:40
  116.0 7.2 %collective-permute-start.34 = (f32[32,896]{1,0:T(8,128)S(1)}, f32[32,896]{1,0:T(8,128)S(1)}, u32[]{:S(2)}, u32[]{:S(2)}) collective-permute-start(f32[32,896]{1,0:T(8,128)S(1)} %add.108), channel_id=1, source_target_pairs={{0,64},{32,96},{64,0},{96,32},{16,80},{48,112},{80,16},{112,48},{1... | collective-permute-start | bytes 344072 | tf_op jit(solution)/shard_map/ppermute | solution.py:40
  118.3 7.2 %collective-permute-start.33 = (f32[32,896]{1,0:T(8,128)S(1)}, f32[32,896]{1,0:T(8,128)S(1)}, u32[]{:S(2)}, u32[]{:S(2)}) collective-permute-start(f32[32,896]{1,0:T(8,128)S(1)} %add.108), channel_id=1, source_target_pairs={{0,96},{32,64},{64,32},{96,0},{16,112},{48,80},{80,48},{112,16},{1... | collective-permute-start | bytes 344072 | tf_op jit(solution)/shard_map/ppermute | solution.py:40
  119.6 6.0 %collective-permute-start.32 = (f32[32,896]{1,0:T(8,128)S(1)}, f32[32,896]{1,0:T(8,128)S(1)}, u32[]{:S(2)}, u32[]{:S(2)}) collective-permute-start(f32[32,896]{1,0:T(8,128)S(1)} %add.108), channel_id=1, source_target_pairs={{0,32},{32,0},{64,96},{96,64},{16,48},{48,16},{80,112},{112,80},{1... | collective-permute-start | bytes 344072 | tf_op jit(solution)/shard_map/ppermute | solution.py:40
  (14 other events, 82.5 us)

commit v5 on v4

--- a/solution.py
+++ b/solution.py
@@ -19,7 +19,6 @@
 LANES = 128
 
 EPSILON = 1e-06
-HIGHEST = lax.Precision.HIGHEST
 F32 = jnp.float32
 BF16 = jnp.bfloat16
 NT = (((1,), (1,)), ((), ()))
@@ -57,10 +56,6 @@
     return lax.dot_general(a, b, dims, preferred_element_type=F32)
 
 
-def full_dot(a, b, dims):
-    return lax.dot_general(a, b, dims, precision=HIGHEST, preferred_element_type=F32)
-
-
 def split2(x):
     high = x.astype(BF16)
     return high, (x - high.astype(F32)).astype(BF16)
@@ -71,6 +66,13 @@
     rest = x - high.astype(F32)
     middle = rest.astype(BF16)
     return high, middle, (rest - middle.astype(F32)).astype(BF16)
+
+
+def mixed(matrix, values):
+    high, middle, low = split3(matrix)
+    left = jnp.concatenate([low, middle, high, middle, high, high], axis=1)
+    high, middle, low = split3(values)
+    return dot(left, jnp.concatenate([high, middle, low, high, middle, high], axis=0), NN)
 
 
 def diagonal(width=LANES, offset=0):
@@ -145,66 +147,68 @@
 Z_AT, CORE_AT = 0, 4
 
 
-def own_places():
-    def kernel(out_ref):
+def left_product_first(right, cross):
+    chunk = QUARTER // 2
+    chunks = ROWS // chunk
+    ahead = 3
+
+    def kernel(right_hbm, cross_hbm, *refs):
+        *outs, kept_ref, places_ref, right_ref, right_sem, sems = refs
         z = lax.rem(lax.axis_index("var"), 4)
         core = lax.rem(lax.axis_index("vox"), 2)
-        out_ref[Z_AT] = z
-        for at, mask in enumerate(MASKS):
-            out_ref[Z_AT + 1 + at] = lax.bitwise_xor(z, jnp.int32(mask))
-        out_ref[CORE_AT] = core
-        out_ref[CORE_AT + 1] = 1 - core
-        out_ref[6] = 0
-        out_ref[7] = 0
-
-    return pl.pallas_call(
-        kernel,
-        out_specs=pl.BlockSpec(memory_space=pltpu.SMEM),
-        out_shape=jax.ShapeDtypeStruct((8,), jnp.int32),
-        compiler_params=PARAMS,
-        name="own_places",
-    )()
-
-
-def left_product_first(right, cross, places):
-    def kernel(places_ref, right_ref, cross_ref, *refs):
-        *outs, kept_ref, both_ref = refs
-        step = pl.program_id(0)
-
-        @pl.when(step == 0)
-        def _():
-            both_ref[...] = jnp.concatenate(split2(right_ref[...]), axis=0)
-
-        block = cross_ref[...]
-        kept_ref[...] = block
-        product = left_terms_of(both_ref, block)
-        for at in range(4):
-
-            @pl.when(step == at)
-            def _():
-                outs[at][...] = product
-
-    quarter = pl.BlockSpec((QUARTER, COLS), lambda i, p: (p[Z_AT + i], 0))
-    return pl.pallas_call(
-        kernel,
-        grid_spec=pltpu.PrefetchScalarGridSpec(
-            num_scalar_prefetch=1,
-            grid=(4,),
-            in_specs=[pl.BlockSpec((K, COLS), lambda i, p: (0, 0)), quarter],
-            out_specs=[pl.BlockSpec((K, QUARTER), lambda i, p: (0, 0))] * 4 + [quarter],
-            scratch_shapes=[pltpu.VMEM((2 * K, COLS), BF16)],
-        ),
+        places = [z] + [lax.bitwise_xor(z, jnp.int32(mask)) for mask in MASKS]
+
+        def rows_of(at):
+            first = places[at // 2] * QUARTER + (at % 2) * chunk
+            return pl.ds(pl.multiple_of(first, chunk), chunk)
+
+        def copy_of(at):
+            return pltpu.make_async_copy(
+                cross_hbm.at[rows_of(at), :], kept_ref.at[rows_of(at), :], sems.at[at]
+            )
+
+        right_copy = pltpu.make_async_copy(right_hbm, right_ref, right_sem)
+        right_copy.start()
+        for at in range(ahead):
+            copy_of(at).start()
+        for at, place in enumerate(places):
+            places_ref[Z_AT + at] = place
+        places_ref[CORE_AT] = core
+        places_ref[CORE_AT + 1] = 1 - core
+        places_ref[6] = 0
+        places_ref[7] = 0
+        right_copy.wait()
+        both = jnp.concatenate(split2(right_ref[...]), axis=0)
+        for quarter in range(4):
+            for at in (2 * quarter, 2 * quarter + 1):
+                copy_of(at).wait()
+                if at + ahead < chunks:
+                    copy_of(at + ahead).start()
+            rows = pl.ds(pl.multiple_of(places[quarter] * QUARTER, QUARTER), QUARTER)
+            outs[quarter][...] = left_terms_of(both, kept_ref[rows, :])
+
+    vmem = pl.BlockSpec(memory_space=pltpu.VMEM)
+    hbm = pl.BlockSpec(memory_space=pltpu.HBM)
+    return pl.pallas_call(
+        kernel,
+        in_specs=[hbm, hbm],
+        out_specs=[vmem] * 5 + [pl.BlockSpec(memory_space=pltpu.SMEM)],
         out_shape=[jax.ShapeDtypeStruct((K, QUARTER), F32)] * 4
-        + [jax.ShapeDtypeStruct((ROWS, COLS), F32)],
+        + [jax.ShapeDtypeStruct((ROWS, COLS), F32), jax.ShapeDtypeStruct((8,), jnp.int32)],
+        scratch_shapes=[
+            pltpu.VMEM((K, COLS), F32),
+            pltpu.SemaphoreType.DMA,
+            pltpu.SemaphoreType.DMA((chunks,)),
+        ],
         compiler_params=FIRST_PARAMS,
         name="left_product_first",
-    )(places, right, cross)
-
-
-def left_terms_of(both_ref, block):
+    )(right, cross)
+
+
+def left_terms_of(both, block):
     high, low = split2(block)
-    whole = dot(both_ref[...], high, NT)
-    return whole[:K] + (whole[K:] + dot(both_ref[:K], low, NT))
+    whole = dot(both, high, NT)
+    return whole[:K] + (whole[K:] + dot(both[:K], low, NT))
 
 
 def left_partners(right_sum, squares, levels, cross, places):
@@ -218,7 +222,7 @@
             both_ref[...] = jnp.concatenate(split2(values), axis=0)
             gram_ref[...] = padded(cross_gram(values, values))
 
-        product = left_terms_of(both_ref, cross_ref[...])
+        product = left_terms_of(both_ref[...], cross_ref[...])
         for at in range(3):
 
             @pl.when(step == at)
@@ -245,7 +249,7 @@
 
 def left_own(both, gram, cross, places):
     def kernel(places_ref, both_ref, gram_ref, cross_ref, out_ref):
-        out_ref[:, :QUARTER] = left_terms_of(both_ref, cross_ref[...])
+        out_ref[:, :QUARTER] = left_terms_of(both_ref[...], cross_ref[...])
         out_ref[:, QUARTER:] = gram_ref[...]
 
     whole = lambda shape: pl.BlockSpec(shape, lambda i, p: (0,) * len(shape))
@@ -330,7 +334,7 @@
         for at, block in enumerate(ins):
             values = block[...]
             if inverse is not None:
-                values = full_dot(inverse_ref[:, :K], values, NN)
+                values = mixed(inverse_ref[:, :K], values)
             out_ref[:, pl.ds(pl.multiple_of(places_ref[start + at] * width, width), width)] = values
             total = total + jnp.sum(values * values, axis=1, keepdims=True)
         squares_ref[...] = jnp.broadcast_to(to_row(total)[None], (copies, 1, LANES))
@@ -372,7 +376,7 @@
 
 def mix_left(inverse, shrunk):
     def kernel(inverse_ref, shrunk_ref, out_ref, terms_ref):
-        left = full_dot(inverse_ref[:, :K], shrunk_ref[...], NN)
+        left = mixed(inverse_ref[:, :K], shrunk_ref[...])
         out_ref[...] = left
         high, middle, low = split3(left)
         terms_ref[...] = jnp.concatenate([high, high, middle, high, middle, low], axis=0).T
@@ -397,7 +401,7 @@
             packed = jnp.sum(last_ref[...], axis=0)
             last = jnp.concatenate([packed[:, : 2 * K], packed[:, 2 * K :]], axis=0)
             inverse = inverse_factor(last[:, :K], NG)
-            right = full_dot(inverse, shrunk_ref[...], NN)
+            right = mixed(inverse, shrunk_ref[...])
             right_ref[...] = right
             strength = jnp.sum(inverse * last[:, K:], axis=1, keepdims=True) / math.sqrt(NV * NG)
             strength_ref[...] = to_row(strength)[:, :K]
@@ -433,10 +437,9 @@
 
 
 def per_device(cross, start, levels):
-    places = own_places()
     for sweep in range(ITERS):
         if sweep == 0:
-            *parts, cross = left_product_first(start, cross, places)
+            *parts, cross, places = left_product_first(start, cross)
             got = [swap(parts[at + 1], "var", Z_RINGS, mask) for at, mask in enumerate(MASKS)]
             total = parts[0]
         else:

time: 159 us -> 157 us (0.987)
  Pallas kernels: 38.5 us -> 36 us
    pallas_call x2 -> x1, Pallas kernels: 8.74 us -> 7.11 us  [left_product_first(): pl.pallas_call(kernel, in_specs=[hbm, hbm], out_specs=[vmem] * 5 + [pl.Bl...]
where the time goes in v5:
time: 157 us
  waiting for transfers between devices  44.4 us (28%)
  starting transfers between devices  40.5 us (26%)
  Pallas kernels  36 us (23%)
  blocking collectives  33.7 us (21%)
    ppermute x36, waiting for transfers between devices, swap(): return lax.ppermute(value, axis, pairs)  44.4 us
    ppermute x36, starting transfers between devices, swap(): return lax.ppermute(value, axis, pairs)  40.5 us
    all_to_all x3, blocking collectives, from_all(): return lax.all_to_all(value, 'var', 0, 0)  33.7 us
    pallas_call x4, Pallas kernels, right_half(): pl.pallas_call(kernel, grid_spec=pltpu.PrefetchScalarGridSpec(num_scalar_...  8.48 us
    pallas_call x1, Pallas kernels, left_product_first(): pl.pallas_call(kernel, in_specs=[hbm, hbm], out_specs=[vmem] * 5 + [pl.Bl...  7.11 us
    pallas_call x1, Pallas kernels, deflate(): pl.pallas_call(kernel, grid=(ROWS // BLOCK,), in_specs=[whole((16, K // 2...  7 us
    pallas_call x1, Pallas kernels, left_partners(): pl.pallas_call(kernel, grid_spec=pltpu.PrefetchScalarGridSpec(num_scalar_...  4.25 us
    pallas_call x4, Pallas kernels, assemble(): pl.pallas_call(kernel, in_specs=[pl.BlockSpec(memory_space=pltpu.SMEM)] +...  3.36 us
  transfers between devices with their start and end apart: 36, of which 25 were waited for; matrix products, arithmetic and copies ran while one was open for 0% of the time, Pallas kernels for 6%

profile of v5, /device:TPU:0, one launch (start us, length us, event | category | flops | bytes accessed | tf_op | source)
XLA Modules:
  0.0 156.6 jit_solution(16716773602356863562)
XLA Ops:
  1.6 7.1 %left_product_first.1 = (f32[32,512]{1,0:T(8,128)S(1)}, f32[32,512]{1,0:T(8,128)S(1)}, f32[32,512]{1,0:T(8,128)S(1)}, f32[32,512]{1,0:T(8,128)S(1)}, f32[2048,1536]{1,0:T(8,128)S(1)}, /*index=5*/s32[8]{0:T(128)S(1)}) custom-call(f32[32,1536]{1,0:T(8,128)S(1)} %copy-done, f32[2048,1536]{1,0:T(8,128)} %cross_hbm.1), custom_call_target="tpu_custom_call" | custom-call | tf_op jit(solution)/shard_map/left_product_first/pallas_call | solution.py:192
  8.7 2.1 %collective-permute-start = (f32[32,512]{1,0:T(8,128)S(1)}, f32[32,512]{1,0:T(8,128)S(1)}, u32[]{:S(2)}, u32[]{:S(2)}) collective-permute-start(f32[32,512]{1,0:T(8,128)S(1)} %get-tuple-element.41), channel_id=1, source_target_pairs={{0,1},{1,0},{2,3},{3,2},{4,5},{5,4},{6,7},{7,6},{8,9},{9,8},{10,11... | collective-permute-start | bytes 196616 | tf_op jit(solution)/shard_map/ppermute | solution.py:39
  10.8 2.5 %collective-permute-start.1 = (f32[32,512]{1,0:T(8,128)S(1)}, f32[32,512]{1,0:T(8,128)S(1)}, u32[]{:S(2)}, u32[]{:S(2)}) collective-permute-start(f32[32,512]{1,0:T(8,128)S(1)} %get-tuple-element.42), channel_id=1, source_target_pairs={{0,3},{1,2},{2,1},{3,0},{4,7},{5,6},{6,5},{7,4},{8,11},{9,10},{10,... | collective-permute-start | bytes 196616 | tf_op jit(solution)/shard_map/ppermute | solution.py:39
  16.2 2.8 %collective-permute-done.2 = f32[32,512]{1,0:T(8,128)S(1)} collective-permute-done((f32[32,512]{1,0:T(8,128)S(1)}, f32[32,512]{1,0:T(8,128)S(1)}, u32[]{:S(2)}, u32[]{:S(2)}) %collective-permute-start.2) | collective-permute-done | bytes 65568 | tf_op jit(solution)/shard_map/ppermute | solution.py:39
  19.1 3.3 %collective-permute-start.5 = (f32[32,512]{1,0:T(8,128)S(1)}, f32[32,512]{1,0:T(8,128)S(1)}, u32[]{:S(2)}, u32[]{:S(2)}) collective-permute-start(f32[32,512]{1,0:T(8,128)S(1)} %add_add_fusion.5), channel_id=1, source_target_pairs={{0,8},{4,12},{8,0},{12,4},{1,9},{5,13},{9,1},{13,5},{2,10},{6,14},... | collective-permute-start | bytes 196616 | tf_op jit(solution)/shard_map/ppermute | solution.py:39
  25.0 2.8 %collective-permute-done.4 = f32[32,512]{1,0:T(8,128)S(1)} collective-permute-done((f32[32,512]{1,0:T(8,128)S(1)}, f32[32,512]{1,0:T(8,128)S(1)}, u32[]{:S(2)}, u32[]{:S(2)}) %collective-permute-start.4) | collective-permute-done | bytes 65568 | tf_op jit(solution)/shard_map/ppermute | solution.py:39
  29.0 2.6 %collective-permute-start.7 = (f32[32,512]{1,0:T(8,128)S(1)}, f32[32,512]{1,0:T(8,128)S(1)}, u32[]{:S(2)}, u32[]{:S(2)}) collective-permute-start(f32[32,512]{1,0:T(8,128)S(1)} %add_add_fusion.4.refs_0_), channel_id=1, source_target_pairs={{0,3},{1,2},{2,1},{3,0},{4,7},{5,6},{6,5},{7,4},{8,11},{9,10},{10,... | collective-permute-start | bytes 196616 | tf_op jit(solution)/shard_map/ppermute | solution.py:39
  37.7 3.0 %collective-permute-start.12 = (f32[1,1,128]{2,1,0:T(1,128)S(1)}, f32[1,1,128]{2,1,0:T(1,128)S(1)}, u32[]{:S(2)}, u32[]{:S(2)}) collective-permute-start(f32[1,1,128]{2,1,0:T(1,128)S(1)} %add.90), channel_id=1, source_target_pairs={{0,64},{32,96},{64,0},{96,32},{16,80},{48,112},{80,16},{112,48},{1... | collective-permute-start | bytes 1544 | tf_op jit(solution)/shard_map/ppermute | solution.py:39
  42.8 2.7 %collective-permute-done.11 = f32[1,1,128]{2,1,0:T(1,128)S(1)} collective-permute-done((f32[1,1,128]{2,1,0:T(1,128)S(1)}, f32[1,1,128]{2,1,0:T(1,128)S(1)}, u32[]{:S(2)}, u32[]{:S(2)}) %collective-permute-start.11) | collective-permute-done | bytes 544 | tf_op jit(solution)/shard_map/ppermute | solution.py:39
  45.5 2.3 %right_half_head.2 = (f32[32,896]{1,0:T(8,128)S(1)}, bf16[64,2048]{1,0:T(8,128)(2,1)S(1)}, f32[32,128]{1,0:T(8,128)S(1)}, f32[32,2048]{1,0:T(8,128)}) custom-call(s32[8]{0:T(128)S(1)} %get-tuple-element.39.places_ref, f32[32,2048]{1,0:T(8,128)S(1)} %get-tuple-element.44.refs_0_, f32[1,1,128]{2,1,0:T(1,128)S(1)} %add_add_fusion.7.refs_1_, ...), custom_call_target="tpu_custom_call" | custom-call | flops 1200000000 | bytes 8000000 | tf_op jit(solution)/shard_map/right_half_head/pallas_call | solution.py:296
  53.5 4.0 %collective-permute-done.16 = f32[32,896]{1,0:T(8,128)S(1)} collective-permute-done((f32[32,896]{1,0:T(8,128)S(1)}, f32[32,896]{1,0:T(8,128)S(1)}, u32[]{:S(2)}, u32[]{:S(2)}) %collective-permute-start.16) | collective-permute-done | bytes 114720 | tf_op jit(solution)/shard_map/ppermute | solution.py:39
  57.5 2.2 %collective-permute-done.15 = f32[32,896]{1,0:T(8,128)S(1)} collective-permute-done((f32[32,896]{1,0:T(8,128)S(1)}, f32[32,896]{1,0:T(8,128)S(1)}, u32[]{:S(2)}, u32[]{:S(2)}) %collective-permute-start.15) | collective-permute-done | bytes 114720 | tf_op jit(solution)/shard_map/ppermute | solution.py:39
  62.0 11.4 %all_to_all.15.squares_ref = f32[16,1,128]{2,1,0:T(1,128)S(1)} all-to-all(f32[16,1,128]{2,1,0:T(1,128)S(1)} %get-tuple-element.51), channel_id=1, replica_groups=mesh['vox'=8,'var'=16] {'var'}, dimensions={0} | all-to-all | bytes 16384 | tf_op jit(solution)/shard_map/all_to_all | solution.py:48
  73.4 4.3 %left_partners.1 = (f32[32,640]{1,0:T(8,128)S(1)}, f32[32,640]{1,0:T(8,128)S(1)}, f32[32,640]{1,0:T(8,128)S(1)}, bf16[64,1536]{1,0:T(8,128)(2,1)S(1)}, f32[32,128]{1,0:T(8,128)S(1)}) custom-call(s32[8]{0:T(128)S(1)} %get-tuple-element.39.places_ref, f32[32,1536]{1,0:T(8,128)S(1)} %get-tuple-element.50.right_ref, f32[16,1,128]{2,1,0:T(1,128)S(1)} %all_to_all.15.squares_ref, ...), custom_call_target="tpu_custom_call" | custom-call | tf_op jit(solution)/shard_map/left_partners/pallas_call | solution.py:235
  79.5 2.3 %collective-permute-start.20 = (f32[32,640]{1,0:T(8,128)S(1)}, f32[32,640]{1,0:T(8,128)S(1)}, u32[]{:S(2)}, u32[]{:S(2)}) collective-permute-start(f32[32,640]{1,0:T(8,128)S(1)} %get-tuple-element.56), channel_id=1, source_target_pairs={{0,2},{1,3},{2,0},{3,1},{4,6},{5,7},{6,4},{7,5},{8,10},{9,11},{10,... | collective-permute-start | bytes 245768 | tf_op jit(solution)/shard_map/ppermute | solution.py:39
  89.1 2.5 %collective-permute-done.23 = f32[32,640]{1,0:T(8,128)S(1)} collective-permute-done((f32[32,640]{1,0:T(8,128)S(1)}, f32[32,640]{1,0:T(8,128)S(1)}, u32[]{:S(2)}, u32[]{:S(2)}) %collective-permute-start.23) | collective-permute-done | bytes 81952 | tf_op jit(solution)/shard_map/ppermute | solution.py:39
  93.3 2.4 %collective-permute-start.26 = (f32[32,512]{1,0:T(8,128)S(1)}, f32[32,512]{1,0:T(8,128)S(1)}, u32[]{:S(2)}, u32[]{:S(2)}) collective-permute-start(f32[32,512]{1,0:T(8,128)S(1)} %slice.27.refs_1_), channel_id=1, source_target_pairs={{0,2},{1,3},{2,0},{3,1},{4,6},{5,7},{6,4},{7,5},{8,10},{9,11},{10,... | collective-permute-start | bytes 196616 | tf_op jit(solution)/shard_map/ppermute | solution.py:39
  109.6 2.3 %right_half_head.3 = (f32[32,896]{1,0:T(8,128)S(1)}, bf16[64,2048]{1,0:T(8,128)(2,1)S(1)}, f32[32,128]{1,0:T(8,128)S(1)}, f32[32,2048]{1,0:T(8,128)S(1)}) custom-call(s32[8]{0:T(128)S(1)} %get-tuple-element.39.places_ref, f32[32,2048]{1,0:T(8,128)S(1)} %get-tuple-element.57.refs_0_, f32[1,1,128]{2,1,0:T(1,128)S(1)} %add_add_fusion.6.refs_1_, ...), custom_call_target="tpu_custom_call" | custom-call | flops 1200000000 | bytes 8000000 | tf_op jit(solution)/shard_map/right_half_head/pallas_call | solution.py:296
  113.9 2.3 %collective-permute-start.34 = (f32[32,896]{1,0:T(8,128)S(1)}, f32[32,896]{1,0:T(8,128)S(1)}, u32[]{:S(2)}, u32[]{:S(2)}) collective-permute-start(f32[32,896]{1,0:T(8,128)S(1)} %add.108), channel_id=1, source_target_pairs={{0,64},{32,96},{64,0},{96,32},{16,80},{48,112},{80,16},{112,48},{1... | collective-permute-start | bytes 344072 | tf_op jit(solution)/shard_map/ppermute | solution.py:39
  117.5 3.9 %collective-permute-done.34 = f32[32,896]{1,0:T(8,128)S(1)} collective-permute-done((f32[32,896]{1,0:T(8,128)S(1)}, f32[32,896]{1,0:T(8,128)S(1)}, u32[]{:S(2)}, u32[]{:S(2)}) %collective-permute-start.34) | collective-permute-done | bytes 114720 | tf_op jit(solution)/shard_map/ppermute | solution.py:39
  121.3 2.4 %collective-permute-done.33 = f32[32,896]{1,0:T(8,128)S(1)} collective-permute-done((f32[32,896]{1,0:T(8,128)S(1)}, f32[32,896]{1,0:T(8,128)S(1)}, u32[]{:S(2)}, u32[]{:S(2)}) %collective-permute-start.33) | collective-permute-done | bytes 114720 | tf_op jit(solution)/shard_map/ppermute | solution.py:39
  126.7 11.4 %all_to_all.16.squares_ref = f32[16,1,128]{2,1,0:T(1,128)S(1)} all-to-all(f32[16,1,128]{2,1,0:T(1,128)S(1)} %get-tuple-element.66), channel_id=1, replica_groups=mesh['vox'=8,'var'=16] {'var'}, dimensions={0} | all-to-all | bytes 16384 | tf_op jit(solution)/shard_map/all_to_all | solution.py:48
  138.8 10.8 %all_to_all.17.last_ref = f32[16,16,128]{2,1,0:T(8,128)S(1)} all-to-all(f32[16,16,128]{2,1,0:T(8,128)S(1)} %get-tuple-element.67), channel_id=1, replica_groups=mesh['vox'=8,'var'=16] {'var'}, dimensions={0} | all-to-all | bytes 262144 | tf_op jit(solution)/shard_map/all_to_all | solution.py:48
  149.6 7.0 %deflate.1 = (f32[2048,1536]{1,0:T(8,128)}, f32[32,1536]{1,0:T(8,128)}, f32[1,32]{1,0:T(1,128)}) custom-call(f32[16,16,128]{2,1,0:T(8,128)S(1)} %all_to_all.17.last_ref, f32[32,1536]{1,0:T(8,128)S(1)} %get-tuple-element.68.shrunk_ref, bf16[2048,192]{1,0:T(8,128)(2,1)S(1)} %get-tuple-element.69.left_ref, ...), custom_call_target="tpu_custom_call" | custom-call | tf_op jit(solution)/shard_map/deflate/pallas_call | solution.py:414
  (90 shorter events, 55.2 us)
Async XLA Ops:
  8.7 5.7 %collective-permute-start = (f32[32,512]{1,0:T(8,128)S(1)}, f32[32,512]{1,0:T(8,128)S(1)}, u32[]{:S(2)}, u32[]{:S(2)}) collective-permute-start(f32[32,512]{1,0:T(8,128)S(1)} %get-tuple-element.41), channel_id=1, source_target_pairs={{0,1},{1,0},{2,3},{3,2},{4,5},{5,4},{6,7},{7,6},{8,9},{9,8},{10,11... | collective-permute-start | bytes 196616 | tf_op jit(solution)/shard_map/ppermute | solution.py:39
  10.8 5.5 %collective-permute-start.1 = (f32[32,512]{1,0:T(8,128)S(1)}, f32[32,512]{1,0:T(8,128)S(1)}, u32[]{:S(2)}, u32[]{:S(2)}) collective-permute-start(f32[32,512]{1,0:T(8,128)S(1)} %get-tuple-element.42), channel_id=1, source_target_pairs={{0,3},{1,2},{2,1},{3,0},{4,7},{5,6},{6,5},{7,4},{8,11},{9,10},{10,... | collective-permute-start | bytes 196616 | tf_op jit(solution)/shard_map/ppermute | solution.py:39
  13.3 5.8 %collective-permute-start.2 = (f32[32,512]{1,0:T(8,128)S(1)}, f32[32,512]{1,0:T(8,128)S(1)}, u32[]{:S(2)}, u32[]{:S(2)}) collective-permute-start(f32[32,512]{1,0:T(8,128)S(1)} %get-tuple-element.43), channel_id=1, source_target_pairs={{0,2},{1,3},{2,0},{3,1},{4,6},{5,7},{6,4},{7,5},{8,10},{9,11},{10,... | collective-permute-start | bytes 196616 | tf_op jit(solution)/shard_map/ppermute | solution.py:39
  19.1 6.0 %collective-permute-start.5 = (f32[32,512]{1,0:T(8,128)S(1)}, f32[32,512]{1,0:T(8,128)S(1)}, u32[]{:S(2)}, u32[]{:S(2)}) collective-permute-start(f32[32,512]{1,0:T(8,128)S(1)} %add_add_fusion.5), channel_id=1, source_target_pairs={{0,8},{4,12},{8,0},{12,4},{1,9},{5,13},{9,1},{13,5},{2,10},{6,14},... | collective-permute-start | bytes 196616 | tf_op jit(solution)/shard_map/ppermute | solution.py:39
  22.4 5.5 %collective-permute-start.4 = (f32[32,512]{1,0:T(8,128)S(1)}, f32[32,512]{1,0:T(8,128)S(1)}, u32[]{:S(2)}, u32[]{:S(2)}) collective-permute-start(f32[32,512]{1,0:T(8,128)S(1)} %add_add_fusion.5), channel_id=1, source_target_pairs={{0,12},{4,8},{8,4},{12,0},{1,13},{5,9},{9,5},{13,1},{2,14},{6,10},... | collective-permute-start | bytes 196616 | tf_op jit(solution)/shard_map/ppermute | solution.py:39
  27.9 5.8 %collective-permute-start.8 = (f32[32,512]{1,0:T(8,128)S(1)}, f32[32,512]{1,0:T(8,128)S(1)}, u32[]{:S(2)}, u32[]{:S(2)}) collective-permute-start(f32[32,512]{1,0:T(8,128)S(1)} %add_add_fusion.4.refs_0_), channel_id=1, source_target_pairs={{0,2},{1,3},{2,0},{3,1},{4,6},{5,7},{6,4},{7,5},{8,10},{9,11},{10,... | collective-permute-start | bytes 196616 | tf_op jit(solution)/shard_map/ppermute | solution.py:39
  29.0 5.5 %collective-permute-start.7 = (f32[32,512]{1,0:T(8,128)S(1)}, f32[32,512]{1,0:T(8,128)S(1)}, u32[]{:S(2)}, u32[]{:S(2)}) collective-permute-start(f32[32,512]{1,0:T(8,128)S(1)} %add_add_fusion.4.refs_0_), channel_id=1, source_target_pairs={{0,3},{1,2},{2,1},{3,0},{4,7},{5,6},{6,5},{7,4},{8,11},{9,10},{10,... | collective-permute-start | bytes 196616 | tf_op jit(solution)/shard_map/ppermute | solution.py:39
  37.7 5.0 %collective-permute-start.12 = (f32[1,1,128]{2,1,0:T(1,128)S(1)}, f32[1,1,128]{2,1,0:T(1,128)S(1)}, u32[]{:S(2)}, u32[]{:S(2)}) collective-permute-start(f32[1,1,128]{2,1,0:T(1,128)S(1)} %add.90), channel_id=1, source_target_pairs={{0,64},{32,96},{64,0},{96,32},{16,80},{48,112},{80,16},{112,48},{1... | collective-permute-start | bytes 1544 | tf_op jit(solution)/shard_map/ppermute | solution.py:39
  40.8 4.8 %collective-permute-start.11 = (f32[1,1,128]{2,1,0:T(1,128)S(1)}, f32[1,1,128]{2,1,0:T(1,128)S(1)}, u32[]{:S(2)}, u32[]{:S(2)}) collective-permute-start(f32[1,1,128]{2,1,0:T(1,128)S(1)} %add.90), channel_id=1, source_target_pairs={{0,96},{32,64},{64,32},{96,0},{16,112},{48,80},{80,48},{112,16},{1... | collective-permute-start | bytes 1544 | tf_op jit(solution)/shard_map/ppermute | solution.py:39
  49.9 7.6 %collective-permute-start.16 = (f32[32,896]{1,0:T(8,128)S(1)}, f32[32,896]{1,0:T(8,128)S(1)}, u32[]{:S(2)}, u32[]{:S(2)}) collective-permute-start(f32[32,896]{1,0:T(8,128)S(1)} %add.94), channel_id=1, source_target_pairs={{0,64},{32,96},{64,0},{96,32},{16,80},{48,112},{80,16},{112,48},{1... | collective-permute-start | bytes 344072 | tf_op jit(solution)/shard_map/ppermute | solution.py:39
  51.4 8.3 %collective-permute-start.15 = (f32[32,896]{1,0:T(8,128)S(1)}, f32[32,896]{1,0:T(8,128)S(1)}, u32[]{:S(2)}, u32[]{:S(2)}) collective-permute-start(f32[32,896]{1,0:T(8,128)S(1)} %add.94), channel_id=1, source_target_pairs={{0,96},{32,64},{64,32},{96,0},{16,112},{48,80},{80,48},{112,16},{1... | collective-permute-start | bytes 344072 | tf_op jit(solution)/shard_map/ppermute | solution.py:39
  52.6 7.1 %collective-permute-start.14 = (f32[32,896]{1,0:T(8,128)S(1)}, f32[32,896]{1,0:T(8,128)S(1)}, u32[]{:S(2)}, u32[]{:S(2)}) collective-permute-start(f32[32,896]{1,0:T(8,128)S(1)} %add.94), channel_id=1, source_target_pairs={{0,32},{32,0},{64,96},{96,64},{16,48},{48,16},{80,112},{112,80},{1... | collective-permute-start | bytes 344072 | tf_op jit(solution)/shard_map/ppermute | solution.py:39
  77.7 5.8 %collective-permute-start.18 = (f32[32,640]{1,0:T(8,128)S(1)}, f32[32,640]{1,0:T(8,128)S(1)}, u32[]{:S(2)}, u32[]{:S(2)}) collective-permute-start(f32[32,640]{1,0:T(8,128)S(1)} %get-tuple-element.54), channel_id=1, source_target_pairs={{0,1},{1,0},{2,3},{3,2},{4,5},{5,4},{6,7},{7,6},{8,9},{9,8},{10,11... | collective-permute-start | bytes 245768 | tf_op jit(solution)/shard_map/ppermute | solution.py:39
  78.3 5.8 %collective-permute-start.19 = (f32[32,640]{1,0:T(8,128)S(1)}, f32[32,640]{1,0:T(8,128)S(1)}, u32[]{:S(2)}, u32[]{:S(2)}) collective-permute-start(f32[32,640]{1,0:T(8,128)S(1)} %get-tuple-element.55), channel_id=1, source_target_pairs={{0,3},{1,2},{2,1},{3,0},{4,7},{5,6},{6,5},{7,4},{8,11},{9,10},{10,... | collective-permute-start | bytes 245768 | tf_op jit(solution)/shard_map/ppermute | solution.py:39
  79.5 5.9 %collective-permute-start.20 = (f32[32,640]{1,0:T(8,128)S(1)}, f32[32,640]{1,0:T(8,128)S(1)}, u32[]{:S(2)}, u32[]{:S(2)}) collective-permute-start(f32[32,640]{1,0:T(8,128)S(1)} %get-tuple-element.56), channel_id=1, source_target_pairs={{0,2},{1,3},{2,0},{3,1},{4,6},{5,7},{6,4},{7,5},{8,10},{9,11},{10,... | collective-permute-start | bytes 245768 | tf_op jit(solution)/shard_map/ppermute | solution.py:39
  85.5 6.0 %collective-permute-start.23 = (f32[32,640]{1,0:T(8,128)S(1)}, f32[32,640]{1,0:T(8,128)S(1)}, u32[]{:S(2)}, u32[]{:S(2)}) collective-permute-start(f32[32,640]{1,0:T(8,128)S(1)} %add_add_fusion.3), channel_id=1, source_target_pairs={{0,8},{4,12},{8,0},{12,4},{1,9},{5,13},{9,1},{13,5},{2,10},{6,14},... | collective-permute-start | bytes 245768 | tf_op jit(solution)/shard_map/ppermute | solution.py:39
  86.8 5.7 %collective-permute-start.22 = (f32[32,640]{1,0:T(8,128)S(1)}, f32[32,640]{1,0:T(8,128)S(1)}, u32[]{:S(2)}, u32[]{:S(2)}) collective-permute-start(f32[32,640]{1,0:T(8,128)S(1)} %add_add_fusion.3), channel_id=1, source_target_pairs={{0,12},{4,8},{8,4},{12,0},{1,13},{5,9},{9,5},{13,1},{2,14},{6,10},... | collective-permute-start | bytes 245768 | tf_op jit(solution)/shard_map/ppermute | solution.py:39
  93.3 5.8 %collective-permute-start.26 = (f32[32,512]{1,0:T(8,128)S(1)}, f32[32,512]{1,0:T(8,128)S(1)}, u32[]{:S(2)}, u32[]{:S(2)}) collective-permute-start(f32[32,512]{1,0:T(8,128)S(1)} %slice.27.refs_1_), channel_id=1, source_target_pairs={{0,2},{1,3},{2,0},{3,1},{4,6},{5,7},{6,4},{7,5},{8,10},{9,11},{10,... | collective-permute-start | bytes 196616 | tf_op jit(solution)/shard_map/ppermute | solution.py:39
  95.7 5.5 %collective-permute-start.25 = (f32[32,512]{1,0:T(8,128)S(1)}, f32[32,512]{1,0:T(8,128)S(1)}, u32[]{:S(2)}, u32[]{:S(2)}) collective-permute-start(f32[32,512]{1,0:T(8,128)S(1)} %slice.27.refs_1_), channel_id=1, source_target_pairs={{0,3},{1,2},{2,1},{3,0},{4,7},{5,6},{6,5},{7,4},{8,11},{9,10},{10,... | collective-permute-start | bytes 196616 | tf_op jit(solution)/shard_map/ppermute | solution.py:39
  103.3 5.0 %collective-permute-start.30 = (f32[1,1,128]{2,1,0:T(1,128)S(1)}, f32[1,1,128]{2,1,0:T(1,128)S(1)}, u32[]{:S(2)}, u32[]{:S(2)}) collective-permute-start(f32[1,1,128]{2,1,0:T(1,128)S(1)} %add.104), channel_id=1, source_target_pairs={{0,64},{32,96},{64,0},{96,32},{16,80},{48,112},{80,16},{112,48},{1... | collective-permute-start | bytes 1544 | tf_op jit(solution)/shard_map/ppermute | solution.py:39
  104.8 4.8 %collective-permute-start.29 = (f32[1,1,128]{2,1,0:T(1,128)S(1)}, f32[1,1,128]{2,1,0:T(1,128)S(1)}, u32[]{:S(2)}, u32[]{:S(2)}) collective-permute-start(f32[1,1,128]{2,1,0:T(1,128)S(1)} %add.104), channel_id=1, source_target_pairs={{0,96},{32,64},{64,32},{96,0},{16,112},{48,80},{80,48},{112,16},{1... | collective-permute-start | bytes 1544 | tf_op jit(solution)/shard_map/ppermute | solution.py:39
  113.9 7.4 %collective-permute-start.34 = (f32[32,896]{1,0:T(8,128)S(1)}, f32[32,896]{1,0:T(8,128)S(1)}, u32[]{:S(2)}, u32[]{:S(2)}) collective-permute-start(f32[32,896]{1,0:T(8,128)S(1)} %add.108), channel_id=1, source_target_pairs={{0,64},{32,96},{64,0},{96,32},{16,80},{48,112},{80,16},{112,48},{1... | collective-permute-start | bytes 344072 | tf_op jit(solution)/shard_map/ppermute | solution.py:39
  116.2 7.5 %collective-permute-start.33 = (f32[32,896]{1,0:T(8,128)S(1)}, f32[32,896]{1,0:T(8,128)S(1)}, u32[]{:S(2)}, u32[]{:S(2)}) collective-permute-start(f32[32,896]{1,0:T(8,128)S(1)} %add.108), channel_id=1, source_target_pairs={{0,96},{32,64},{64,32},{96,0},{16,112},{48,80},{80,48},{112,16},{1... | collective-permute-start | bytes 344072 | tf_op jit(solution)/shard_map/ppermute | solution.py:39
  117.5 6.2 %collective-permute-start.32 = (f32[32,896]{1,0:T(8,128)S(1)}, f32[32,896]{1,0:T(8,128)S(1)}, u32[]{:S(2)}, u32[]{:S(2)}) collective-permute-start(f32[32,896]{1,0:T(8,128)S(1)} %add.108), channel_id=1, source_target_pairs={{0,32},{32,0},{64,96},{96,64},{16,48},{48,16},{80,112},{112,80},{1... | collective-permute-start | bytes 344072 | tf_op jit(solution)/shard_map/ppermute | solution.py:39
  (14 other events, 79.4 us)

commit v6 on v5

--- a/solution.py
+++ b/solution.py
@@ -17,6 +17,9 @@
 HALF = COLS // 2
 BLOCK = 1024
 LANES = 128
+LEFT_ROWS = K * QUARTER // LANES
+RIGHT_ROWS = K * HALF // LANES
+GRAM_ROWS = K * K // LANES
 
 EPSILON = 1e-06
 F32 = jnp.float32
@@ -100,6 +103,23 @@
     thresholds = levels[side : side + 1, :].astype(F32) / 1024.0
     level = to_column(thresholds * jnp.sqrt(squares[:, :K] / count + EPSILON))
     return values - jnp.clip(values, -level, level)
+
+
+def stack(ref, values):
+    for at in range(values.shape[1] // LANES):
+        ref[at * K : (at + 1) * K, :] = values[:, at * LANES : (at + 1) * LANES]
+
+
+def unstacked(values):
+    return jnp.concatenate([values[at : at + K] for at in range(0, values.shape[0], K)], axis=1)
+
+
+def packed_gram(gram):
+    return jnp.concatenate([gram[at : at + GRAM_ROWS] for at in range(0, K, GRAM_ROWS)], axis=1)
+
+
+def unpacked_gram(packed):
+    return jnp.concatenate([packed[:, at : at + K] for at in range(0, LANES, K)], axis=0)
 
 
 def padded(small):
@@ -150,7 +170,7 @@
 def left_product_first(right, cross):
     chunk = QUARTER // 2
     chunks = ROWS // chunk
-    ahead = 3
+    ahead = 6
 
     def kernel(right_hbm, cross_hbm, *refs):
         *outs, kept_ref, places_ref, right_ref, right_sem, sems = refs
@@ -185,7 +205,7 @@
                 if at + ahead < chunks:
                     copy_of(at + ahead).start()
             rows = pl.ds(pl.multiple_of(places[quarter] * QUARTER, QUARTER), QUARTER)
-            outs[quarter][...] = left_terms_of(both, kept_ref[rows, :])
+            stack(outs[quarter], left_terms_of(both, kept_ref[rows, :]))
 
     vmem = pl.BlockSpec(memory_space=pltpu.VMEM)
     hbm = pl.BlockSpec(memory_space=pltpu.HBM)
@@ -193,7 +213,7 @@
         kernel,
         in_specs=[hbm, hbm],
         out_specs=[vmem] * 5 + [pl.BlockSpec(memory_space=pltpu.SMEM)],
-        out_shape=[jax.ShapeDtypeStruct((K, QUARTER), F32)] * 4
+        out_shape=[jax.ShapeDtypeStruct((LEFT_ROWS, LANES), F32)] * 4
         + [jax.ShapeDtypeStruct((ROWS, COLS), F32), jax.ShapeDtypeStruct((8,), jnp.int32)],
         scratch_shapes=[
             pltpu.VMEM((K, COLS), F32),
@@ -220,18 +240,18 @@
         def _():
             values = shrunk_of(right_ref[...], squares_ref[...], levels_ref[...], 1, NG)
             both_ref[...] = jnp.concatenate(split2(values), axis=0)
-            gram_ref[...] = padded(cross_gram(values, values))
+            gram_ref[...] = packed_gram(cross_gram(values, values))
 
         product = left_terms_of(both_ref[...], cross_ref[...])
         for at in range(3):
 
             @pl.when(step == at)
             def _():
-                outs[at][:, :QUARTER] = product
-                outs[at][:, QUARTER:] = gram_ref[...]
+                stack(outs[at], product)
+                outs[at][LEFT_ROWS:, :] = gram_ref[...]
 
     whole = lambda shape: pl.BlockSpec(shape, lambda i, p: (0,) * len(shape))
-    shapes = [((K, QUARTER + LANES), F32)] * 3 + [((2 * K, COLS), BF16), ((K, LANES), F32)]
+    shapes = [((LEFT_ROWS + GRAM_ROWS, LANES), F32)] * 3 + [((2 * K, COLS), BF16), ((GRAM_ROWS, LANES), F32)]
     return pl.pallas_call(
         kernel,
         grid_spec=pltpu.PrefetchScalarGridSpec(
@@ -249,8 +269,8 @@
 
 def left_own(both, gram, cross, places):
     def kernel(places_ref, both_ref, gram_ref, cross_ref, out_ref):
-        out_ref[:, :QUARTER] = left_terms_of(both_ref[...], cross_ref[...])
-        out_ref[:, QUARTER:] = gram_ref[...]
+        stack(out_ref, left_terms_of(both_ref[...], cross_ref[...]))
+        out_ref[LEFT_ROWS:, :] = gram_ref[...]
 
     whole = lambda shape: pl.BlockSpec(shape, lambda i, p: (0,) * len(shape))
     return pl.pallas_call(
@@ -258,11 +278,11 @@
         grid_spec=pltpu.PrefetchScalarGridSpec(
             num_scalar_prefetch=1,
             grid=(1,),
-            in_specs=[whole((2 * K, COLS)), whole((K, LANES))]
+            in_specs=[whole((2 * K, COLS)), whole((GRAM_ROWS, LANES))]
             + [pl.BlockSpec((QUARTER, COLS), lambda i, p: (p[Z_AT], 0))],
-            out_specs=whole((K, QUARTER + LANES)),
+            out_specs=whole((LEFT_ROWS + GRAM_ROWS, LANES)),
         ),
-        out_shape=jax.ShapeDtypeStruct((K, QUARTER + LANES), F32),
+        out_shape=jax.ShapeDtypeStruct((LEFT_ROWS + GRAM_ROWS, LANES), F32),
         compiler_params=PARAMS,
         cost_estimate=pl.CostEstimate(flops=600_000_000, bytes_accessed=4_000_000, transcendentals=0),
         name="left_own",
@@ -277,20 +297,20 @@
             values = shrunk_of(left_ref[...], squares_ref[...], levels_ref[...], 0, NV)
             shrunk_ref[...] = values
             both_ref[...] = jnp.concatenate(split2(values), axis=0)
-            gram_ref[...] = padded(cross_gram(values, values))
+            gram_ref[...] = packed_gram(cross_gram(values, values))
         else:
             both_ref, gram_ref, cross_ref, out_ref = refs
         high, low = split2(cross_ref[...])
         product = dot(both_ref[...], high, NN)
-        out_ref[:, :HALF] = product[:K] + (product[K:] + dot(both_ref[:K], low, NN))
-        out_ref[:, HALF:] = gram_ref[...]
+        stack(out_ref, product[:K] + (product[K:] + dot(both_ref[:K], low, NN)))
+        out_ref[RIGHT_ROWS:, :] = gram_ref[...]
 
     whole = lambda shape: pl.BlockSpec(shape, lambda i, p: (0,) * len(shape))
-    out_shape = [jax.ShapeDtypeStruct((K, HALF + LANES), F32)]
+    out_shape = [jax.ShapeDtypeStruct((RIGHT_ROWS + GRAM_ROWS, LANES), F32)]
     if head:
         out_shape += [
             jax.ShapeDtypeStruct((2 * K, ROWS), BF16),
-            jax.ShapeDtypeStruct((K, LANES), F32),
+            jax.ShapeDtypeStruct((GRAM_ROWS, LANES), F32),
             jax.ShapeDtypeStruct((K, ROWS), F32),
         ]
     return pl.pallas_call(
@@ -311,7 +331,7 @@
 
 def factor(gram, count):
     def kernel(gram_ref, out_ref):
-        out_ref[...] = padded(inverse_factor(gram_ref[:, :K], count))
+        out_ref[...] = padded(inverse_factor(unpacked_gram(gram_ref[...]), count))
 
     return pl.pallas_call(
         kernel,
@@ -323,7 +343,7 @@
 
 
 def assemble(inverse, blocks, places, start, copies, order):
-    width = blocks[0].shape[1]
+    width = blocks[0].shape[0] * LANES // K
     n = len(blocks)
 
     def kernel(places_ref, *refs):
@@ -332,7 +352,7 @@
         *ins, out_ref, squares_ref = refs
         total = jnp.zeros((K, 1), F32)
         for at, block in enumerate(ins):
-            values = block[...]
+            values = unstacked(block[...])
             if inverse is not None:
                 values = mixed(inverse_ref[:, :K], values)
             out_ref[:, pl.ds(pl.multiple_of(places_ref[start + at] * width, width), width)] = values
@@ -448,9 +468,9 @@
             total = left_own(both, gram, cross, places)
         total = (total + got[0]) + (got[1] + got[2])
         total = ring_sum(total, "var", Y_RINGS)
-        block = total[:, :QUARTER]
+        block = total[:LEFT_ROWS]
         blocks = [block] + [swap(block, "var", Z_RINGS, mask) for mask in MASKS]
-        inverse = factor(total[:, QUARTER:], NG) if sweep else None
+        inverse = factor(total[LEFT_ROWS:], NG) if sweep else None
         left_sum, squares = assemble(inverse, blocks, places, Z_AT, 1, "assemble_left")
         squares = ring_sum(pair_sum(squares), "vox", X_RINGS)
 
@@ -458,9 +478,9 @@
         got = swap(part, "vox", CORE_PAIRS, 1)
         (total,) = right_half(False, (both, gram), cross, places, 0)
         total = ring_sum(total + got, "vox", X_RINGS)
-        block = total[:, :HALF]
+        block = total[:RIGHT_ROWS]
         got = swap(block, "vox", CORE_PAIRS, 1)
-        inverse = factor(total[:, HALF:], NV)
+        inverse = factor(total[RIGHT_ROWS:], NV)
         if sweep == ITERS - 1:
             left_dirs, left_terms = mix_left(inverse, left_shrunk)
             got, left_terms = lax.optimization_barrier((got, left_terms))

time: 157 us -> 155 us (0.987)
  waiting for transfers between devices: 44.4 us -> 42.8 us
    ppermute x36, waiting for transfers between devices: 44.4 us -> 42.8 us  [swap(): return lax.ppermute(value, axis, pairs)]
where the time goes in v6:
time: 155 us
  waiting for transfers between devices  42.8 us (28%)
  starting transfers between devices  40.5 us (26%)
  Pallas kernels  35.8 us (23%)
  blocking collectives  33.7 us (22%)
    ppermute x36, waiting for transfers between devices, swap(): return lax.ppermute(value, axis, pairs)  42.8 us
    ppermute x36, starting transfers between devices, swap(): return lax.ppermute(value, axis, pairs)  40.5 us
    all_to_all x3, blocking collectives, from_all(): return lax.all_to_all(value, 'var', 0, 0)  33.7 us
    pallas_call x4, Pallas kernels, right_half(): pl.pallas_call(kernel, grid_spec=pltpu.PrefetchScalarGridSpec(num_scalar_...  8.44 us
    pallas_call x1, Pallas kernels, deflate(): pl.pallas_call(kernel, grid=(ROWS // BLOCK,), in_specs=[whole((16, K // 2...  7 us
    pallas_call x1, Pallas kernels, left_product_first(): pl.pallas_call(kernel, in_specs=[hbm, hbm], out_specs=[vmem] * 5 + [pl.Bl...  6.43 us
    pallas_call x1, Pallas kernels, left_partners(): pl.pallas_call(kernel, grid_spec=pltpu.PrefetchScalarGridSpec(num_scalar_...  4.37 us
    pallas_call x4, Pallas kernels, assemble(): pl.pallas_call(kernel, in_specs=[pl.BlockSpec(memory_space=pltpu.SMEM)] +...  3.36 us
  transfers between devices with their start and end apart: 36, of which 25 were waited for; matrix products, arithmetic and copies ran while one was open for 0% of the time, Pallas kernels for 6%

profile of v6, /device:TPU:0, one launch (start us, length us, event | category | flops | bytes accessed | tf_op | source)
XLA Modules:
  0.0 154.8 jit_solution(9283630055995776367)
XLA Ops:
  1.6 6.4 %left_product_first.1 = (f32[128,128]{1,0:T(8,128)S(1)}, f32[128,128]{1,0:T(8,128)S(1)}, f32[128,128]{1,0:T(8,128)S(1)}, f32[128,128]{1,0:T(8,128)S(1)}, f32[2048,1536]{1,0:T(8,128)S(1)}, /*index=5*/s32[8]{0:T(128)S(1)}) custom-call(f32[32,1536]{1,0:T(8,128)S(1)} %copy-done, f32[2048,1536]{1,0:T(8,128)} %cross_hbm.1), custom_call_target="tpu_custom_call" | custom-call | tf_op jit(solution)/shard_map/left_product_first/pallas_call | solution.py:212
  8.0 2.1 %collective-permute-start = (f32[128,128]{1,0:T(8,128)S(1)}, f32[128,128]{1,0:T(8,128)S(1)}, u32[]{:S(2)}, u32[]{:S(2)}) collective-permute-start(f32[128,128]{1,0:T(8,128)S(1)} %get-tuple-element.41), channel_id=1, source_target_pairs={{0,1},{1,0},{2,3},{3,2},{4,5},{5,4},{6,7},{7,6},{8,9},{9,8},{10,11... | collective-permute-start | bytes 196616 | tf_op jit(solution)/shard_map/ppermute | solution.py:42
  10.1 2.5 %collective-permute-start.1 = (f32[128,128]{1,0:T(8,128)S(1)}, f32[128,128]{1,0:T(8,128)S(1)}, u32[]{:S(2)}, u32[]{:S(2)}) collective-permute-start(f32[128,128]{1,0:T(8,128)S(1)} %get-tuple-element.42), channel_id=1, source_target_pairs={{0,3},{1,2},{2,1},{3,0},{4,7},{5,6},{6,5},{7,4},{8,11},{9,10},{10,... | collective-permute-start | bytes 196616 | tf_op jit(solution)/shard_map/ppermute | solution.py:42
  15.6 2.8 %collective-permute-done.2 = f32[128,128]{1,0:T(8,128)S(1)} collective-permute-done((f32[128,128]{1,0:T(8,128)S(1)}, f32[128,128]{1,0:T(8,128)S(1)}, u32[]{:S(2)}, u32[]{:S(2)}) %collective-permute-start.2) | collective-permute-done | bytes 65568 | tf_op jit(solution)/shard_map/ppermute | solution.py:42
  18.4 3.3 %collective-permute-start.5 = (f32[128,128]{1,0:T(8,128)S(1)}, f32[128,128]{1,0:T(8,128)S(1)}, u32[]{:S(2)}, u32[]{:S(2)}) collective-permute-start(f32[128,128]{1,0:T(8,128)S(1)} %add_add_fusion.5), channel_id=1, source_target_pairs={{0,8},{4,12},{8,0},{12,4},{1,9},{5,13},{9,1},{13,5},{2,10},{6,14},... | collective-permute-start | bytes 196616 | tf_op jit(solution)/shard_map/ppermute | solution.py:42
  24.3 2.8 %collective-permute-done.4 = f32[128,128]{1,0:T(8,128)S(1)} collective-permute-done((f32[128,128]{1,0:T(8,128)S(1)}, f32[128,128]{1,0:T(8,128)S(1)}, u32[]{:S(2)}, u32[]{:S(2)}) %collective-permute-start.4) | collective-permute-done | bytes 65568 | tf_op jit(solution)/shard_map/ppermute | solution.py:42
  28.3 2.6 %collective-permute-start.7 = (f32[128,128]{1,0:T(8,128)S(1)}, f32[128,128]{1,0:T(8,128)S(1)}, u32[]{:S(2)}, u32[]{:S(2)}) collective-permute-start(f32[128,128]{1,0:T(8,128)S(1)} %add_add_fusion.4.refs_0_), channel_id=1, source_target_pairs={{0,3},{1,2},{2,1},{3,0},{4,7},{5,6},{6,5},{7,4},{8,11},{9,10},{10,... | collective-permute-start | bytes 196616 | tf_op jit(solution)/shard_map/ppermute | solution.py:42
  37.1 3.0 %collective-permute-start.12 = (f32[1,1,128]{2,1,0:T(1,128)S(1)}, f32[1,1,128]{2,1,0:T(1,128)S(1)}, u32[]{:S(2)}, u32[]{:S(2)}) collective-permute-start(f32[1,1,128]{2,1,0:T(1,128)S(1)} %add.90), channel_id=1, source_target_pairs={{0,64},{32,96},{64,0},{96,32},{16,80},{48,112},{80,16},{112,48},{1... | collective-permute-start | bytes 1544 | tf_op jit(solution)/shard_map/ppermute | solution.py:42
  42.1 2.7 %collective-permute-done.11 = f32[1,1,128]{2,1,0:T(1,128)S(1)} collective-permute-done((f32[1,1,128]{2,1,0:T(1,128)S(1)}, f32[1,1,128]{2,1,0:T(1,128)S(1)}, u32[]{:S(2)}, u32[]{:S(2)}) %collective-permute-start.11) | collective-permute-done | bytes 544 | tf_op jit(solution)/shard_map/ppermute | solution.py:42
  44.9 2.3 %right_half_head.2 = (f32[200,128]{1,0:T(8,128)S(1)}, bf16[64,2048]{1,0:T(8,128)(2,1)S(1)}, f32[8,128]{1,0:T(8,128)S(1)}, f32[32,2048]{1,0:T(8,128)}) custom-call(s32[8]{0:T(128)S(1)} %get-tuple-element.39.places_ref, f32[32,2048]{1,0:T(8,128)S(1)} %get-tuple-element.44.refs_0_, f32[1,1,128]{2,1,0:T(1,128)S(1)} %add_add_fusion.7.refs_1_, ...), custom_call_target="tpu_custom_call" | custom-call | flops 1200000000 | bytes 8000000 | tf_op jit(solution)/shard_map/right_half_head/pallas_call | solution.py:316
  52.8 3.6 %collective-permute-done.16 = f32[200,128]{1,0:T(8,128)S(1)} collective-permute-done((f32[200,128]{1,0:T(8,128)S(1)}, f32[200,128]{1,0:T(8,128)S(1)}, u32[]{:S(2)}, u32[]{:S(2)}) %collective-permute-start.16) | collective-permute-done | bytes 102432 | tf_op jit(solution)/shard_map/ppermute | solution.py:42
  56.4 2.1 %collective-permute-done.15 = f32[200,128]{1,0:T(8,128)S(1)} collective-permute-done((f32[200,128]{1,0:T(8,128)S(1)}, f32[200,128]{1,0:T(8,128)S(1)}, u32[]{:S(2)}, u32[]{:S(2)}) %collective-permute-start.15) | collective-permute-done | bytes 102432 | tf_op jit(solution)/shard_map/ppermute | solution.py:42
  60.8 11.4 %all_to_all.15.squares_ref = f32[16,1,128]{2,1,0:T(1,128)S(1)} all-to-all(f32[16,1,128]{2,1,0:T(1,128)S(1)} %get-tuple-element.51), channel_id=1, replica_groups=mesh['vox'=8,'var'=16] {'var'}, dimensions={0} | all-to-all | bytes 16384 | tf_op jit(solution)/shard_map/all_to_all | solution.py:51
  72.2 4.4 %left_partners.1 = (f32[136,128]{1,0:T(8,128)S(1)}, f32[136,128]{1,0:T(8,128)S(1)}, f32[136,128]{1,0:T(8,128)S(1)}, bf16[64,1536]{1,0:T(8,128)(2,1)S(1)}, f32[8,128]{1,0:T(8,128)S(1)}) custom-call(s32[8]{0:T(128)S(1)} %get-tuple-element.39.places_ref, f32[32,1536]{1,0:T(8,128)S(1)} %get-tuple-element.50.right_ref, f32[16,1,128]{2,1,0:T(1,128)S(1)} %all_to_all.15.squares_ref, ...), custom_call_target="tpu_custom_call" | custom-call | tf_op jit(solution)/shard_map/left_partners/pallas_call | solution.py:255
  78.4 2.3 %collective-permute-start.20 = (f32[136,128]{1,0:T(8,128)S(1)}, f32[136,128]{1,0:T(8,128)S(1)}, u32[]{:S(2)}, u32[]{:S(2)}) collective-permute-start(f32[136,128]{1,0:T(8,128)S(1)} %get-tuple-element.56), channel_id=1, source_target_pairs={{0,2},{1,3},{2,0},{3,1},{4,6},{5,7},{6,4},{7,5},{8,10},{9,11},{10,... | collective-permute-start | bytes 208904 | tf_op jit(solution)/shard_map/ppermute | solution.py:42
  87.8 2.3 %collective-permute-done.23 = f32[136,128]{1,0:T(8,128)S(1)} collective-permute-done((f32[136,128]{1,0:T(8,128)S(1)}, f32[136,128]{1,0:T(8,128)S(1)}, u32[]{:S(2)}, u32[]{:S(2)}) %collective-permute-start.23) | collective-permute-done | bytes 69664 | tf_op jit(solution)/shard_map/ppermute | solution.py:42
  91.9 2.4 %collective-permute-start.26 = (f32[128,128]{1,0:T(8,128)S(1)}, f32[128,128]{1,0:T(8,128)S(1)}, u32[]{:S(2)}, u32[]{:S(2)}) collective-permute-start(f32[128,128]{1,0:T(8,128)S(1)} %slice.27.refs_1_), channel_id=1, source_target_pairs={{0,2},{1,3},{2,0},{3,1},{4,6},{5,7},{6,4},{7,5},{8,10},{9,11},{10,... | collective-permute-start | bytes 196616 | tf_op jit(solution)/shard_map/ppermute | solution.py:42
  108.2 2.3 %right_half_head.3 = (f32[200,128]{1,0:T(8,128)S(1)}, bf16[64,2048]{1,0:T(8,128)(2,1)S(1)}, f32[8,128]{1,0:T(8,128)S(1)}, f32[32,2048]{1,0:T(8,128)S(1)}) custom-call(s32[8]{0:T(128)S(1)} %get-tuple-element.39.places_ref, f32[32,2048]{1,0:T(8,128)S(1)} %get-tuple-element.57.refs_0_, f32[1,1,128]{2,1,0:T(1,128)S(1)} %add_add_fusion.6.refs_1_, ...), custom_call_target="tpu_custom_call" | custom-call | flops 1200000000 | bytes 8000000 | tf_op jit(solution)/shard_map/right_half_head/pallas_call | solution.py:316
  112.5 2.4 %collective-permute-start.34 = (f32[200,128]{1,0:T(8,128)S(1)}, f32[200,128]{1,0:T(8,128)S(1)}, u32[]{:S(2)}, u32[]{:S(2)}) collective-permute-start(f32[200,128]{1,0:T(8,128)S(1)} %add.108), channel_id=1, source_target_pairs={{0,64},{32,96},{64,0},{96,32},{16,80},{48,112},{80,16},{112,48},{1... | collective-permute-start | bytes 307208 | tf_op jit(solution)/shard_map/ppermute | solution.py:42
  116.1 3.6 %collective-permute-done.34 = f32[200,128]{1,0:T(8,128)S(1)} collective-permute-done((f32[200,128]{1,0:T(8,128)S(1)}, f32[200,128]{1,0:T(8,128)S(1)}, u32[]{:S(2)}, u32[]{:S(2)}) %collective-permute-start.34) | collective-permute-done | bytes 102432 | tf_op jit(solution)/shard_map/ppermute | solution.py:42
  119.6 2.1 %collective-permute-done.33 = f32[200,128]{1,0:T(8,128)S(1)} collective-permute-done((f32[200,128]{1,0:T(8,128)S(1)}, f32[200,128]{1,0:T(8,128)S(1)}, u32[]{:S(2)}, u32[]{:S(2)}) %collective-permute-start.33) | collective-permute-done | bytes 102432 | tf_op jit(solution)/shard_map/ppermute | solution.py:42
  124.9 11.4 %all_to_all.16.squares_ref = f32[16,1,128]{2,1,0:T(1,128)S(1)} all-to-all(f32[16,1,128]{2,1,0:T(1,128)S(1)} %get-tuple-element.66), channel_id=1, replica_groups=mesh['vox'=8,'var'=16] {'var'}, dimensions={0} | all-to-all | bytes 16384 | tf_op jit(solution)/shard_map/all_to_all | solution.py:51
  137.0 10.8 %all_to_all.17.last_ref = f32[16,16,128]{2,1,0:T(8,128)S(1)} all-to-all(f32[16,16,128]{2,1,0:T(8,128)S(1)} %get-tuple-element.67), channel_id=1, replica_groups=mesh['vox'=8,'var'=16] {'var'}, dimensions={0} | all-to-all | bytes 262144 | tf_op jit(solution)/shard_map/all_to_all | solution.py:51
  147.8 7.0 %deflate.1 = (f32[2048,1536]{1,0:T(8,128)}, f32[32,1536]{1,0:T(8,128)}, f32[1,32]{1,0:T(1,128)}) custom-call(f32[16,16,128]{2,1,0:T(8,128)S(1)} %all_to_all.17.last_ref, f32[32,1536]{1,0:T(8,128)S(1)} %get-tuple-element.68.shrunk_ref, bf16[2048,192]{1,0:T(8,128)(2,1)S(1)} %get-tuple-element.69.left_ref, ...), custom_call_target="tpu_custom_call" | custom-call | tf_op jit(solution)/shard_map/deflate/pallas_call | solution.py:434
  (90 shorter events, 55.2 us)
Async XLA Ops:
  8.0 5.7 %collective-permute-start = (f32[128,128]{1,0:T(8,128)S(1)}, f32[128,128]{1,0:T(8,128)S(1)}, u32[]{:S(2)}, u32[]{:S(2)}) collective-permute-start(f32[128,128]{1,0:T(8,128)S(1)} %get-tuple-element.41), channel_id=1, source_target_pairs={{0,1},{1,0},{2,3},{3,2},{4,5},{5,4},{6,7},{7,6},{8,9},{9,8},{10,11... | collective-permute-start | bytes 196616 | tf_op jit(solution)/shard_map/ppermute | solution.py:42
  10.1 5.5 %collective-permute-start.1 = (f32[128,128]{1,0:T(8,128)S(1)}, f32[128,128]{1,0:T(8,128)S(1)}, u32[]{:S(2)}, u32[]{:S(2)}) collective-permute-start(f32[128,128]{1,0:T(8,128)S(1)} %get-tuple-element.42), channel_id=1, source_target_pairs={{0,3},{1,2},{2,1},{3,0},{4,7},{5,6},{6,5},{7,4},{8,11},{9,10},{10,... | collective-permute-start | bytes 196616 | tf_op jit(solution)/shard_map/ppermute | solution.py:42
  12.6 5.8 %collective-permute-start.2 = (f32[128,128]{1,0:T(8,128)S(1)}, f32[128,128]{1,0:T(8,128)S(1)}, u32[]{:S(2)}, u32[]{:S(2)}) collective-permute-start(f32[128,128]{1,0:T(8,128)S(1)} %get-tuple-element.43), channel_id=1, source_target_pairs={{0,2},{1,3},{2,0},{3,1},{4,6},{5,7},{6,4},{7,5},{8,10},{9,11},{10,... | collective-permute-start | bytes 196616 | tf_op jit(solution)/shard_map/ppermute | solution.py:42
  18.4 6.0 %collective-permute-start.5 = (f32[128,128]{1,0:T(8,128)S(1)}, f32[128,128]{1,0:T(8,128)S(1)}, u32[]{:S(2)}, u32[]{:S(2)}) collective-permute-start(f32[128,128]{1,0:T(8,128)S(1)} %add_add_fusion.5), channel_id=1, source_target_pairs={{0,8},{4,12},{8,0},{12,4},{1,9},{5,13},{9,1},{13,5},{2,10},{6,14},... | collective-permute-start | bytes 196616 | tf_op jit(solution)/shard_map/ppermute | solution.py:42
  21.7 5.5 %collective-permute-start.4 = (f32[128,128]{1,0:T(8,128)S(1)}, f32[128,128]{1,0:T(8,128)S(1)}, u32[]{:S(2)}, u32[]{:S(2)}) collective-permute-start(f32[128,128]{1,0:T(8,128)S(1)} %add_add_fusion.5), channel_id=1, source_target_pairs={{0,12},{4,8},{8,4},{12,0},{1,13},{5,9},{9,5},{13,1},{2,14},{6,10},... | collective-permute-start | bytes 196616 | tf_op jit(solution)/shard_map/ppermute | solution.py:42
  27.2 5.8 %collective-permute-start.8 = (f32[128,128]{1,0:T(8,128)S(1)}, f32[128,128]{1,0:T(8,128)S(1)}, u32[]{:S(2)}, u32[]{:S(2)}) collective-permute-start(f32[128,128]{1,0:T(8,128)S(1)} %add_add_fusion.4.refs_0_), channel_id=1, source_target_pairs={{0,2},{1,3},{2,0},{3,1},{4,6},{5,7},{6,4},{7,5},{8,10},{9,11},{10,... | collective-permute-start | bytes 196616 | tf_op jit(solution)/shard_map/ppermute | solution.py:42
  28.3 5.5 %collective-permute-start.7 = (f32[128,128]{1,0:T(8,128)S(1)}, f32[128,128]{1,0:T(8,128)S(1)}, u32[]{:S(2)}, u32[]{:S(2)}) collective-permute-start(f32[128,128]{1,0:T(8,128)S(1)} %add_add_fusion.4.refs_0_), channel_id=1, source_target_pairs={{0,3},{1,2},{2,1},{3,0},{4,7},{5,6},{6,5},{7,4},{8,11},{9,10},{10,... | collective-permute-start | bytes 196616 | tf_op jit(solution)/shard_map/ppermute | solution.py:42
  37.1 5.0 %collective-permute-start.12 = (f32[1,1,128]{2,1,0:T(1,128)S(1)}, f32[1,1,128]{2,1,0:T(1,128)S(1)}, u32[]{:S(2)}, u32[]{:S(2)}) collective-permute-start(f32[1,1,128]{2,1,0:T(1,128)S(1)} %add.90), channel_id=1, source_target_pairs={{0,64},{32,96},{64,0},{96,32},{16,80},{48,112},{80,16},{112,48},{1... | collective-permute-start | bytes 1544 | tf_op jit(solution)/shard_map/ppermute | solution.py:42
  40.1 4.8 %collective-permute-start.11 = (f32[1,1,128]{2,1,0:T(1,128)S(1)}, f32[1,1,128]{2,1,0:T(1,128)S(1)}, u32[]{:S(2)}, u32[]{:S(2)}) collective-permute-start(f32[1,1,128]{2,1,0:T(1,128)S(1)} %add.90), channel_id=1, source_target_pairs={{0,96},{32,64},{64,32},{96,0},{16,112},{48,80},{80,48},{112,16},{1... | collective-permute-start | bytes 1544 | tf_op jit(solution)/shard_map/ppermute | solution.py:42
  49.2 7.2 %collective-permute-start.16 = (f32[200,128]{1,0:T(8,128)S(1)}, f32[200,128]{1,0:T(8,128)S(1)}, u32[]{:S(2)}, u32[]{:S(2)}) collective-permute-start(f32[200,128]{1,0:T(8,128)S(1)} %add.94), channel_id=1, source_target_pairs={{0,64},{32,96},{64,0},{96,32},{16,80},{48,112},{80,16},{112,48},{1... | collective-permute-start | bytes 307208 | tf_op jit(solution)/shard_map/ppermute | solution.py:42
  50.7 7.7 %collective-permute-start.15 = (f32[200,128]{1,0:T(8,128)S(1)}, f32[200,128]{1,0:T(8,128)S(1)}, u32[]{:S(2)}, u32[]{:S(2)}) collective-permute-start(f32[200,128]{1,0:T(8,128)S(1)} %add.94), channel_id=1, source_target_pairs={{0,96},{32,64},{64,32},{96,0},{16,112},{48,80},{80,48},{112,16},{1... | collective-permute-start | bytes 307208 | tf_op jit(solution)/shard_map/ppermute | solution.py:42
  51.9 6.6 %collective-permute-start.14 = (f32[200,128]{1,0:T(8,128)S(1)}, f32[200,128]{1,0:T(8,128)S(1)}, u32[]{:S(2)}, u32[]{:S(2)}) collective-permute-start(f32[200,128]{1,0:T(8,128)S(1)} %add.94), channel_id=1, source_target_pairs={{0,32},{32,0},{64,96},{96,64},{16,48},{48,16},{80,112},{112,80},{1... | collective-permute-start | bytes 307208 | tf_op jit(solution)/shard_map/ppermute | solution.py:42
  76.6 5.8 %collective-permute-start.18 = (f32[136,128]{1,0:T(8,128)S(1)}, f32[136,128]{1,0:T(8,128)S(1)}, u32[]{:S(2)}, u32[]{:S(2)}) collective-permute-start(f32[136,128]{1,0:T(8,128)S(1)} %get-tuple-element.54), channel_id=1, source_target_pairs={{0,1},{1,0},{2,3},{3,2},{4,5},{5,4},{6,7},{7,6},{8,9},{9,8},{10,11... | collective-permute-start | bytes 208904 | tf_op jit(solution)/shard_map/ppermute | solution.py:42
  77.2 5.6 %collective-permute-start.19 = (f32[136,128]{1,0:T(8,128)S(1)}, f32[136,128]{1,0:T(8,128)S(1)}, u32[]{:S(2)}, u32[]{:S(2)}) collective-permute-start(f32[136,128]{1,0:T(8,128)S(1)} %get-tuple-element.55), channel_id=1, source_target_pairs={{0,3},{1,2},{2,1},{3,0},{4,7},{5,6},{6,5},{7,4},{8,11},{9,10},{10,... | collective-permute-start | bytes 208904 | tf_op jit(solution)/shard_map/ppermute | solution.py:42
  78.4 5.8 %collective-permute-start.20 = (f32[136,128]{1,0:T(8,128)S(1)}, f32[136,128]{1,0:T(8,128)S(1)}, u32[]{:S(2)}, u32[]{:S(2)}) collective-permute-start(f32[136,128]{1,0:T(8,128)S(1)} %get-tuple-element.56), channel_id=1, source_target_pairs={{0,2},{1,3},{2,0},{3,1},{4,6},{5,7},{6,4},{7,5},{8,10},{9,11},{10,... | collective-permute-start | bytes 208904 | tf_op jit(solution)/shard_map/ppermute | solution.py:42
  84.3 5.9 %collective-permute-start.23 = (f32[136,128]{1,0:T(8,128)S(1)}, f32[136,128]{1,0:T(8,128)S(1)}, u32[]{:S(2)}, u32[]{:S(2)}) collective-permute-start(f32[136,128]{1,0:T(8,128)S(1)} %add_add_fusion.3), channel_id=1, source_target_pairs={{0,8},{4,12},{8,0},{12,4},{1,9},{5,13},{9,1},{13,5},{2,10},{6,14},... | collective-permute-start | bytes 208904 | tf_op jit(solution)/shard_map/ppermute | solution.py:42
  85.5 5.5 %collective-permute-start.22 = (f32[136,128]{1,0:T(8,128)S(1)}, f32[136,128]{1,0:T(8,128)S(1)}, u32[]{:S(2)}, u32[]{:S(2)}) collective-permute-start(f32[136,128]{1,0:T(8,128)S(1)} %add_add_fusion.3), channel_id=1, source_target_pairs={{0,12},{4,8},{8,4},{12,0},{1,13},{5,9},{9,5},{13,1},{2,14},{6,10},... | collective-permute-start | bytes 208904 | tf_op jit(solution)/shard_map/ppermute | solution.py:42
  91.9 5.8 %collective-permute-start.26 = (f32[128,128]{1,0:T(8,128)S(1)}, f32[128,128]{1,0:T(8,128)S(1)}, u32[]{:S(2)}, u32[]{:S(2)}) collective-permute-start(f32[128,128]{1,0:T(8,128)S(1)} %slice.27.refs_1_), channel_id=1, source_target_pairs={{0,2},{1,3},{2,0},{3,1},{4,6},{5,7},{6,4},{7,5},{8,10},{9,11},{10,... | collective-permute-start | bytes 196616 | tf_op jit(solution)/shard_map/ppermute | solution.py:42
  94.3 5.5 %collective-permute-start.25 = (f32[128,128]{1,0:T(8,128)S(1)}, f32[128,128]{1,0:T(8,128)S(1)}, u32[]{:S(2)}, u32[]{:S(2)}) collective-permute-start(f32[128,128]{1,0:T(8,128)S(1)} %slice.27.refs_1_), channel_id=1, source_target_pairs={{0,3},{1,2},{2,1},{3,0},{4,7},{5,6},{6,5},{7,4},{8,11},{9,10},{10,... | collective-permute-start | bytes 196616 | tf_op jit(solution)/shard_map/ppermute | solution.py:42
  101.9 5.0 %collective-permute-start.30 = (f32[1,1,128]{2,1,0:T(1,128)S(1)}, f32[1,1,128]{2,1,0:T(1,128)S(1)}, u32[]{:S(2)}, u32[]{:S(2)}) collective-permute-start(f32[1,1,128]{2,1,0:T(1,128)S(1)} %add.104), channel_id=1, source_target_pairs={{0,64},{32,96},{64,0},{96,32},{16,80},{48,112},{80,16},{112,48},{1... | collective-permute-start | bytes 1544 | tf_op jit(solution)/shard_map/ppermute | solution.py:42
  103.4 4.8 %collective-permute-start.29 = (f32[1,1,128]{2,1,0:T(1,128)S(1)}, f32[1,1,128]{2,1,0:T(1,128)S(1)}, u32[]{:S(2)}, u32[]{:S(2)}) collective-permute-start(f32[1,1,128]{2,1,0:T(1,128)S(1)} %add.104), channel_id=1, source_target_pairs={{0,96},{32,64},{64,32},{96,0},{16,112},{48,80},{80,48},{112,16},{1... | collective-permute-start | bytes 1544 | tf_op jit(solution)/shard_map/ppermute | solution.py:42
  112.5 7.1 %collective-permute-start.34 = (f32[200,128]{1,0:T(8,128)S(1)}, f32[200,128]{1,0:T(8,128)S(1)}, u32[]{:S(2)}, u32[]{:S(2)}) collective-permute-start(f32[200,128]{1,0:T(8,128)S(1)} %add.108), channel_id=1, source_target_pairs={{0,64},{32,96},{64,0},{96,32},{16,80},{48,112},{80,16},{112,48},{1... | collective-permute-start | bytes 307208 | tf_op jit(solution)/shard_map/ppermute | solution.py:42
  114.8 6.9 %collective-permute-start.33 = (f32[200,128]{1,0:T(8,128)S(1)}, f32[200,128]{1,0:T(8,128)S(1)}, u32[]{:S(2)}, u32[]{:S(2)}) collective-permute-start(f32[200,128]{1,0:T(8,128)S(1)} %add.108), channel_id=1, source_target_pairs={{0,96},{32,64},{64,32},{96,0},{16,112},{48,80},{80,48},{112,16},{1... | collective-permute-start | bytes 307208 | tf_op jit(solution)/shard_map/ppermute | solution.py:42
  116.1 5.7 %collective-permute-start.32 = (f32[200,128]{1,0:T(8,128)S(1)}, f32[200,128]{1,0:T(8,128)S(1)}, u32[]{:S(2)}, u32[]{:S(2)}) collective-permute-start(f32[200,128]{1,0:T(8,128)S(1)} %add.108), channel_id=1, source_target_pairs={{0,32},{32,0},{64,96},{96,64},{16,48},{48,16},{80,112},{112,80},{1... | collective-permute-start | bytes 307208 | tf_op jit(solution)/shard_map/ppermute | solution.py:42
  (14 other events, 78.7 us)

commit v7 on v6

--- a/solution.py
+++ b/solution.py
@@ -105,9 +105,9 @@
     return values - jnp.clip(values, -level, level)
 
 
-def stack(ref, values):
+def stack(ref, values, first=0):
     for at in range(values.shape[1] // LANES):
-        ref[at * K : (at + 1) * K, :] = values[:, at * LANES : (at + 1) * LANES]
+        ref[first + at * K : first + (at + 1) * K, :] = values[:, at * LANES : (at + 1) * LANES]
 
 
 def unstacked(values):
@@ -170,7 +170,6 @@
 def left_product_first(right, cross):
     chunk = QUARTER // 2
     chunks = ROWS // chunk
-    ahead = 6
 
     def kernel(right_hbm, cross_hbm, *refs):
         *outs, kept_ref, places_ref, right_ref, right_sem, sems = refs
@@ -189,7 +188,7 @@
 
         right_copy = pltpu.make_async_copy(right_hbm, right_ref, right_sem)
         right_copy.start()
-        for at in range(ahead):
+        for at in range(chunks):
             copy_of(at).start()
         for at, place in enumerate(places):
             places_ref[Z_AT + at] = place
@@ -199,13 +198,10 @@
         places_ref[7] = 0
         right_copy.wait()
         both = jnp.concatenate(split2(right_ref[...]), axis=0)
-        for quarter in range(4):
-            for at in (2 * quarter, 2 * quarter + 1):
-                copy_of(at).wait()
-                if at + ahead < chunks:
-                    copy_of(at + ahead).start()
-            rows = pl.ds(pl.multiple_of(places[quarter] * QUARTER, QUARTER), QUARTER)
-            stack(outs[quarter], left_terms_of(both, kept_ref[rows, :]))
+        for at in range(chunks):
+            copy_of(at).wait()
+            product = left_terms_of(both, kept_ref[rows_of(at), :])
+            stack(outs[at // 2], product, at % 2 * (LEFT_ROWS // 2))
 
     vmem = pl.BlockSpec(memory_space=pltpu.VMEM)
     hbm = pl.BlockSpec(memory_space=pltpu.HBM)

time: 155 us -> 158 us (1.019)
  Pallas kernels: 35.8 us -> 38.6 us
    pallas_call x1, Pallas kernels: 6.43 us -> 9.27 us  [left_product_first(): pl.pallas_call(kernel, in_specs=[hbm, hbm], out_specs=[vmem] * 5 + [pl.Bl...]
where the time goes in v7:
time: 158 us
  waiting for transfers between devices  42.9 us (27%)
  starting transfers between devices  40.7 us (26%)
  Pallas kernels  38.6 us (24%)
  blocking collectives  33.7 us (21%)
    ppermute x36, waiting for transfers between devices, swap(): return lax.ppermute(value, axis, pairs)  42.9 us
    ppermute x36, starting transfers between devices, swap(): return lax.ppermute(value, axis, pairs)  40.7 us
    all_to_all x3, blocking collectives, from_all(): return lax.all_to_all(value, 'var', 0, 0)  33.7 us
    pallas_call x1, Pallas kernels, left_product_first(): pl.pallas_call(kernel, in_specs=[hbm, hbm], out_specs=[vmem] * 5 + [pl.Bl...  9.27 us
    pallas_call x4, Pallas kernels, right_half(): pl.pallas_call(kernel, grid_spec=pltpu.PrefetchScalarGridSpec(num_scalar_...  8.43 us
    pallas_call x1, Pallas kernels, deflate(): pl.pallas_call(kernel, grid=(ROWS // BLOCK,), in_specs=[whole((16, K // 2...  7 us
    pallas_call x1, Pallas kernels, left_partners(): pl.pallas_call(kernel, grid_spec=pltpu.PrefetchScalarGridSpec(num_scalar_...  4.37 us
    pallas_call x4, Pallas kernels, assemble(): pl.pallas_call(kernel, in_specs=[pl.BlockSpec(memory_space=pltpu.SMEM)] +...  3.36 us
  transfers between devices with their start and end apart: 36, of which 25 were waited for; matrix products, arithmetic and copies ran while one was open for 0% of the time, Pallas kernels for 6%

profile of v7, /device:TPU:0, one launch (start us, length us, event | category | flops | bytes accessed | tf_op | source)
XLA Modules:
  0.0 157.8 jit_solution(7945556688143273448)
XLA Ops:
  1.6 9.3 %left_product_first.1 = (f32[128,128]{1,0:T(8,128)S(1)}, f32[128,128]{1,0:T(8,128)S(1)}, f32[128,128]{1,0:T(8,128)S(1)}, f32[128,128]{1,0:T(8,128)S(1)}, f32[2048,1536]{1,0:T(8,128)S(1)}, /*index=5*/s32[8]{0:T(128)S(1)}) custom-call(f32[32,1536]{1,0:T(8,128)S(1)} %copy-done, f32[2048,1536]{1,0:T(8,128)} %cross_hbm.1), custom_call_target="tpu_custom_call" | custom-call | tf_op jit(solution)/shard_map/left_product_first/pallas_call | solution.py:208
  10.8 2.1 %collective-permute-start = (f32[128,128]{1,0:T(8,128)S(1)}, f32[128,128]{1,0:T(8,128)S(1)}, u32[]{:S(2)}, u32[]{:S(2)}) collective-permute-start(f32[128,128]{1,0:T(8,128)S(1)} %get-tuple-element.41), channel_id=1, source_target_pairs={{0,1},{1,0},{2,3},{3,2},{4,5},{5,4},{6,7},{7,6},{8,9},{9,8},{10,11... | collective-permute-start | bytes 196616 | tf_op jit(solution)/shard_map/ppermute | solution.py:42
  12.9 2.5 %collective-permute-start.1 = (f32[128,128]{1,0:T(8,128)S(1)}, f32[128,128]{1,0:T(8,128)S(1)}, u32[]{:S(2)}, u32[]{:S(2)}) collective-permute-start(f32[128,128]{1,0:T(8,128)S(1)} %get-tuple-element.42), channel_id=1, source_target_pairs={{0,3},{1,2},{2,1},{3,0},{4,7},{5,6},{6,5},{7,4},{8,11},{9,10},{10,... | collective-permute-start | bytes 196616 | tf_op jit(solution)/shard_map/ppermute | solution.py:42
  18.4 2.8 %collective-permute-done.2 = f32[128,128]{1,0:T(8,128)S(1)} collective-permute-done((f32[128,128]{1,0:T(8,128)S(1)}, f32[128,128]{1,0:T(8,128)S(1)}, u32[]{:S(2)}, u32[]{:S(2)}) %collective-permute-start.2) | collective-permute-done | bytes 65568 | tf_op jit(solution)/shard_map/ppermute | solution.py:42
  21.2 3.3 %collective-permute-start.5 = (f32[128,128]{1,0:T(8,128)S(1)}, f32[128,128]{1,0:T(8,128)S(1)}, u32[]{:S(2)}, u32[]{:S(2)}) collective-permute-start(f32[128,128]{1,0:T(8,128)S(1)} %add_add_fusion.5), channel_id=1, source_target_pairs={{0,8},{4,12},{8,0},{12,4},{1,9},{5,13},{9,1},{13,5},{2,10},{6,14},... | collective-permute-start | bytes 196616 | tf_op jit(solution)/shard_map/ppermute | solution.py:42
  27.2 2.8 %collective-permute-done.4 = f32[128,128]{1,0:T(8,128)S(1)} collective-permute-done((f32[128,128]{1,0:T(8,128)S(1)}, f32[128,128]{1,0:T(8,128)S(1)}, u32[]{:S(2)}, u32[]{:S(2)}) %collective-permute-start.4) | collective-permute-done | bytes 65568 | tf_op jit(solution)/shard_map/ppermute | solution.py:42
  31.2 2.6 %collective-permute-start.7 = (f32[128,128]{1,0:T(8,128)S(1)}, f32[128,128]{1,0:T(8,128)S(1)}, u32[]{:S(2)}, u32[]{:S(2)}) collective-permute-start(f32[128,128]{1,0:T(8,128)S(1)} %add_add_fusion.4.refs_0_), channel_id=1, source_target_pairs={{0,3},{1,2},{2,1},{3,0},{4,7},{5,6},{6,5},{7,4},{8,11},{9,10},{10,... | collective-permute-start | bytes 196616 | tf_op jit(solution)/shard_map/ppermute | solution.py:42
  39.9 3.0 %collective-permute-start.12 = (f32[1,1,128]{2,1,0:T(1,128)S(1)}, f32[1,1,128]{2,1,0:T(1,128)S(1)}, u32[]{:S(2)}, u32[]{:S(2)}) collective-permute-start(f32[1,1,128]{2,1,0:T(1,128)S(1)} %add.90), channel_id=1, source_target_pairs={{0,64},{32,96},{64,0},{96,32},{16,80},{48,112},{80,16},{112,48},{1... | collective-permute-start | bytes 1544 | tf_op jit(solution)/shard_map/ppermute | solution.py:42
  44.9 2.7 %collective-permute-done.11 = f32[1,1,128]{2,1,0:T(1,128)S(1)} collective-permute-done((f32[1,1,128]{2,1,0:T(1,128)S(1)}, f32[1,1,128]{2,1,0:T(1,128)S(1)}, u32[]{:S(2)}, u32[]{:S(2)}) %collective-permute-start.11) | collective-permute-done | bytes 544 | tf_op jit(solution)/shard_map/ppermute | solution.py:42
  47.7 2.2 %right_half_head.2 = (f32[200,128]{1,0:T(8,128)S(1)}, bf16[64,2048]{1,0:T(8,128)(2,1)S(1)}, f32[8,128]{1,0:T(8,128)S(1)}, f32[32,2048]{1,0:T(8,128)}) custom-call(s32[8]{0:T(128)S(1)} %get-tuple-element.39.places_ref, f32[32,2048]{1,0:T(8,128)S(1)} %get-tuple-element.44.refs_0_, f32[1,1,128]{2,1,0:T(1,128)S(1)} %add_add_fusion.7.refs_1_, ...), custom_call_target="tpu_custom_call" | custom-call | flops 1200000000 | bytes 8000000 | tf_op jit(solution)/shard_map/right_half_head/pallas_call | solution.py:312
  55.6 3.6 %collective-permute-done.16 = f32[200,128]{1,0:T(8,128)S(1)} collective-permute-done((f32[200,128]{1,0:T(8,128)S(1)}, f32[200,128]{1,0:T(8,128)S(1)}, u32[]{:S(2)}, u32[]{:S(2)}) %collective-permute-start.16) | collective-permute-done | bytes 102432 | tf_op jit(solution)/shard_map/ppermute | solution.py:42
  59.2 2.1 %collective-permute-done.15 = f32[200,128]{1,0:T(8,128)S(1)} collective-permute-done((f32[200,128]{1,0:T(8,128)S(1)}, f32[200,128]{1,0:T(8,128)S(1)}, u32[]{:S(2)}, u32[]{:S(2)}) %collective-permute-start.15) | collective-permute-done | bytes 102432 | tf_op jit(solution)/shard_map/ppermute | solution.py:42
  63.8 11.4 %all_to_all.15.squares_ref = f32[16,1,128]{2,1,0:T(1,128)S(1)} all-to-all(f32[16,1,128]{2,1,0:T(1,128)S(1)} %get-tuple-element.51), channel_id=1, replica_groups=mesh['vox'=8,'var'=16] {'var'}, dimensions={0} | all-to-all | bytes 16384 | tf_op jit(solution)/shard_map/all_to_all | solution.py:51
  75.2 4.4 %left_partners.1 = (f32[136,128]{1,0:T(8,128)S(1)}, f32[136,128]{1,0:T(8,128)S(1)}, f32[136,128]{1,0:T(8,128)S(1)}, bf16[64,1536]{1,0:T(8,128)(2,1)S(1)}, f32[8,128]{1,0:T(8,128)S(1)}) custom-call(s32[8]{0:T(128)S(1)} %get-tuple-element.39.places_ref, f32[32,1536]{1,0:T(8,128)S(1)} %get-tuple-element.50.right_ref, f32[16,1,128]{2,1,0:T(1,128)S(1)} %all_to_all.15.squares_ref, ...), custom_call_target="tpu_custom_call" | custom-call | tf_op jit(solution)/shard_map/left_partners/pallas_call | solution.py:251
  81.4 2.3 %collective-permute-start.20 = (f32[136,128]{1,0:T(8,128)S(1)}, f32[136,128]{1,0:T(8,128)S(1)}, u32[]{:S(2)}, u32[]{:S(2)}) collective-permute-start(f32[136,128]{1,0:T(8,128)S(1)} %get-tuple-element.56), channel_id=1, source_target_pairs={{0,2},{1,3},{2,0},{3,1},{4,6},{5,7},{6,4},{7,5},{8,10},{9,11},{10,... | collective-permute-start | bytes 208904 | tf_op jit(solution)/shard_map/ppermute | solution.py:42
  90.8 2.3 %collective-permute-done.23 = f32[136,128]{1,0:T(8,128)S(1)} collective-permute-done((f32[136,128]{1,0:T(8,128)S(1)}, f32[136,128]{1,0:T(8,128)S(1)}, u32[]{:S(2)}, u32[]{:S(2)}) %collective-permute-start.23) | collective-permute-done | bytes 69664 | tf_op jit(solution)/shard_map/ppermute | solution.py:42
  94.9 2.4 %collective-permute-start.26 = (f32[128,128]{1,0:T(8,128)S(1)}, f32[128,128]{1,0:T(8,128)S(1)}, u32[]{:S(2)}, u32[]{:S(2)}) collective-permute-start(f32[128,128]{1,0:T(8,128)S(1)} %slice.27.refs_1_), channel_id=1, source_target_pairs={{0,2},{1,3},{2,0},{3,1},{4,6},{5,7},{6,4},{7,5},{8,10},{9,11},{10,... | collective-permute-start | bytes 196616 | tf_op jit(solution)/shard_map/ppermute | solution.py:42
  111.2 2.3 %right_half_head.3 = (f32[200,128]{1,0:T(8,128)S(1)}, bf16[64,2048]{1,0:T(8,128)(2,1)S(1)}, f32[8,128]{1,0:T(8,128)S(1)}, f32[32,2048]{1,0:T(8,128)S(1)}) custom-call(s32[8]{0:T(128)S(1)} %get-tuple-element.39.places_ref, f32[32,2048]{1,0:T(8,128)S(1)} %get-tuple-element.57.refs_0_, f32[1,1,128]{2,1,0:T(1,128)S(1)} %add_add_fusion.6.refs_1_, ...), custom_call_target="tpu_custom_call" | custom-call | flops 1200000000 | bytes 8000000 | tf_op jit(solution)/shard_map/right_half_head/pallas_call | solution.py:312
  115.5 2.3 %collective-permute-start.34 = (f32[200,128]{1,0:T(8,128)S(1)}, f32[200,128]{1,0:T(8,128)S(1)}, u32[]{:S(2)}, u32[]{:S(2)}) collective-permute-start(f32[200,128]{1,0:T(8,128)S(1)} %add.108), channel_id=1, source_target_pairs={{0,64},{32,96},{64,0},{96,32},{16,80},{48,112},{80,16},{112,48},{1... | collective-permute-start | bytes 307208 | tf_op jit(solution)/shard_map/ppermute | solution.py:42
  119.1 3.6 %collective-permute-done.34 = f32[200,128]{1,0:T(8,128)S(1)} collective-permute-done((f32[200,128]{1,0:T(8,128)S(1)}, f32[200,128]{1,0:T(8,128)S(1)}, u32[]{:S(2)}, u32[]{:S(2)}) %collective-permute-start.34) | collective-permute-done | bytes 102432 | tf_op jit(solution)/shard_map/ppermute | solution.py:42
  122.6 2.1 %collective-permute-done.33 = f32[200,128]{1,0:T(8,128)S(1)} collective-permute-done((f32[200,128]{1,0:T(8,128)S(1)}, f32[200,128]{1,0:T(8,128)S(1)}, u32[]{:S(2)}, u32[]{:S(2)}) %collective-permute-start.33) | collective-permute-done | bytes 102432 | tf_op jit(solution)/shard_map/ppermute | solution.py:42
  127.9 11.4 %all_to_all.16.squares_ref = f32[16,1,128]{2,1,0:T(1,128)S(1)} all-to-all(f32[16,1,128]{2,1,0:T(1,128)S(1)} %get-tuple-element.66), channel_id=1, replica_groups=mesh['vox'=8,'var'=16] {'var'}, dimensions={0} | all-to-all | bytes 16384 | tf_op jit(solution)/shard_map/all_to_all | solution.py:51
  140.0 10.8 %all_to_all.17.last_ref = f32[16,16,128]{2,1,0:T(8,128)S(1)} all-to-all(f32[16,16,128]{2,1,0:T(8,128)S(1)} %get-tuple-element.67), channel_id=1, replica_groups=mesh['vox'=8,'var'=16] {'var'}, dimensions={0} | all-to-all | bytes 262144 | tf_op jit(solution)/shard_map/all_to_all | solution.py:51
  150.8 7.0 %deflate.1 = (f32[2048,1536]{1,0:T(8,128)}, f32[32,1536]{1,0:T(8,128)}, f32[1,32]{1,0:T(1,128)}) custom-call(f32[16,16,128]{2,1,0:T(8,128)S(1)} %all_to_all.17.last_ref, f32[32,1536]{1,0:T(8,128)S(1)} %get-tuple-element.68.shrunk_ref, bf16[2048,192]{1,0:T(8,128)(2,1)S(1)} %get-tuple-element.69.left_ref, ...), custom_call_target="tpu_custom_call" | custom-call | tf_op jit(solution)/shard_map/deflate/pallas_call | solution.py:430
  (90 shorter events, 55.4 us)
Async XLA Ops:
  10.8 5.7 %collective-permute-start = (f32[128,128]{1,0:T(8,128)S(1)}, f32[128,128]{1,0:T(8,128)S(1)}, u32[]{:S(2)}, u32[]{:S(2)}) collective-permute-start(f32[128,128]{1,0:T(8,128)S(1)} %get-tuple-element.41), channel_id=1, source_target_pairs={{0,1},{1,0},{2,3},{3,2},{4,5},{5,4},{6,7},{7,6},{8,9},{9,8},{10,11... | collective-permute-start | bytes 196616 | tf_op jit(solution)/shard_map/ppermute | solution.py:42
  12.9 5.5 %collective-permute-start.1 = (f32[128,128]{1,0:T(8,128)S(1)}, f32[128,128]{1,0:T(8,128)S(1)}, u32[]{:S(2)}, u32[]{:S(2)}) collective-permute-start(f32[128,128]{1,0:T(8,128)S(1)} %get-tuple-element.42), channel_id=1, source_target_pairs={{0,3},{1,2},{2,1},{3,0},{4,7},{5,6},{6,5},{7,4},{8,11},{9,10},{10,... | collective-permute-start | bytes 196616 | tf_op jit(solution)/shard_map/ppermute | solution.py:42
  15.4 5.8 %collective-permute-start.2 = (f32[128,128]{1,0:T(8,128)S(1)}, f32[128,128]{1,0:T(8,128)S(1)}, u32[]{:S(2)}, u32[]{:S(2)}) collective-permute-start(f32[128,128]{1,0:T(8,128)S(1)} %get-tuple-element.43), channel_id=1, source_target_pairs={{0,2},{1,3},{2,0},{3,1},{4,6},{5,7},{6,4},{7,5},{8,10},{9,11},{10,... | collective-permute-start | bytes 196616 | tf_op jit(solution)/shard_map/ppermute | solution.py:42
  21.2 6.0 %collective-permute-start.5 = (f32[128,128]{1,0:T(8,128)S(1)}, f32[128,128]{1,0:T(8,128)S(1)}, u32[]{:S(2)}, u32[]{:S(2)}) collective-permute-start(f32[128,128]{1,0:T(8,128)S(1)} %add_add_fusion.5), channel_id=1, source_target_pairs={{0,8},{4,12},{8,0},{12,4},{1,9},{5,13},{9,1},{13,5},{2,10},{6,14},... | collective-permute-start | bytes 196616 | tf_op jit(solution)/shard_map/ppermute | solution.py:42
  24.5 5.5 %collective-permute-start.4 = (f32[128,128]{1,0:T(8,128)S(1)}, f32[128,128]{1,0:T(8,128)S(1)}, u32[]{:S(2)}, u32[]{:S(2)}) collective-permute-start(f32[128,128]{1,0:T(8,128)S(1)} %add_add_fusion.5), channel_id=1, source_target_pairs={{0,12},{4,8},{8,4},{12,0},{1,13},{5,9},{9,5},{13,1},{2,14},{6,10},... | collective-permute-start | bytes 196616 | tf_op jit(solution)/shard_map/ppermute | solution.py:42
  30.0 5.8 %collective-permute-start.8 = (f32[128,128]{1,0:T(8,128)S(1)}, f32[128,128]{1,0:T(8,128)S(1)}, u32[]{:S(2)}, u32[]{:S(2)}) collective-permute-start(f32[128,128]{1,0:T(8,128)S(1)} %add_add_fusion.4.refs_0_), channel_id=1, source_target_pairs={{0,2},{1,3},{2,0},{3,1},{4,6},{5,7},{6,4},{7,5},{8,10},{9,11},{10,... | collective-permute-start | bytes 196616 | tf_op jit(solution)/shard_map/ppermute | solution.py:42
  31.2 5.5 %collective-permute-start.7 = (f32[128,128]{1,0:T(8,128)S(1)}, f32[128,128]{1,0:T(8,128)S(1)}, u32[]{:S(2)}, u32[]{:S(2)}) collective-permute-start(f32[128,128]{1,0:T(8,128)S(1)} %add_add_fusion.4.refs_0_), channel_id=1, source_target_pairs={{0,3},{1,2},{2,1},{3,0},{4,7},{5,6},{6,5},{7,4},{8,11},{9,10},{10,... | collective-permute-start | bytes 196616 | tf_op jit(solution)/shard_map/ppermute | solution.py:42
  39.9 5.0 %collective-permute-start.12 = (f32[1,1,128]{2,1,0:T(1,128)S(1)}, f32[1,1,128]{2,1,0:T(1,128)S(1)}, u32[]{:S(2)}, u32[]{:S(2)}) collective-permute-start(f32[1,1,128]{2,1,0:T(1,128)S(1)} %add.90), channel_id=1, source_target_pairs={{0,64},{32,96},{64,0},{96,32},{16,80},{48,112},{80,16},{112,48},{1... | collective-permute-start | bytes 1544 | tf_op jit(solution)/shard_map/ppermute | solution.py:42
  42.9 4.8 %collective-permute-start.11 = (f32[1,1,128]{2,1,0:T(1,128)S(1)}, f32[1,1,128]{2,1,0:T(1,128)S(1)}, u32[]{:S(2)}, u32[]{:S(2)}) collective-permute-start(f32[1,1,128]{2,1,0:T(1,128)S(1)} %add.90), channel_id=1, source_target_pairs={{0,96},{32,64},{64,32},{96,0},{16,112},{48,80},{80,48},{112,16},{1... | collective-permute-start | bytes 1544 | tf_op jit(solution)/shard_map/ppermute | solution.py:42
  52.0 7.2 %collective-permute-start.16 = (f32[200,128]{1,0:T(8,128)S(1)}, f32[200,128]{1,0:T(8,128)S(1)}, u32[]{:S(2)}, u32[]{:S(2)}) collective-permute-start(f32[200,128]{1,0:T(8,128)S(1)} %add.94), channel_id=1, source_target_pairs={{0,64},{32,96},{64,0},{96,32},{16,80},{48,112},{80,16},{112,48},{1... | collective-permute-start | bytes 307208 | tf_op jit(solution)/shard_map/ppermute | solution.py:42
  53.6 7.7 %collective-permute-start.15 = (f32[200,128]{1,0:T(8,128)S(1)}, f32[200,128]{1,0:T(8,128)S(1)}, u32[]{:S(2)}, u32[]{:S(2)}) collective-permute-start(f32[200,128]{1,0:T(8,128)S(1)} %add.94), channel_id=1, source_target_pairs={{0,96},{32,64},{64,32},{96,0},{16,112},{48,80},{80,48},{112,16},{1... | collective-permute-start | bytes 307208 | tf_op jit(solution)/shard_map/ppermute | solution.py:42
  54.7 6.6 %collective-permute-start.14 = (f32[200,128]{1,0:T(8,128)S(1)}, f32[200,128]{1,0:T(8,128)S(1)}, u32[]{:S(2)}, u32[]{:S(2)}) collective-permute-start(f32[200,128]{1,0:T(8,128)S(1)} %add.94), channel_id=1, source_target_pairs={{0,32},{32,0},{64,96},{96,64},{16,48},{48,16},{80,112},{112,80},{1... | collective-permute-start | bytes 307208 | tf_op jit(solution)/shard_map/ppermute | solution.py:42
  79.6 5.8 %collective-permute-start.18 = (f32[136,128]{1,0:T(8,128)S(1)}, f32[136,128]{1,0:T(8,128)S(1)}, u32[]{:S(2)}, u32[]{:S(2)}) collective-permute-start(f32[136,128]{1,0:T(8,128)S(1)} %get-tuple-element.54), channel_id=1, source_target_pairs={{0,1},{1,0},{2,3},{3,2},{4,5},{5,4},{6,7},{7,6},{8,9},{9,8},{10,11... | collective-permute-start | bytes 208904 | tf_op jit(solution)/shard_map/ppermute | solution.py:42
  80.2 5.6 %collective-permute-start.19 = (f32[136,128]{1,0:T(8,128)S(1)}, f32[136,128]{1,0:T(8,128)S(1)}, u32[]{:S(2)}, u32[]{:S(2)}) collective-permute-start(f32[136,128]{1,0:T(8,128)S(1)} %get-tuple-element.55), channel_id=1, source_target_pairs={{0,3},{1,2},{2,1},{3,0},{4,7},{5,6},{6,5},{7,4},{8,11},{9,10},{10,... | collective-permute-start | bytes 208904 | tf_op jit(solution)/shard_map/ppermute | solution.py:42
  81.4 5.8 %collective-permute-start.20 = (f32[136,128]{1,0:T(8,128)S(1)}, f32[136,128]{1,0:T(8,128)S(1)}, u32[]{:S(2)}, u32[]{:S(2)}) collective-permute-start(f32[136,128]{1,0:T(8,128)S(1)} %get-tuple-element.56), channel_id=1, source_target_pairs={{0,2},{1,3},{2,0},{3,1},{4,6},{5,7},{6,4},{7,5},{8,10},{9,11},{10,... | collective-permute-start | bytes 208904 | tf_op jit(solution)/shard_map/ppermute | solution.py:42
  87.3 5.9 %collective-permute-start.23 = (f32[136,128]{1,0:T(8,128)S(1)}, f32[136,128]{1,0:T(8,128)S(1)}, u32[]{:S(2)}, u32[]{:S(2)}) collective-permute-start(f32[136,128]{1,0:T(8,128)S(1)} %add_add_fusion.3), channel_id=1, source_target_pairs={{0,8},{4,12},{8,0},{12,4},{1,9},{5,13},{9,1},{13,5},{2,10},{6,14},... | collective-permute-start | bytes 208904 | tf_op jit(solution)/shard_map/ppermute | solution.py:42
  88.5 5.5 %collective-permute-start.22 = (f32[136,128]{1,0:T(8,128)S(1)}, f32[136,128]{1,0:T(8,128)S(1)}, u32[]{:S(2)}, u32[]{:S(2)}) collective-permute-start(f32[136,128]{1,0:T(8,128)S(1)} %add_add_fusion.3), channel_id=1, source_target_pairs={{0,12},{4,8},{8,4},{12,0},{1,13},{5,9},{9,5},{13,1},{2,14},{6,10},... | collective-permute-start | bytes 208904 | tf_op jit(solution)/shard_map/ppermute | solution.py:42
  94.9 5.8 %collective-permute-start.26 = (f32[128,128]{1,0:T(8,128)S(1)}, f32[128,128]{1,0:T(8,128)S(1)}, u32[]{:S(2)}, u32[]{:S(2)}) collective-permute-start(f32[128,128]{1,0:T(8,128)S(1)} %slice.27.refs_1_), channel_id=1, source_target_pairs={{0,2},{1,3},{2,0},{3,1},{4,6},{5,7},{6,4},{7,5},{8,10},{9,11},{10,... | collective-permute-start | bytes 196616 | tf_op jit(solution)/shard_map/ppermute | solution.py:42
  97.3 5.5 %collective-permute-start.25 = (f32[128,128]{1,0:T(8,128)S(1)}, f32[128,128]{1,0:T(8,128)S(1)}, u32[]{:S(2)}, u32[]{:S(2)}) collective-permute-start(f32[128,128]{1,0:T(8,128)S(1)} %slice.27.refs_1_), channel_id=1, source_target_pairs={{0,3},{1,2},{2,1},{3,0},{4,7},{5,6},{6,5},{7,4},{8,11},{9,10},{10,... | collective-permute-start | bytes 196616 | tf_op jit(solution)/shard_map/ppermute | solution.py:42
  105.0 5.0 %collective-permute-start.30 = (f32[1,1,128]{2,1,0:T(1,128)S(1)}, f32[1,1,128]{2,1,0:T(1,128)S(1)}, u32[]{:S(2)}, u32[]{:S(2)}) collective-permute-start(f32[1,1,128]{2,1,0:T(1,128)S(1)} %add.104), channel_id=1, source_target_pairs={{0,64},{32,96},{64,0},{96,32},{16,80},{48,112},{80,16},{112,48},{1... | collective-permute-start | bytes 1544 | tf_op jit(solution)/shard_map/ppermute | solution.py:42
  106.4 4.8 %collective-permute-start.29 = (f32[1,1,128]{2,1,0:T(1,128)S(1)}, f32[1,1,128]{2,1,0:T(1,128)S(1)}, u32[]{:S(2)}, u32[]{:S(2)}) collective-permute-start(f32[1,1,128]{2,1,0:T(1,128)S(1)} %add.104), channel_id=1, source_target_pairs={{0,96},{32,64},{64,32},{96,0},{16,112},{48,80},{80,48},{112,16},{1... | collective-permute-start | bytes 1544 | tf_op jit(solution)/shard_map/ppermute | solution.py:42
  115.5 7.1 %collective-permute-start.34 = (f32[200,128]{1,0:T(8,128)S(1)}, f32[200,128]{1,0:T(8,128)S(1)}, u32[]{:S(2)}, u32[]{:S(2)}) collective-permute-start(f32[200,128]{1,0:T(8,128)S(1)} %add.108), channel_id=1, source_target_pairs={{0,64},{32,96},{64,0},{96,32},{16,80},{48,112},{80,16},{112,48},{1... | collective-permute-start | bytes 307208 | tf_op jit(solution)/shard_map/ppermute | solution.py:42
  117.8 6.9 %collective-permute-start.33 = (f32[200,128]{1,0:T(8,128)S(1)}, f32[200,128]{1,0:T(8,128)S(1)}, u32[]{:S(2)}, u32[]{:S(2)}) collective-permute-start(f32[200,128]{1,0:T(8,128)S(1)} %add.108), channel_id=1, source_target_pairs={{0,96},{32,64},{64,32},{96,0},{16,112},{48,80},{80,48},{112,16},{1... | collective-permute-start | bytes 307208 | tf_op jit(solution)/shard_map/ppermute | solution.py:42
  119.1 5.7 %collective-permute-start.32 = (f32[200,128]{1,0:T(8,128)S(1)}, f32[200,128]{1,0:T(8,128)S(1)}, u32[]{:S(2)}, u32[]{:S(2)}) collective-permute-start(f32[200,128]{1,0:T(8,128)S(1)} %add.108), channel_id=1, source_target_pairs={{0,32},{32,0},{64,96},{96,64},{16,48},{48,16},{80,112},{112,80},{1... | collective-permute-start | bytes 307208 | tf_op jit(solution)/shard_map/ppermute | solution.py:42
  (14 other events, 81.8 us)

commit v8 on v6

--- a/solution.py
+++ b/solution.py
@@ -15,7 +15,7 @@
 COLS = 1536
 QUARTER = ROWS // 4
 HALF = COLS // 2
-BLOCK = 1024
+BLOCK = 512
 LANES = 128
 LEFT_ROWS = K * QUARTER // LANES
 RIGHT_ROWS = K * HALF // LANES

time: 155 us -> 155 us (level)
  no operation moved by 1% of the time
where the time goes in v8:
time: 155 us; the launch traced here: 154 us
  waiting for transfers between devices  42.8 us (28%)
  starting transfers between devices  40.5 us (26%)
  Pallas kernels  35.5 us (23%)
  blocking collectives  33.7 us (22%)
    ppermute x36, waiting for transfers between devices, swap(): return lax.ppermute(value, axis, pairs)  42.8 us
    ppermute x36, starting transfers between devices, swap(): return lax.ppermute(value, axis, pairs)  40.5 us
    all_to_all x3, blocking collectives, from_all(): return lax.all_to_all(value, 'var', 0, 0)  33.7 us
    pallas_call x4, Pallas kernels, right_half(): pl.pallas_call(kernel, grid_spec=pltpu.PrefetchScalarGridSpec(num_scalar_...  8.44 us
    pallas_call x1, Pallas kernels, deflate(): pl.pallas_call(kernel, grid=(ROWS // BLOCK,), in_specs=[whole((16, K // 2...  6.68 us
    pallas_call x1, Pallas kernels, left_product_first(): pl.pallas_call(kernel, in_specs=[hbm, hbm], out_specs=[vmem] * 5 + [pl.Bl...  6.43 us
    pallas_call x1, Pallas kernels, left_partners(): pl.pallas_call(kernel, grid_spec=pltpu.PrefetchScalarGridSpec(num_scalar_...  4.37 us
    pallas_call x4, Pallas kernels, assemble(): pl.pallas_call(kernel, in_specs=[pl.BlockSpec(memory_space=pltpu.SMEM)] +...  3.36 us
  transfers between devices with their start and end apart: 36, of which 25 were waited for; matrix products, arithmetic and copies ran while one was open for 0% of the time, Pallas kernels for 6%

profile of v8, /device:TPU:0, one launch (start us, length us, event | category | flops | bytes accessed | tf_op | source)
XLA Modules:
  0.0 154.5 jit_solution(5672861147670767365)
XLA Ops:
  1.6 6.4 %left_product_first.1 = (f32[128,128]{1,0:T(8,128)S(1)}, f32[128,128]{1,0:T(8,128)S(1)}, f32[128,128]{1,0:T(8,128)S(1)}, f32[128,128]{1,0:T(8,128)S(1)}, f32[2048,1536]{1,0:T(8,128)S(1)}, /*index=5*/s32[8]{0:T(128)S(1)}) custom-call(f32[32,1536]{1,0:T(8,128)S(1)} %copy-done, f32[2048,1536]{1,0:T(8,128)} %cross_hbm.1), custom_call_target="tpu_custom_call" | custom-call | tf_op jit(solution)/shard_map/left_product_first/pallas_call | solution.py:212
  8.0 2.1 %collective-permute-start = (f32[128,128]{1,0:T(8,128)S(1)}, f32[128,128]{1,0:T(8,128)S(1)}, u32[]{:S(2)}, u32[]{:S(2)}) collective-permute-start(f32[128,128]{1,0:T(8,128)S(1)} %get-tuple-element.41), channel_id=1, source_target_pairs={{0,1},{1,0},{2,3},{3,2},{4,5},{5,4},{6,7},{7,6},{8,9},{9,8},{10,11... | collective-permute-start | bytes 196616 | tf_op jit(solution)/shard_map/ppermute | solution.py:42
  10.1 2.5 %collective-permute-start.1 = (f32[128,128]{1,0:T(8,128)S(1)}, f32[128,128]{1,0:T(8,128)S(1)}, u32[]{:S(2)}, u32[]{:S(2)}) collective-permute-start(f32[128,128]{1,0:T(8,128)S(1)} %get-tuple-element.42), channel_id=1, source_target_pairs={{0,3},{1,2},{2,1},{3,0},{4,7},{5,6},{6,5},{7,4},{8,11},{9,10},{10,... | collective-permute-start | bytes 196616 | tf_op jit(solution)/shard_map/ppermute | solution.py:42
  15.6 2.8 %collective-permute-done.2 = f32[128,128]{1,0:T(8,128)S(1)} collective-permute-done((f32[128,128]{1,0:T(8,128)S(1)}, f32[128,128]{1,0:T(8,128)S(1)}, u32[]{:S(2)}, u32[]{:S(2)}) %collective-permute-start.2) | collective-permute-done | bytes 65568 | tf_op jit(solution)/shard_map/ppermute | solution.py:42
  18.4 3.3 %collective-permute-start.5 = (f32[128,128]{1,0:T(8,128)S(1)}, f32[128,128]{1,0:T(8,128)S(1)}, u32[]{:S(2)}, u32[]{:S(2)}) collective-permute-start(f32[128,128]{1,0:T(8,128)S(1)} %add_add_fusion.5), channel_id=1, source_target_pairs={{0,8},{4,12},{8,0},{12,4},{1,9},{5,13},{9,1},{13,5},{2,10},{6,14},... | collective-permute-start | bytes 196616 | tf_op jit(solution)/shard_map/ppermute | solution.py:42
  24.3 2.8 %collective-permute-done.4 = f32[128,128]{1,0:T(8,128)S(1)} collective-permute-done((f32[128,128]{1,0:T(8,128)S(1)}, f32[128,128]{1,0:T(8,128)S(1)}, u32[]{:S(2)}, u32[]{:S(2)}) %collective-permute-start.4) | collective-permute-done | bytes 65568 | tf_op jit(solution)/shard_map/ppermute | solution.py:42
  28.3 2.6 %collective-permute-start.7 = (f32[128,128]{1,0:T(8,128)S(1)}, f32[128,128]{1,0:T(8,128)S(1)}, u32[]{:S(2)}, u32[]{:S(2)}) collective-permute-start(f32[128,128]{1,0:T(8,128)S(1)} %add_add_fusion.4.refs_0_), channel_id=1, source_target_pairs={{0,3},{1,2},{2,1},{3,0},{4,7},{5,6},{6,5},{7,4},{8,11},{9,10},{10,... | collective-permute-start | bytes 196616 | tf_op jit(solution)/shard_map/ppermute | solution.py:42
  37.1 3.0 %collective-permute-start.12 = (f32[1,1,128]{2,1,0:T(1,128)S(1)}, f32[1,1,128]{2,1,0:T(1,128)S(1)}, u32[]{:S(2)}, u32[]{:S(2)}) collective-permute-start(f32[1,1,128]{2,1,0:T(1,128)S(1)} %add.90), channel_id=1, source_target_pairs={{0,64},{32,96},{64,0},{96,32},{16,80},{48,112},{80,16},{112,48},{1... | collective-permute-start | bytes 1544 | tf_op jit(solution)/shard_map/ppermute | solution.py:42
  42.1 2.7 %collective-permute-done.11 = f32[1,1,128]{2,1,0:T(1,128)S(1)} collective-permute-done((f32[1,1,128]{2,1,0:T(1,128)S(1)}, f32[1,1,128]{2,1,0:T(1,128)S(1)}, u32[]{:S(2)}, u32[]{:S(2)}) %collective-permute-start.11) | collective-permute-done | bytes 544 | tf_op jit(solution)/shard_map/ppermute | solution.py:42
  44.9 2.3 %right_half_head.2 = (f32[200,128]{1,0:T(8,128)S(1)}, bf16[64,2048]{1,0:T(8,128)(2,1)S(1)}, f32[8,128]{1,0:T(8,128)S(1)}, f32[32,2048]{1,0:T(8,128)}) custom-call(s32[8]{0:T(128)S(1)} %get-tuple-element.39.places_ref, f32[32,2048]{1,0:T(8,128)S(1)} %get-tuple-element.44.refs_0_, f32[1,1,128]{2,1,0:T(1,128)S(1)} %add_add_fusion.7.refs_1_, ...), custom_call_target="tpu_custom_call" | custom-call | flops 1200000000 | bytes 8000000 | tf_op jit(solution)/shard_map/right_half_head/pallas_call | solution.py:316
  52.8 3.6 %collective-permute-done.16 = f32[200,128]{1,0:T(8,128)S(1)} collective-permute-done((f32[200,128]{1,0:T(8,128)S(1)}, f32[200,128]{1,0:T(8,128)S(1)}, u32[]{:S(2)}, u32[]{:S(2)}) %collective-permute-start.16) | collective-permute-done | bytes 102432 | tf_op jit(solution)/shard_map/ppermute | solution.py:42
  56.4 2.1 %collective-permute-done.15 = f32[200,128]{1,0:T(8,128)S(1)} collective-permute-done((f32[200,128]{1,0:T(8,128)S(1)}, f32[200,128]{1,0:T(8,128)S(1)}, u32[]{:S(2)}, u32[]{:S(2)}) %collective-permute-start.15) | collective-permute-done | bytes 102432 | tf_op jit(solution)/shard_map/ppermute | solution.py:42
  60.8 11.4 %all_to_all.15.squares_ref = f32[16,1,128]{2,1,0:T(1,128)S(1)} all-to-all(f32[16,1,128]{2,1,0:T(1,128)S(1)} %get-tuple-element.51), channel_id=1, replica_groups=mesh['vox'=8,'var'=16] {'var'}, dimensions={0} | all-to-all | bytes 16384 | tf_op jit(solution)/shard_map/all_to_all | solution.py:51
  72.2 4.4 %left_partners.1 = (f32[136,128]{1,0:T(8,128)S(1)}, f32[136,128]{1,0:T(8,128)S(1)}, f32[136,128]{1,0:T(8,128)S(1)}, bf16[64,1536]{1,0:T(8,128)(2,1)S(1)}, f32[8,128]{1,0:T(8,128)S(1)}) custom-call(s32[8]{0:T(128)S(1)} %get-tuple-element.39.places_ref, f32[32,1536]{1,0:T(8,128)S(1)} %get-tuple-element.50.right_ref, f32[16,1,128]{2,1,0:T(1,128)S(1)} %all_to_all.15.squares_ref, ...), custom_call_target="tpu_custom_call" | custom-call | tf_op jit(solution)/shard_map/left_partners/pallas_call | solution.py:255
  78.4 2.3 %collective-permute-start.20 = (f32[136,128]{1,0:T(8,128)S(1)}, f32[136,128]{1,0:T(8,128)S(1)}, u32[]{:S(2)}, u32[]{:S(2)}) collective-permute-start(f32[136,128]{1,0:T(8,128)S(1)} %get-tuple-element.56), channel_id=1, source_target_pairs={{0,2},{1,3},{2,0},{3,1},{4,6},{5,7},{6,4},{7,5},{8,10},{9,11},{10,... | collective-permute-start | bytes 208904 | tf_op jit(solution)/shard_map/ppermute | solution.py:42
  87.8 2.3 %collective-permute-done.23 = f32[136,128]{1,0:T(8,128)S(1)} collective-permute-done((f32[136,128]{1,0:T(8,128)S(1)}, f32[136,128]{1,0:T(8,128)S(1)}, u32[]{:S(2)}, u32[]{:S(2)}) %collective-permute-start.23) | collective-permute-done | bytes 69664 | tf_op jit(solution)/shard_map/ppermute | solution.py:42
  91.9 2.4 %collective-permute-start.26 = (f32[128,128]{1,0:T(8,128)S(1)}, f32[128,128]{1,0:T(8,128)S(1)}, u32[]{:S(2)}, u32[]{:S(2)}) collective-permute-start(f32[128,128]{1,0:T(8,128)S(1)} %slice.27.refs_1_), channel_id=1, source_target_pairs={{0,2},{1,3},{2,0},{3,1},{4,6},{5,7},{6,4},{7,5},{8,10},{9,11},{10,... | collective-permute-start | bytes 196616 | tf_op jit(solution)/shard_map/ppermute | solution.py:42
  108.2 2.3 %right_half_head.3 = (f32[200,128]{1,0:T(8,128)S(1)}, bf16[64,2048]{1,0:T(8,128)(2,1)S(1)}, f32[8,128]{1,0:T(8,128)S(1)}, f32[32,2048]{1,0:T(8,128)S(1)}) custom-call(s32[8]{0:T(128)S(1)} %get-tuple-element.39.places_ref, f32[32,2048]{1,0:T(8,128)S(1)} %get-tuple-element.57.refs_0_, f32[1,1,128]{2,1,0:T(1,128)S(1)} %add_add_fusion.6.refs_1_, ...), custom_call_target="tpu_custom_call" | custom-call | flops 1200000000 | bytes 8000000 | tf_op jit(solution)/shard_map/right_half_head/pallas_call | solution.py:316
  112.5 2.4 %collective-permute-start.34 = (f32[200,128]{1,0:T(8,128)S(1)}, f32[200,128]{1,0:T(8,128)S(1)}, u32[]{:S(2)}, u32[]{:S(2)}) collective-permute-start(f32[200,128]{1,0:T(8,128)S(1)} %add.108), channel_id=1, source_target_pairs={{0,64},{32,96},{64,0},{96,32},{16,80},{48,112},{80,16},{112,48},{1... | collective-permute-start | bytes 307208 | tf_op jit(solution)/shard_map/ppermute | solution.py:42
  116.1 3.6 %collective-permute-done.34 = f32[200,128]{1,0:T(8,128)S(1)} collective-permute-done((f32[200,128]{1,0:T(8,128)S(1)}, f32[200,128]{1,0:T(8,128)S(1)}, u32[]{:S(2)}, u32[]{:S(2)}) %collective-permute-start.34) | collective-permute-done | bytes 102432 | tf_op jit(solution)/shard_map/ppermute | solution.py:42
  119.6 2.1 %collective-permute-done.33 = f32[200,128]{1,0:T(8,128)S(1)} collective-permute-done((f32[200,128]{1,0:T(8,128)S(1)}, f32[200,128]{1,0:T(8,128)S(1)}, u32[]{:S(2)}, u32[]{:S(2)}) %collective-permute-start.33) | collective-permute-done | bytes 102432 | tf_op jit(solution)/shard_map/ppermute | solution.py:42
  124.9 11.4 %all_to_all.16.squares_ref = f32[16,1,128]{2,1,0:T(1,128)S(1)} all-to-all(f32[16,1,128]{2,1,0:T(1,128)S(1)} %get-tuple-element.66), channel_id=1, replica_groups=mesh['vox'=8,'var'=16] {'var'}, dimensions={0} | all-to-all | bytes 16384 | tf_op jit(solution)/shard_map/all_to_all | solution.py:51
  137.0 10.8 %all_to_all.17.last_ref = f32[16,16,128]{2,1,0:T(8,128)S(1)} all-to-all(f32[16,16,128]{2,1,0:T(8,128)S(1)} %get-tuple-element.67), channel_id=1, replica_groups=mesh['vox'=8,'var'=16] {'var'}, dimensions={0} | all-to-all | bytes 262144 | tf_op jit(solution)/shard_map/all_to_all | solution.py:51
  147.8 6.7 %deflate.1 = (f32[2048,1536]{1,0:T(8,128)}, f32[32,1536]{1,0:T(8,128)}, f32[1,32]{1,0:T(1,128)}) custom-call(f32[16,16,128]{2,1,0:T(8,128)S(1)} %all_to_all.17.last_ref, f32[32,1536]{1,0:T(8,128)S(1)} %get-tuple-element.68.shrunk_ref, bf16[2048,192]{1,0:T(8,128)(2,1)S(1)} %get-tuple-element.69.left_ref, ...), custom_call_target="tpu_custom_call" | custom-call | tf_op jit(solution)/shard_map/deflate/pallas_call | solution.py:434
  (90 shorter events, 55.2 us)
Async XLA Ops:
  8.0 5.7 %collective-permute-start = (f32[128,128]{1,0:T(8,128)S(1)}, f32[128,128]{1,0:T(8,128)S(1)}, u32[]{:S(2)}, u32[]{:S(2)}) collective-permute-start(f32[128,128]{1,0:T(8,128)S(1)} %get-tuple-element.41), channel_id=1, source_target_pairs={{0,1},{1,0},{2,3},{3,2},{4,5},{5,4},{6,7},{7,6},{8,9},{9,8},{10,11... | collective-permute-start | bytes 196616 | tf_op jit(solution)/shard_map/ppermute | solution.py:42
  10.1 5.5 %collective-permute-start.1 = (f32[128,128]{1,0:T(8,128)S(1)}, f32[128,128]{1,0:T(8,128)S(1)}, u32[]{:S(2)}, u32[]{:S(2)}) collective-permute-start(f32[128,128]{1,0:T(8,128)S(1)} %get-tuple-element.42), channel_id=1, source_target_pairs={{0,3},{1,2},{2,1},{3,0},{4,7},{5,6},{6,5},{7,4},{8,11},{9,10},{10,... | collective-permute-start | bytes 196616 | tf_op jit(solution)/shard_map/ppermute | solution.py:42
  12.6 5.8 %collective-permute-start.2 = (f32[128,128]{1,0:T(8,128)S(1)}, f32[128,128]{1,0:T(8,128)S(1)}, u32[]{:S(2)}, u32[]{:S(2)}) collective-permute-start(f32[128,128]{1,0:T(8,128)S(1)} %get-tuple-element.43), channel_id=1, source_target_pairs={{0,2},{1,3},{2,0},{3,1},{4,6},{5,7},{6,4},{7,5},{8,10},{9,11},{10,... | collective-permute-start | bytes 196616 | tf_op jit(solution)/shard_map/ppermute | solution.py:42
  18.4 6.0 %collective-permute-start.5 = (f32[128,128]{1,0:T(8,128)S(1)}, f32[128,128]{1,0:T(8,128)S(1)}, u32[]{:S(2)}, u32[]{:S(2)}) collective-permute-start(f32[128,128]{1,0:T(8,128)S(1)} %add_add_fusion.5), channel_id=1, source_target_pairs={{0,8},{4,12},{8,0},{12,4},{1,9},{5,13},{9,1},{13,5},{2,10},{6,14},... | collective-permute-start | bytes 196616 | tf_op jit(solution)/shard_map/ppermute | solution.py:42
  21.7 5.5 %collective-permute-start.4 = (f32[128,128]{1,0:T(8,128)S(1)}, f32[128,128]{1,0:T(8,128)S(1)}, u32[]{:S(2)}, u32[]{:S(2)}) collective-permute-start(f32[128,128]{1,0:T(8,128)S(1)} %add_add_fusion.5), channel_id=1, source_target_pairs={{0,12},{4,8},{8,4},{12,0},{1,13},{5,9},{9,5},{13,1},{2,14},{6,10},... | collective-permute-start | bytes 196616 | tf_op jit(solution)/shard_map/ppermute | solution.py:42
  27.2 5.8 %collective-permute-start.8 = (f32[128,128]{1,0:T(8,128)S(1)}, f32[128,128]{1,0:T(8,128)S(1)}, u32[]{:S(2)}, u32[]{:S(2)}) collective-permute-start(f32[128,128]{1,0:T(8,128)S(1)} %add_add_fusion.4.refs_0_), channel_id=1, source_target_pairs={{0,2},{1,3},{2,0},{3,1},{4,6},{5,7},{6,4},{7,5},{8,10},{9,11},{10,... | collective-permute-start | bytes 196616 | tf_op jit(solution)/shard_map/ppermute | solution.py:42
  28.3 5.5 %collective-permute-start.7 = (f32[128,128]{1,0:T(8,128)S(1)}, f32[128,128]{1,0:T(8,128)S(1)}, u32[]{:S(2)}, u32[]{:S(2)}) collective-permute-start(f32[128,128]{1,0:T(8,128)S(1)} %add_add_fusion.4.refs_0_), channel_id=1, source_target_pairs={{0,3},{1,2},{2,1},{3,0},{4,7},{5,6},{6,5},{7,4},{8,11},{9,10},{10,... | collective-permute-start | bytes 196616 | tf_op jit(solution)/shard_map/ppermute | solution.py:42
  37.1 5.0 %collective-permute-start.12 = (f32[1,1,128]{2,1,0:T(1,128)S(1)}, f32[1,1,128]{2,1,0:T(1,128)S(1)}, u32[]{:S(2)}, u32[]{:S(2)}) collective-permute-start(f32[1,1,128]{2,1,0:T(1,128)S(1)} %add.90), channel_id=1, source_target_pairs={{0,64},{32,96},{64,0},{96,32},{16,80},{48,112},{80,16},{112,48},{1... | collective-permute-start | bytes 1544 | tf_op jit(solution)/shard_map/ppermute | solution.py:42
  40.1 4.8 %collective-permute-start.11 = (f32[1,1,128]{2,1,0:T(1,128)S(1)}, f32[1,1,128]{2,1,0:T(1,128)S(1)}, u32[]{:S(2)}, u32[]{:S(2)}) collective-permute-start(f32[1,1,128]{2,1,0:T(1,128)S(1)} %add.90), channel_id=1, source_target_pairs={{0,96},{32,64},{64,32},{96,0},{16,112},{48,80},{80,48},{112,16},{1... | collective-permute-start | bytes 1544 | tf_op jit(solution)/shard_map/ppermute | solution.py:42
  49.2 7.2 %collective-permute-start.16 = (f32[200,128]{1,0:T(8,128)S(1)}, f32[200,128]{1,0:T(8,128)S(1)}, u32[]{:S(2)}, u32[]{:S(2)}) collective-permute-start(f32[200,128]{1,0:T(8,128)S(1)} %add.94), channel_id=1, source_target_pairs={{0,64},{32,96},{64,0},{96,32},{16,80},{48,112},{80,16},{112,48},{1... | collective-permute-start | bytes 307208 | tf_op jit(solution)/shard_map/ppermute | solution.py:42
  50.7 7.7 %collective-permute-start.15 = (f32[200,128]{1,0:T(8,128)S(1)}, f32[200,128]{1,0:T(8,128)S(1)}, u32[]{:S(2)}, u32[]{:S(2)}) collective-permute-start(f32[200,128]{1,0:T(8,128)S(1)} %add.94), channel_id=1, source_target_pairs={{0,96},{32,64},{64,32},{96,0},{16,112},{48,80},{80,48},{112,16},{1... | collective-permute-start | bytes 307208 | tf_op jit(solution)/shard_map/ppermute | solution.py:42
  51.9 6.6 %collective-permute-start.14 = (f32[200,128]{1,0:T(8,128)S(1)}, f32[200,128]{1,0:T(8,128)S(1)}, u32[]{:S(2)}, u32[]{:S(2)}) collective-permute-start(f32[200,128]{1,0:T(8,128)S(1)} %add.94), channel_id=1, source_target_pairs={{0,32},{32,0},{64,96},{96,64},{16,48},{48,16},{80,112},{112,80},{1... | collective-permute-start | bytes 307208 | tf_op jit(solution)/shard_map/ppermute | solution.py:42
  76.6 5.8 %collective-permute-start.18 = (f32[136,128]{1,0:T(8,128)S(1)}, f32[136,128]{1,0:T(8,128)S(1)}, u32[]{:S(2)}, u32[]{:S(2)}) collective-permute-start(f32[136,128]{1,0:T(8,128)S(1)} %get-tuple-element.54), channel_id=1, source_target_pairs={{0,1},{1,0},{2,3},{3,2},{4,5},{5,4},{6,7},{7,6},{8,9},{9,8},{10,11... | collective-permute-start | bytes 208904 | tf_op jit(solution)/shard_map/ppermute | solution.py:42
  77.2 5.6 %collective-permute-start.19 = (f32[136,128]{1,0:T(8,128)S(1)}, f32[136,128]{1,0:T(8,128)S(1)}, u32[]{:S(2)}, u32[]{:S(2)}) collective-permute-start(f32[136,128]{1,0:T(8,128)S(1)} %get-tuple-element.55), channel_id=1, source_target_pairs={{0,3},{1,2},{2,1},{3,0},{4,7},{5,6},{6,5},{7,4},{8,11},{9,10},{10,... | collective-permute-start | bytes 208904 | tf_op jit(solution)/shard_map/ppermute | solution.py:42
  78.4 5.8 %collective-permute-start.20 = (f32[136,128]{1,0:T(8,128)S(1)}, f32[136,128]{1,0:T(8,128)S(1)}, u32[]{:S(2)}, u32[]{:S(2)}) collective-permute-start(f32[136,128]{1,0:T(8,128)S(1)} %get-tuple-element.56), channel_id=1, source_target_pairs={{0,2},{1,3},{2,0},{3,1},{4,6},{5,7},{6,4},{7,5},{8,10},{9,11},{10,... | collective-permute-start | bytes 208904 | tf_op jit(solution)/shard_map/ppermute | solution.py:42
  84.3 5.9 %collective-permute-start.23 = (f32[136,128]{1,0:T(8,128)S(1)}, f32[136,128]{1,0:T(8,128)S(1)}, u32[]{:S(2)}, u32[]{:S(2)}) collective-permute-start(f32[136,128]{1,0:T(8,128)S(1)} %add_add_fusion.3), channel_id=1, source_target_pairs={{0,8},{4,12},{8,0},{12,4},{1,9},{5,13},{9,1},{13,5},{2,10},{6,14},... | collective-permute-start | bytes 208904 | tf_op jit(solution)/shard_map/ppermute | solution.py:42
  85.5 5.5 %collective-permute-start.22 = (f32[136,128]{1,0:T(8,128)S(1)}, f32[136,128]{1,0:T(8,128)S(1)}, u32[]{:S(2)}, u32[]{:S(2)}) collective-permute-start(f32[136,128]{1,0:T(8,128)S(1)} %add_add_fusion.3), channel_id=1, source_target_pairs={{0,12},{4,8},{8,4},{12,0},{1,13},{5,9},{9,5},{13,1},{2,14},{6,10},... | collective-permute-start | bytes 208904 | tf_op jit(solution)/shard_map/ppermute | solution.py:42
  91.9 5.8 %collective-permute-start.26 = (f32[128,128]{1,0:T(8,128)S(1)}, f32[128,128]{1,0:T(8,128)S(1)}, u32[]{:S(2)}, u32[]{:S(2)}) collective-permute-start(f32[128,128]{1,0:T(8,128)S(1)} %slice.27.refs_1_), channel_id=1, source_target_pairs={{0,2},{1,3},{2,0},{3,1},{4,6},{5,7},{6,4},{7,5},{8,10},{9,11},{10,... | collective-permute-start | bytes 196616 | tf_op jit(solution)/shard_map/ppermute | solution.py:42
  94.3 5.5 %collective-permute-start.25 = (f32[128,128]{1,0:T(8,128)S(1)}, f32[128,128]{1,0:T(8,128)S(1)}, u32[]{:S(2)}, u32[]{:S(2)}) collective-permute-start(f32[128,128]{1,0:T(8,128)S(1)} %slice.27.refs_1_), channel_id=1, source_target_pairs={{0,3},{1,2},{2,1},{3,0},{4,7},{5,6},{6,5},{7,4},{8,11},{9,10},{10,... | collective-permute-start | bytes 196616 | tf_op jit(solution)/shard_map/ppermute | solution.py:42
  101.9 5.0 %collective-permute-start.30 = (f32[1,1,128]{2,1,0:T(1,128)S(1)}, f32[1,1,128]{2,1,0:T(1,128)S(1)}, u32[]{:S(2)}, u32[]{:S(2)}) collective-permute-start(f32[1,1,128]{2,1,0:T(1,128)S(1)} %add.104), channel_id=1, source_target_pairs={{0,64},{32,96},{64,0},{96,32},{16,80},{48,112},{80,16},{112,48},{1... | collective-permute-start | bytes 1544 | tf_op jit(solution)/shard_map/ppermute | solution.py:42
  103.4 4.8 %collective-permute-start.29 = (f32[1,1,128]{2,1,0:T(1,128)S(1)}, f32[1,1,128]{2,1,0:T(1,128)S(1)}, u32[]{:S(2)}, u32[]{:S(2)}) collective-permute-start(f32[1,1,128]{2,1,0:T(1,128)S(1)} %add.104), channel_id=1, source_target_pairs={{0,96},{32,64},{64,32},{96,0},{16,112},{48,80},{80,48},{112,16},{1... | collective-permute-start | bytes 1544 | tf_op jit(solution)/shard_map/ppermute | solution.py:42
  112.5 7.1 %collective-permute-start.34 = (f32[200,128]{1,0:T(8,128)S(1)}, f32[200,128]{1,0:T(8,128)S(1)}, u32[]{:S(2)}, u32[]{:S(2)}) collective-permute-start(f32[200,128]{1,0:T(8,128)S(1)} %add.108), channel_id=1, source_target_pairs={{0,64},{32,96},{64,0},{96,32},{16,80},{48,112},{80,16},{112,48},{1... | collective-permute-start | bytes 307208 | tf_op jit(solution)/shard_map/ppermute | solution.py:42
  114.8 6.9 %collective-permute-start.33 = (f32[200,128]{1,0:T(8,128)S(1)}, f32[200,128]{1,0:T(8,128)S(1)}, u32[]{:S(2)}, u32[]{:S(2)}) collective-permute-start(f32[200,128]{1,0:T(8,128)S(1)} %add.108), channel_id=1, source_target_pairs={{0,96},{32,64},{64,32},{96,0},{16,112},{48,80},{80,48},{112,16},{1... | collective-permute-start | bytes 307208 | tf_op jit(solution)/shard_map/ppermute | solution.py:42
  116.1 5.7 %collective-permute-start.32 = (f32[200,128]{1,0:T(8,128)S(1)}, f32[200,128]{1,0:T(8,128)S(1)}, u32[]{:S(2)}, u32[]{:S(2)}) collective-permute-start(f32[200,128]{1,0:T(8,128)S(1)} %add.108), channel_id=1, source_target_pairs={{0,32},{32,0},{64,96},{96,64},{16,48},{48,16},{80,112},{112,80},{1... | collective-permute-start | bytes 307208 | tf_op jit(solution)/shard_map/ppermute | solution.py:42
  (14 other events, 78.7 us)
